TPU v7x, 256 devices: a whole 4x4x8 slice. The times are simulated.
256 devices in a mesh: dp: 32 (over x_hi, z, core), grp: 8 (over y, x_lo).
Axes of the slice: x: 4 (x_hi: 2, x_lo: 2; x = x_hi * 2 + x_lo), y: 4, z: 8, core: 2. Of those that a mesh axis runs over, the one named last changes fastest.
Arguments:
- images: bfloat16 [16384, 1152], P(('dp', 'grp')), may hold values from -24 to 24
- texts: bfloat16 [16384, 1152], P(('dp', 'grp')), may hold values from -24 to 24
- log_scale: float32 [1], replicated, may hold values from 4 to 4.8
- bias: float32 [1], replicated, may hold values from -12 to -8
Outputs:
- image_grad: float32 [16384, 1152], P(('dp', 'grp'))
- text_grad: float32 [16384, 1152], P(('dp', 'grp'))
- stats: float32 [3], replicated
All inputs are finite; a program needn't handle non-finite values.
Results may differ from a plain program's by a relative error of at most 0.002.
The roundings to bfloat16 on the way count: a program that leaves them out, or rounds other values in their place, can miss the bound.
Values may be sent and summed in bfloat16 or wider, within the bound.
No kernel may reach another device: no remote copies, remote signals or barrier semaphores. Data moves between devices by JAX's collectives and lax.ppermute only.
A program may use at most 64 MiB of HBM per device.

v0:
```python
import jax
import jax.numpy as jnp
from jax import lax
from jax.sharding import PartitionSpec as P

EPS = 1e-06


def normalize(rows):
    values = rows.astype(jnp.float32)
    norms = jnp.sqrt(jnp.sum(values * values, axis=-1, keepdims=True) + EPS)
    return (values / norms, norms)


def project(direction, unit, norms):
    along = jnp.sum(direction * unit, axis=-1, keepdims=True)
    return (direction - unit * along) / norms


def on_device(images, texts, log_scale, bias):
    rows = images.shape[0]
    img_unit, img_norm = normalize(images)
    txt_unit, txt_norm = normalize(texts)
    img_low = img_unit.astype(jnp.bfloat16)
    txt_low = txt_unit.astype(jnp.bfloat16)
    scale = jnp.exp(log_scale[0])
    shift = bias[0]
    dp_index = lax.axis_index("dp")
    grp_index = lax.axis_index("grp")
    block_imgs = lax.all_gather(img_low, "grp", axis=0, tiled=True)
    img_count = block_imgs.shape[0]
    img_pos = lax.broadcasted_iota(jnp.int32, (img_count, 1), 0)
    piece = lax.all_gather(txt_low, "dp", axis=0, tiled=True)
    count = piece.shape[0]
    cosine = jnp.einsum("ie,je->ij", block_imgs, piece, preferred_element_type=jnp.float32)
    scaled = scale * cosine
    logits = scaled + shift
    local = lax.broadcasted_iota(jnp.int32, (1, count), 1) - dp_index * rows
    positive = (local >= 0) & (local < rows) & (img_pos == grp_index * rows + local)
    sign = jnp.where(positive, 1.0, -1.0).astype(jnp.float32)
    losses = jax.nn.softplus(-sign * logits)
    grad = jax.nn.sigmoid(logits) - positive.astype(jnp.float32)
    sums = jnp.stack([jnp.sum(losses), jnp.sum(grad * scaled), jnp.sum(grad)])
    grad_low, sums = (grad.astype(jnp.bfloat16), sums)
    img_acc = jnp.dot(grad_low, piece, preferred_element_type=jnp.float32)
    term = jnp.einsum("ij,ie->je", grad_low, block_imgs, preferred_element_type=jnp.float32)
    txt_acc = term
    img_acc, txt_acc, totals = (img_acc, txt_acc, sums)
    txt_part = lax.psum_scatter(txt_acc, "dp", scatter_dimension=0, tiled=True)
    img_part = lax.psum_scatter(img_acc, "grp", scatter_dimension=0, tiled=True)
    overall = lax.psum(totals, ("dp", "grp"))
    batch_rows = rows * lax.axis_size("dp") * lax.axis_size("grp")
    image_grad = project(scale * img_part, img_unit, img_norm)
    text_grad = project(scale * txt_part, txt_unit, txt_norm)
    return (image_grad, text_grad, overall / batch_rows)


def solution(mesh):
    in_specs = (P(("dp", "grp"), None), P(("dp", "grp"), None), P(), P())
    out_specs = (P(("dp", "grp"), None), P(("dp", "grp"), None), P())
    return jax.shard_map(
        on_device, mesh=mesh, in_specs=in_specs, out_specs=out_specs, check_vma=False
    )
```

profile of v0, /device:TPU:2, one launch (start us, length us, event | category | flops | bytes accessed | tf_op | source)
XLA Modules:
  0.0 394.4 jit_solution(9898853837945935118)
XLA Ops:
  7.2 0.0 all-gather.3.cloned.1.call-start
  7.2 1.0 fusion.6
  8.3 1.7 fusion.12
  9.9 0.0 all-gather.3.cloned.1.call-update
  10.0 0.0 all-gather.5.cloned.1.call-start
  10.0 1.0 fusion.7
  11.1 1.7 fusion.13
  12.8 0.0 all-gather.5.cloned.1.call-update
  12.8 0.0 reduce-scatter.3.cloned.1.call-start
  14.2 40.4 %all-gather.3.cloned.1.call-done = bf16[512,1152]{1,0:T(8,128)(2,1)} async-done(((bf16[64,1152]{1,0:T(8,128)(2,1)}), bf16[512,1152]{1,0:T(8,128)(2,1)}) %all-gather.3.cloned.1.call-update) | async-done | bytes 1179664 | tf_op jit(solution)/shard_map/all_gather | solution.py:30
  54.6 92.7 %all-gather.5.cloned.1.call-done = bf16[2048,1152]{1,0:T(8,128)(2,1)} async-done(((bf16[64,1152]{1,0:T(8,128)(2,1)}), bf16[2048,1152]{1,0:T(8,128)(2,1)}) %all-gather.5.cloned.1.call-update) | async-done | bytes 4718608 | tf_op jit(solution)/shard_map/all_gather | solution.py:33
  147.3 0.0 copy-start.2
  147.3 10.1 %fusion = (f32[]{:T(128)}, f32[]{:T(128)}, f32[]{:T(128)}, f32[512,2048]{1,0:T(8,128)S(1)}) fusion(s32[2048]{0:T(1024)S(1)} %fusion.8, f32[]{:T(128)} %bitcast.10, f32[]{:T(128)} %bitcast, pred[2048]{0:T(1024)(128)(4,1)S(1)} %fusion.11, bf16[512,1152]{1,0:T(8,128)(2,1)} %all-gather.3.cloned.1.call-done, bf16[2048,1152]{1,0:T(8,128)(2,1)} %all-gather.5.cloned.1.call-done), kind=kOutput, calls=%fused_computation.1 | convolution fusion | flops 2438987776 | bytes 10102804 | tf_op jit(solution)/shard_map/ie,je->ij/dot_general | solution.py:35
  157.4 0.0 copy-start.4
  157.4 2.1 copy-done.4
  159.5 0.0 copy-done.2
  159.5 5.4 %fusion.4 = f32[512,1152]{1,0:T(8,128)} fusion(bf16[2048,1152]{1,0:T(8,128)(2,1)S(1)} %copy-done.2, f32[512,2048]{1,0:T(8,128)S(1)} %get-tuple-element.6, s32[2048]{0:T(1024)S(1)} %fusion.8, f32[]{:T(128)} %bitcast.9, f32[]{:T(128)} %bitcast, pred[2048]{0:T(1024)(128)(4,1)S(1)} %fusion.11), kind=kOutput, calls=%fused_computation.8 | convolution fusion | flops 2426404864 | bytes 11282440 | tf_op jit(solution)/shard_map/dot_general | solution.py:45
  164.9 0.0 reduce-scatter.3.cloned.1.call-update
  165.0 0.0 reduce-scatter.5.cloned.1.call-start
  165.0 0.0 copy-done.3
  165.0 9.8 %fusion.2 = f32[2048,1152]{1,0:T(8,128)} fusion(bf16[512,1152]{1,0:T(8,128)(2,1)S(1)} %copy-done.3, f32[512,2048]{1,0:T(8,128)} %copy-done.4, s32[2048]{0:T(1024)S(1)} %fusion.8, f32[]{:T(128)} %bitcast.11, f32[]{:T(128)} %bitcast, pred[2048]{0:T(1024)(128)(4,1)S(1)} %fusion.11), kind=kOutput, calls=%fused_computation.6 | convolution fusion | flops 2426404864 | bytes 14821384 | tf_op jit(solution)/shard_map/ij,ie->je/dot_general | solution.py:46
  174.8 0.0 reduce-scatter.5.cloned.1.call-update
  174.8 2.0 pad_maximum_fusion
  176.8 76.9 %psum.7 = f32[3]{0:T(128)S(1)} all-reduce(f32[3]{0:T(128)S(1)} %pad_maximum_fusion), channel_id=1, replica_groups=mesh['dp'=32,'grp'=8] {'dp','grp'}, use_global_device_ids=true, to_apply=%region_9.10 | all-reduce | flops 3 | bytes 24 | tf_op jit(solution)/shard_map/psum | solution.py:51
  253.7 0.5 broadcast_multiply_fusion
  254.2 0.0 copy-done
  254.2 1.2 multiply_reduce_fusion.2
  255.4 1.9 subtract_divide_fusion.1
  257.3 127.6 %reduce-scatter.5.cloned.1.call-done = f32[64,1152]{1,0:T(8,128)} async-done(((f32[2048,1152]{1,0:T(8,128)}), f32[64,1152]{1,0:T(8,128)}) %reduce-scatter.5.cloned.1.call-update) | async-done | bytes 294928 | tf_op jit(solution)/shard_map/reduce_scatter | solution.py:49
  384.9 0.0 copy-done.1
  384.9 1.2 multiply_reduce_fusion.1
  386.1 1.8 subtract_divide_fusion
  (8 shorter events, 0.0 us)
Async XLA Ops:
  7.2 47.4 %all-gather.3.cloned.1.call-start = ((), (), s32[]{:S(2)}) async-start(), calls=%async_computation.2 | async-start | bytes 1327104 | tf_op jit(solution)/shard_map/all_gather | solution.py:30
  10.0 137.3 %all-gather.5.cloned.1.call-start = ((), (), s32[]{:S(2)}) async-start(), calls=%async_computation.3 | async-start | bytes 4866048 | tf_op jit(solution)/shard_map/all_gather | solution.py:33
  12.8 241.5 %reduce-scatter.3.cloned.1.call-start = ((), (), s32[]{:S(2)}) async-start(), calls=%async_computation.4 | async-start | bytes 2654208 | tf_op jit(solution)/shard_map/reduce_scatter | solution.py:50
  147.3 12.2 %copy-start.2 = (bf16[2048,1152]{1,0:T(8,128)(2,1)S(1)}, bf16[2048,1152]{1,0:T(8,128)(2,1)}, u32[]{:S(2)}) copy-start(bf16[2048,1152]{1,0:T(8,128)(2,1)} %all-gather.5.cloned.1.call-done) | copy-start | bytes 14155780
  157.4 2.1 copy-start.4
  159.5 5.5 %copy-start.3 = (bf16[512,1152]{1,0:T(8,128)(2,1)S(1)}, bf16[512,1152]{1,0:T(8,128)(2,1)}, u32[]{:S(2)}) copy-start(bf16[512,1152]{1,0:T(8,128)(2,1)} %all-gather.3.cloned.1.call-done) | copy-start | bytes 3538948
  165.0 220.0 %reduce-scatter.5.cloned.1.call-start = ((), (), s32[]{:S(2)}) async-start(), calls=%async_computation.5 | async-start | bytes 9732096 | tf_op jit(solution)/shard_map/reduce_scatter | solution.py:49
  174.8 79.4 %copy-start = (bf16[64,1152]{1,0:T(8,128)(2,1)S(1)}, bf16[64,1152]{1,0:T(8,128)(2,1)}, u32[]{:S(2)}) copy-start(bf16[64,1152]{1,0:T(8,128)(2,1)} %param.4) | copy-start | bytes 442372
  174.8 210.1 %copy-start.1 = (bf16[64,1152]{1,0:T(8,128)(2,1)S(1)}, bf16[64,1152]{1,0:T(8,128)(2,1)}, u32[]{:S(2)}) copy-start(bf16[64,1152]{1,0:T(8,128)(2,1)} %param.5) | copy-start | bytes 442372
Sparse Core Ops, SparseCore 0:
  10.4 44.1 all-gather.2
  57.9 89.3 all-gather.4
  165.1 56.8 reduce-scatter.2
  226.3 158.6 reduce-scatter.4
where the time goes:
time: 396 us; the launch traced here: 394 us
  waiting for transfers between devices  261 us (66%)
  blocking collectives  76.9 us (19%)
  matrix products  25.3 us (6%)
  between operations  15.2 us (4%)
  other arithmetic  14 us (4%)
    reduce_scatter x1, waiting for transfers between devices, on_device(): txt_part = lax.psum_scatter(txt_acc, 'dp', scatter_dimension=0, tiled=True)  128 us
    all_gather x1, waiting for transfers between devices, on_device(): piece = lax.all_gather(txt_low, 'dp', axis=0, tiled=True)  92.7 us
    psum x1, blocking collectives, on_device(): overall = lax.psum(totals, ('dp', 'grp'))  76.9 us
    all_gather x1, waiting for transfers between devices, on_device(): block_imgs = lax.all_gather(img_low, 'grp', axis=0, tiled=True)  40.4 us
    dot_general x1, matrix products, on_device(): jnp.einsum('ie,je->ij', block_imgs, piece, preferred_element_type=jnp.flo...  10.1 us
    dot_general x1, matrix products, on_device(): jnp.einsum('ij,ie->je', grad_low, block_imgs, preferred_element_type=jnp....  9.78 us
  transfers between devices with their start and end apart: 4, of which 3 were waited for; matrix products, arithmetic and copies ran while one was open for 5% of the time, Pallas kernels for 0%

commit v1 on v0

v1 whole, which is shorter than its diff:
```python
import jax
import jax.numpy as jnp
from jax import lax
from jax.experimental import pallas as pl
from jax.experimental.pallas import tpu as pltpu
from jax.sharding import Mesh
from jax.sharding import PartitionSpec as P

EPS = 1e-06
AXES = ("x_hi", "z", "core", "y", "x_lo")
SIZES = (2, 8, 2, 4, 2)
PLANE = ("x_hi", "y", "x_lo")
PEERS = 16
DEPTH = 8
BF16 = jnp.bfloat16
F32 = jnp.float32
VMEM = pl.BlockSpec(memory_space=pltpu.VMEM)
SMEM = pl.BlockSpec(memory_space=pltpu.SMEM)
PARAMS = pltpu.CompilerParams(vmem_limit_bytes=48 * 1024 * 1024)


def cost(flops, nbytes):
    return pl.CostEstimate(flops=flops, bytes_accessed=nbytes, transcendentals=0)


def place(index):
    out = []
    for size in reversed(SIZES):
        out.append(index % size)
        index //= size
    return list(reversed(out))


def number(where):
    index = 0
    for size, at in zip(SIZES, where):
        index = index * size + at
    return index


def shifted(array, axis, by):
    pairs = []
    for source in range(256):
        where = place(source)
        where[axis] = (where[axis] + by) % SIZES[axis]
        pairs.append((source, number(where)))
    return lax.ppermute(array, AXES, pairs)


def flipped(array, axis, by):
    pairs = []
    for source in range(256):
        where = place(source)
        where[axis] ^= by
        pairs.append((source, number(where)))
    return lax.ppermute(array, AXES, pairs)


def along_z(array, by):
    return shifted(array, 1, by)


def other_core(array):
    return shifted(array, 2, 1)


def unit_of(ref):
    values = ref[...].astype(F32)
    norms = jnp.sqrt(jnp.sum(values * values, axis=-1, keepdims=True) + EPS)
    return values / norms, norms


def copies_kernel(rows_ref, out_ref):
    low = unit_of(rows_ref)[0].astype(BF16)
    for k in range(PEERS):
        out_ref[k] = low


def low_kernel(rows_ref, out_ref):
    out_ref[...] = unit_of(rows_ref)[0].astype(BF16)


def fold_sum(array):
    return jnp.sum(array.reshape(-1, 8, array.shape[-1]), axis=0)


def fold_growth(array):
    parts = array.reshape(-1, 8, array.shape[-1])
    while parts.shape[0] > 1:
        half = parts.shape[0] // 2
        a, b = parts[:half], parts[half:]
        parts = a + (b + a * b)
    return parts[0]


def lanes(array):
    out = array[:, :128]
    for at in range(128, array.shape[-1], 128):
        out = out + array[:, at : at + 128]
    return out


def pair_kernel(first_ref, scale_ref, shift_ref, img_ref, mine_ref, theirs_ref, grad_ref, sums_ref):
    tile = pl.program_id(0)
    rows = img_ref.shape[0]
    half = mine_ref.shape[0]
    wide = 256
    scale = scale_ref[0]
    shift = shift_ref[0]
    imgs = img_ref[...]
    loss_sum = jnp.zeros((8, 128), F32)
    scaled_sum = jnp.zeros((8, 128), F32)
    grad_sum = jnp.zeros((8, 128), F32)
    for side, txt_ref in enumerate((mine_ref, theirs_ref)):
        for at in range(0, half, wide):
            cosine = lax.dot_general(
                imgs, txt_ref[at : at + wide, :], (((1,), (1,)), ((), ())), preferred_element_type=F32
            )
            scaled = scale * cosine
            logits = scaled + shift
            small = jnp.exp(-jnp.abs(logits))
            whole = 1.0 + small
            grad = jnp.where(logits >= 0.0, 1.0, small) / whole
            signed = logits
            if side == 0 and at == 0:
                row = lax.broadcasted_iota(jnp.int32, (rows, wide), 0) + (tile * rows - first_ref[0])
                col = lax.broadcasted_iota(jnp.int32, (rows, wide), 1)
                positive = (row == col) & (col < 64)
                signed = jnp.where(positive, -logits, logits)
                grad = jnp.where(positive, grad - 1.0, grad)
            loss_sum += lanes(fold_sum(jnp.maximum(signed, 0.0)) + jnp.log1p(fold_growth(small)))
            scaled_sum += lanes(fold_sum(grad * scaled))
            grad_sum += lanes(fold_sum(grad))
            grad_ref[:, side * half + at : side * half + at + wide] = grad.astype(BF16)

    @pl.when(tile == 0)
    def _():
        sums_ref[...] = jnp.zeros_like(sums_ref)

    sums_ref[0:8, :] += loss_sum
    sums_ref[8:16, :] += scaled_sum
    sums_ref[16:24, :] += grad_sum


def pairs(first, scale, shift, imgs, mine, theirs):
    count, emb = imgs.shape
    half = mine.shape[0]
    rows = 256
    return pl.pallas_call(
        pair_kernel,
        grid=(count // rows,),
        in_specs=[
            SMEM,
            SMEM,
            SMEM,
            pl.BlockSpec((rows, emb), lambda i: (i, 0)),
            pl.BlockSpec((half, emb), lambda i: (0, 0)),
            pl.BlockSpec((half, emb), lambda i: (0, 0)),
        ],
        out_specs=[
            pl.BlockSpec((rows, 2 * half), lambda i: (i, 0)),
            pl.BlockSpec((24, 128), lambda i: (0, 0)),
        ],
        out_shape=[
            jax.ShapeDtypeStruct((count, 2 * half), BF16),
            jax.ShapeDtypeStruct((24, 128), F32),
        ],
        compiler_params=PARAMS,
        cost_estimate=cost(2 * count * 2 * half * emb, 8 * 2**20),
    )(first, scale, shift, imgs, mine, theirs)


def project_kernel(scale_ref, rows_ref, parts_ref, out_ref):
    unit, norms = unit_of(rows_ref)
    total = parts_ref[0].astype(F32)
    for k in range(1, parts_ref.shape[0]):
        total = total + parts_ref[k].astype(F32)
    direction = scale_ref[0] * total
    along = jnp.sum(direction * unit, axis=-1, keepdims=True)
    out_ref[...] = (direction - unit * along) / norms


def projected(scale, rows, parts):
    return pl.pallas_call(
        project_kernel,
        in_specs=[SMEM, VMEM, VMEM],
        out_specs=VMEM,
        out_shape=jax.ShapeDtypeStruct(rows.shape, F32),
        compiler_params=PARAMS,
        cost_estimate=cost(10**6, 4 * 2**20),
    )(scale, rows, parts)


def on_device(images, texts, log_scale, bias):
    rows, emb = images.shape
    scale = jnp.exp(log_scale)
    plane = (lax.axis_index("x_hi") * 4 + lax.axis_index("y")) * 2 + lax.axis_index("x_lo")
    first = (plane * rows).astype(jnp.int32).reshape(1)

    copies = pl.pallas_call(
        copies_kernel,
        in_specs=[VMEM],
        out_specs=VMEM,
        out_shape=jax.ShapeDtypeStruct((PEERS, rows, emb), BF16),
        compiler_params=PARAMS,
        cost_estimate=cost(10**6, 3 * 2**20),
    )(images)
    txt_low = pl.pallas_call(
        low_kernel,
        in_specs=[VMEM],
        out_specs=VMEM,
        out_shape=jax.ShapeDtypeStruct((rows, emb), BF16),
        compiler_params=PARAMS,
        cost_estimate=cost(10**6, 2**19),
    )(texts)

    imgs = lax.all_to_all(copies, PLANE, 0, 0).reshape(PEERS * rows, emb)
    up, down = [txt_low], []
    for _ in range(4):
        up.append(along_z(up[-1], 1))
    down.append(along_z(txt_low, -1))
    for _ in range(2):
        down.append(along_z(down[-1], -1))
    mine = jnp.concatenate(up + down[::-1], axis=0)
    theirs = other_core(mine)

    grad_low, sums = pairs(first, scale, bias, imgs, mine, theirs)
    half = DEPTH * rows
    img_part = jnp.dot(grad_low[:, :half], mine, preferred_element_type=F32) + jnp.dot(
        grad_low[:, half:], theirs, preferred_element_type=F32
    )
    img_part = img_part.astype(BF16).reshape(PEERS, rows, emb)
    txt_part = lax.dot_general(grad_low, imgs, (((0,), (0,)), ((), ())), preferred_element_type=F32)

    img_recv = lax.all_to_all(img_part, PLANE, 0, 0)

    blocks = (txt_part[:half] + other_core(txt_part[half:])).reshape(DEPTH, rows, emb)
    left = blocks[4]
    for k in (3, 2, 1):
        left = along_z(left, -1) + blocks[k]
    left = along_z(left, -1)
    right = blocks[5]
    for k in (6, 7):
        right = along_z(right, 1) + blocks[k]
    right = along_z(right, 1)
    txt_total = (blocks[0] + left + right)[None]

    sums = jnp.sum(sums.reshape(3, -1), axis=-1)
    for axis, by in ((2, 1), (1, 4), (1, 2), (1, 1), (0, 1), (3, 2), (3, 1), (4, 1)):
        sums = sums + flipped(sums, axis, by)
    stats = sums / (rows * 256)

    image_grad = projected(scale, images, img_recv)
    text_grad = projected(scale, texts, txt_total)
    return image_grad, text_grad, stats


def solution(mesh):
    fine = Mesh(mesh.devices.reshape(SIZES), AXES)
    whole = P(AXES, None)
    return jax.shard_map(
        on_device, mesh=fine, in_specs=(whole, whole, P(), P()), out_specs=(whole, whole, P()), check_vma=False
    )
```

time: 396 us -> 143 us (0.36)
  waiting for transfers between devices: 261 us -> 65.9 us
  blocking collectives: 76.9 us -> 0 us
  starting transfers between devices: 0.16 us -> 47.2 us
  matrix products: 25.3 us -> 9.15 us
  between operations: 15.2 us -> 2.18 us
  Pallas kernels: 0 us -> 10.8 us
  other arithmetic: 14 us -> 5.44 us
    all_gather x2 -> x0, waiting for transfers between devices: 133 us -> none  [the longest x1 92.7 us: on_device(): piece = lax.all_gather(txt_low, 'dp', axis=0, tiled=True)]
    reduce_scatter x2 -> x0, waiting for transfers between devices: 128 us -> none  [the longest x1 128 us: on_device(): txt_part = lax.psum_scatter(txt_acc, 'dp', scatter_dimension=0, tiled=True)]
    psum x1 -> x0, blocking collectives: 76.9 us -> none  [on_device(): overall = lax.psum(totals, ('dp', 'grp'))]
    ppermute x0 -> x24, waiting for transfers between devices: none -> 55.6 us  [the longest x16 31.6 us: shifted(): return lax.ppermute(array, AXES, pairs)]
    ppermute x0 -> x24, starting transfers between devices: none -> 31.4 us  [the longest x16 21.6 us: shifted(): return lax.ppermute(array, AXES, pairs)]
    dot_general x3, matrix products: 25.3 us -> 9.15 us  [the longest x1 4.6 us: on_device(): lax.dot_general(grad_low, imgs, (((0,), (0,)), ((), ())), preferred_eleme...]
    all_to_all x0 -> x2, starting transfers between devices: none -> 15.8 us  [the longest x1 8.35 us: on_device(): img_recv = lax.all_to_all(img_part, PLANE, 0, 0)]
    pallas_call x0 -> x5, Pallas kernels: none -> 10.8 us  [the longest x1 6.79 us: pairs(): pl.pallas_call(pair_kernel, grid=(count // rows,), in_specs=[SMEM, SMEM,...]
  transfers between devices with their start and end apart: 4 -> 26, of which waited for: 3 -> 18; matrix products, arithmetic and copies ran while one was open for 5% -> 6% of each run, Pallas kernels for 0% -> 2%
where the time goes in v1:
time: 143 us
  waiting for transfers between devices  65.9 us (46%)
  starting transfers between devices  47.2 us (33%)
  Pallas kernels  10.8 us (8%)
  matrix products  9.15 us (6%)
  other arithmetic  5.44 us (4%)
  local copies, waits for them, and re-layouts  2.23 us (2%)
  between operations  2.18 us (2%)
    ppermute x16, waiting for transfers between devices, shifted(): return lax.ppermute(array, AXES, pairs)  31.6 us
    ppermute x8, waiting for transfers between devices, flipped(): return lax.ppermute(array, AXES, pairs)  24 us
    ppermute x16, starting transfers between devices, shifted(): return lax.ppermute(array, AXES, pairs)  21.6 us
    all_to_all x1, waiting for transfers between devices, on_device(): imgs = lax.all_to_all(copies, PLANE, 0, 0).reshape(PEERS * rows, emb)  10.2 us
    ppermute x8, starting transfers between devices, flipped(): return lax.ppermute(array, AXES, pairs)  9.76 us
    all_to_all x1, starting transfers between devices, on_device(): img_recv = lax.all_to_all(img_part, PLANE, 0, 0)  8.35 us
    all_to_all x1, starting transfers between devices, on_device(): imgs = lax.all_to_all(copies, PLANE, 0, 0).reshape(PEERS * rows, emb)  7.48 us
    pallas_call x1, Pallas kernels, pairs(): pl.pallas_call(pair_kernel, grid=(count // rows,), in_specs=[SMEM, SMEM,...  6.79 us
  transfers between devices with their start and end apart: 26, of which 18 were waited for; matrix products, arithmetic and copies ran while one was open for 6% of the time, Pallas kernels for 2%

profile of v1, /device:TPU:2, one launch (start us, length us, event | category | flops | bytes accessed | tf_op | source)
XLA Modules:
  0.0 142.8 jit_solution(6872213252440599218)
XLA Ops:
  1.7 2.0 %collective-permute-start = (bf16[64,1152]{1,0:T(8,128)(2,1)S(1)}, bf16[64,1152]{1,0:T(8,128)(2,1)S(1)}, u32[]{:S(2)}, u32[]{:S(2)}) collective-permute-start(bf16[64,1152]{1,0:T(8,128)(2,1)S(1)} %shard_map.68), channel_id=1, source_target_pairs={{0,16},{1,17},{2,18},{3,19},{4,20},{5,21},{6,22},{7,23},{8,24},{9,... | collective-permute-start | bytes 442376 | tf_op jit(solution)/shard_map/ppermute | solution.py:47
  3.7 4.0 %collective-permute-start.4 = (bf16[64,1152]{1,0:T(8,128)(2,1)S(1)}, bf16[64,1152]{1,0:T(8,128)(2,1)S(1)}, u32[]{:S(2)}, u32[]{:S(2)}) collective-permute-start(bf16[64,1152]{1,0:T(8,128)(2,1)S(1)} %shard_map.68), channel_id=1, source_target_pairs={{0,112},{1,113},{2,114},{3,115},{4,116},{5,117},{6,118},{7,119},{8... | collective-permute-start | bytes 442376 | tf_op jit(solution)/shard_map/ppermute | solution.py:47
  8.6 1.7 %shard_map.67 = bf16[16,64,1152]{2,1,0:T(8,128)(2,1)} custom-call(bf16[64,1152]{1,0:T(8,128)(2,1)S(1)} %copy-done), custom_call_target="tpu_custom_call" | custom-call | flops 1000000 | bytes 3145728 | tf_op jit(solution)/shard_map/pallas_call | solution.py:200
  10.3 7.5 %all-to-all-start = ((bf16[16,64,1152]{2,1,0:T(8,128)(2,1)}), bf16[16,64,1152]{2,1,0:T(8,128)(2,1)}, u32[]{:S(2)}, u32[]{:S(2)}) async-start(bf16[16,64,1152]{2,1,0:T(8,128)(2,1)} %shard_map.67), calls=%async_computation | async-start | bytes 4718592 | tf_op jit(solution)/shard_map/all_to_all | solution.py:217
  17.9 3.2 %collective-permute-start.5 = (bf16[64,1152]{1,0:T(8,128)(2,1)S(1)}, bf16[64,1152]{1,0:T(8,128)(2,1)S(1)}, u32[]{:S(2)}, u32[]{:S(2)}) collective-permute-start(bf16[64,1152]{1,0:T(8,128)(2,1)S(1)} %collective-permute-done.4), channel_id=1, source_target_pairs={{0,112},{1,113},{2,114},{3,115},{4,116},{5,117},{6,118},{7,119},{8... | collective-permute-start | bytes 442376 | tf_op jit(solution)/shard_map/ppermute | solution.py:47
  21.2 3.1 %collective-permute-done.1 = bf16[64,1152]{1,0:T(8,128)(2,1)S(1)} collective-permute-done((bf16[64,1152]{1,0:T(8,128)(2,1)S(1)}, bf16[64,1152]{1,0:T(8,128)(2,1)S(1)}, u32[]{:S(2)}, u32[]{:S(2)}) %collective-permute-start.1) | collective-permute-done | bytes 147488 | tf_op jit(solution)/shard_map/ppermute | solution.py:47
  24.3 3.2 %collective-permute-start.6 = (bf16[64,1152]{1,0:T(8,128)(2,1)S(1)}, bf16[64,1152]{1,0:T(8,128)(2,1)S(1)}, u32[]{:S(2)}, u32[]{:S(2)}) collective-permute-start(bf16[64,1152]{1,0:T(8,128)(2,1)S(1)} %collective-permute-done.5), channel_id=1, source_target_pairs={{0,112},{1,113},{2,114},{3,115},{4,116},{5,117},{6,118},{7,119},{8... | collective-permute-start | bytes 442376 | tf_op jit(solution)/shard_map/ppermute | solution.py:47
  27.5 3.1 %collective-permute-done.2 = bf16[64,1152]{1,0:T(8,128)(2,1)S(1)} collective-permute-done((bf16[64,1152]{1,0:T(8,128)(2,1)S(1)}, bf16[64,1152]{1,0:T(8,128)(2,1)S(1)}, u32[]{:S(2)}, u32[]{:S(2)}) %collective-permute-start.2) | collective-permute-done | bytes 147488 | tf_op jit(solution)/shard_map/ppermute | solution.py:47
  30.7 6.3 %collective-permute-done.3 = bf16[64,1152]{1,0:T(8,128)(2,1)S(1)} collective-permute-done((bf16[64,1152]{1,0:T(8,128)(2,1)S(1)}, bf16[64,1152]{1,0:T(8,128)(2,1)S(1)}, u32[]{:S(2)}, u32[]{:S(2)}) %collective-permute-start.3) | collective-permute-done | bytes 147488 | tf_op jit(solution)/shard_map/ppermute | solution.py:47
  40.0 10.2 %all-to-all-done = bf16[16,64,1152]{2,1,0:T(8,128)(2,1)} async-done(((bf16[16,64,1152]{2,1,0:T(8,128)(2,1)}), bf16[16,64,1152]{2,1,0:T(8,128)(2,1)}, u32[]{:S(2)}, u32[]{:S(2)}) %all-to-all-start) | async-done | bytes 2359328 | tf_op jit(solution)/shard_map/all_to_all | solution.py:217
  50.2 6.8 %shard_map.69 = (bf16[1024,1024]{1,0:T(8,128)(2,1)S(1)}, f32[24,128]{1,0:T(8,128)S(1)}) custom-call(s32[1]{0:T(128)} %bitcast.first_ref, f32[1]{0:T(128)S(6)} %exp.3.scale_ref, f32[1]{0:T(128)S(6)} %copy.15.shift_ref, bf16[1024,1152]{1,0:T(8,128)(2,1)} %bitcast.1.img_ref, bf16[512,1152]{1,0:T(8,128)(2,1)S(1)} %constant_dynamic-update-slice_fusion.mine_ref, ...), custom_call_target="tpu_custom_call" | custom-call | flops 2415919104 | bytes 8388608 | tf_op jit(solution)/shard_map/pallas_call | solution.py:149
  57.0 4.6 %fusion.6 = f32[1024,1152]{1,0:T(8,128)S(1)} fusion(bf16[1024,1024]{1,0:T(8,128)(2,1)S(1)} %get-tuple-element.5, bf16[1024,1152]{1,0:T(8,128)(2,1)} %bitcast.1.img_ref), kind=kOutput, calls=%fused_computation.23 | convolution fusion | flops 2415919104 | bytes 9175040 | tf_op jit(solution)/shard_map/dot_general | solution.py:233
  62.1 1.5 %fusion.1 = f32[1024,1152]{1,0:T(8,128)S(1)} fusion(bf16[512,1152]{1,0:T(8,128)(2,1)S(1)} %collective-permute-done.7.theirs_ref, bf16[1024,1024]{1,0:T(8,128)(2,1)S(1)} %get-tuple-element.5), kind=kOutput, calls=%fused_computation.3 | convolution fusion | flops 1207959552 | bytes 6946816 | tf_op jit(solution)/shard_map/dot_general | solution.py:229
  63.6 3.0 %collective-permute-done.8 = f32[512,1152]{1,0:T(8,128)S(1)} collective-permute-done((f32[512,1152]{1,0:T(8,128)S(1)}, f32[512,1152]{1,0:T(8,128)S(1)}, u32[]{:S(2)}, u32[]{:S(2)}) %collective-permute-start.8) | collective-permute-done | bytes 2359328 | tf_op jit(solution)/shard_map/ppermute | solution.py:47
  68.1 3.0 %fusion = bf16[1024,1152]{1,0:T(8,128)(2,1)} fusion(f32[1024,1152]{1,0:T(8,128)S(1)} %fusion.1, bf16[512,1152]{1,0:T(8,128)(2,1)S(1)} %constant_dynamic-update-slice_fusion.mine_ref, bf16[1024,1024]{1,0:T(8,128)(2,1)S(1)} %get-tuple-element.5), kind=kOutput, calls=%fused_computation.1 | convolution fusion | flops 1210318848 | bytes 9306112 | tf_op jit(solution)/shard_map/dot_general | solution.py:229
  71.1 8.4 %all-to-all-start.1 = ((bf16[16,64,1152]{2,1,0:T(8,128)(2,1)}), bf16[16,64,1152]{2,1,0:T(8,128)(2,1)S(1)}, u32[]{:S(2)}, u32[]{:S(2)}) async-start(bf16[16,64,1152]{2,1,0:T(8,128)(2,1)} %bitcast.9), calls=%async_computation.1 | async-start | bytes 4718592 | tf_op jit(solution)/shard_map/all_to_all | solution.py:235
  82.7 6.2 %collective-permute-done.10 = f32[64,1152]{1,0:T(8,128)S(1)} collective-permute-done((f32[64,1152]{1,0:T(8,128)S(1)}, f32[64,1152]{1,0:T(8,128)S(1)}, u32[]{:S(2)}, u32[]{:S(2)}) %collective-permute-start.10) | collective-permute-done | bytes 294944 | tf_op jit(solution)/shard_map/ppermute | solution.py:47
  88.9 1.9 %collective-permute-done.13 = f32[64,1152]{1,0:T(8,128)S(1)} collective-permute-done((f32[64,1152]{1,0:T(8,128)S(1)}, f32[64,1152]{1,0:T(8,128)S(1)}, u32[]{:S(2)}, u32[]{:S(2)}) %collective-permute-start.13) | collective-permute-done | bytes 294944 | tf_op jit(solution)/shard_map/ppermute | solution.py:47
  92.3 1.7 %collective-permute-start.14 = (f32[64,1152]{1,0:T(8,128)S(1)}, f32[64,1152]{1,0:T(8,128)S(1)}, u32[]{:S(2)}, u32[]{:S(2)}) collective-permute-start(f32[64,1152]{1,0:T(8,128)S(1)} %get-tuple-element.10), channel_id=1, source_target_pairs={{0,16},{1,17},{2,18},{3,19},{4,20},{5,21},{6,22},{7,23},{8,24},{9,... | collective-permute-start | bytes 884744 | tf_op jit(solution)/shard_map/ppermute | solution.py:47
  94.0 5.0 %collective-permute-done.11 = f32[64,1152]{1,0:T(8,128)S(1)} collective-permute-done((f32[64,1152]{1,0:T(8,128)S(1)}, f32[64,1152]{1,0:T(8,128)S(1)}, u32[]{:S(2)}, u32[]{:S(2)}) %collective-permute-start.11) | collective-permute-done | bytes 294944 | tf_op jit(solution)/shard_map/ppermute | solution.py:47
  99.0 1.5 %collective-permute-done.14 = f32[64,1152]{1,0:T(8,128)S(1)} collective-permute-done((f32[64,1152]{1,0:T(8,128)S(1)}, f32[64,1152]{1,0:T(8,128)S(1)}, u32[]{:S(2)}, u32[]{:S(2)}) %collective-permute-start.14) | collective-permute-done | bytes 294944 | tf_op jit(solution)/shard_map/ppermute | solution.py:47
  102.0 3.0 %collective-permute-start.12 = (f32[64,1152]{1,0:T(8,128)S(1)}, f32[64,1152]{1,0:T(8,128)}, u32[]{:S(2)}, u32[]{:S(2)}) collective-permute-start(f32[64,1152]{1,0:T(8,128)S(1)} %get-tuple-element.7), channel_id=1, source_target_pairs={{0,112},{1,113},{2,114},{3,115},{4,116},{5,117},{6,118},{7,119},{8... | collective-permute-start | bytes 884744 | tf_op jit(solution)/shard_map/ppermute | solution.py:47
  106.5 2.5 %collective-permute-start.17 = (f32[3]{0:T(128)S(1)}, f32[3]{0:T(128)S(1)}, u32[]{:S(2)}, u32[]{:S(2)}) collective-permute-start(f32[3]{0:T(128)S(1)} %add.68), channel_id=1, source_target_pairs={{0,64},{1,65},{2,66},{3,67},{4,68},{5,69},{6,70},{7,71},{8,72},{9,... | collective-permute-start | bytes 44 | tf_op jit(solution)/shard_map/ppermute | solution.py:56
  109.0 5.0 %collective-permute-done.17 = f32[3]{0:T(128)S(1)} collective-permute-done((f32[3]{0:T(128)S(1)}, f32[3]{0:T(128)S(1)}, u32[]{:S(2)}, u32[]{:S(2)}) %collective-permute-start.17) | collective-permute-done | bytes 44 | tf_op jit(solution)/shard_map/ppermute | solution.py:56
  113.9 4.4 %collective-permute-done.18 = f32[3]{0:T(128)S(1)} collective-permute-done((f32[3]{0:T(128)S(1)}, f32[3]{0:T(128)S(1)}, u32[]{:S(2)}, u32[]{:S(2)}) %collective-permute-start.18) | collective-permute-done | bytes 44 | tf_op jit(solution)/shard_map/ppermute | solution.py:56
  118.4 3.5 %collective-permute-done.19 = f32[3]{0:T(128)S(1)} collective-permute-done((f32[3]{0:T(128)S(1)}, f32[3]{0:T(128)S(1)}, u32[]{:S(2)}, u32[]{:S(2)}) %collective-permute-start.19) | collective-permute-done | bytes 44 | tf_op jit(solution)/shard_map/ppermute | solution.py:56
  121.9 2.1 %collective-permute-start.20 = (f32[3]{0:T(128)S(1)}, f32[3]{0:T(128)S(1)}, u32[]{:S(2)}, u32[]{:S(2)}) collective-permute-start(f32[3]{0:T(128)S(1)} %add.71), channel_id=1, source_target_pairs={{0,128},{1,129},{2,130},{3,131},{4,132},{5,133},{6,134},{7,135},{8... | collective-permute-start | bytes 44 | tf_op jit(solution)/shard_map/ppermute | solution.py:56
  124.0 3.0 %collective-permute-done.20 = f32[3]{0:T(128)S(1)} collective-permute-done((f32[3]{0:T(128)S(1)}, f32[3]{0:T(128)S(1)}, u32[]{:S(2)}, u32[]{:S(2)}) %collective-permute-start.20) | collective-permute-done | bytes 44 | tf_op jit(solution)/shard_map/ppermute | solution.py:56
  127.0 3.0 %collective-permute-start.21 = (f32[3]{0:T(128)S(1)}, f32[3]{0:T(128)S(1)}, u32[]{:S(2)}, u32[]{:S(2)}) collective-permute-start(f32[3]{0:T(128)S(1)} %add.72), channel_id=1, source_target_pairs={{0,4},{1,5},{2,6},{3,7},{4,0},{5,1},{6,2},{7,3},{8,12},{9,13},{10,... | collective-permute-start | bytes 44 | tf_op jit(solution)/shard_map/ppermute | solution.py:56
  129.9 2.1 %collective-permute-done.21 = f32[3]{0:T(128)S(1)} collective-permute-done((f32[3]{0:T(128)S(1)}, f32[3]{0:T(128)S(1)}, u32[]{:S(2)}, u32[]{:S(2)}) %collective-permute-start.21) | collective-permute-done | bytes 44 | tf_op jit(solution)/shard_map/ppermute | solution.py:56
  133.5 2.1 %collective-permute-done.22 = f32[3]{0:T(128)S(1)} collective-permute-done((f32[3]{0:T(128)S(1)}, f32[3]{0:T(128)S(1)}, u32[]{:S(2)}, u32[]{:S(2)}) %collective-permute-start.22) | collective-permute-done | bytes 44 | tf_op jit(solution)/shard_map/ppermute | solution.py:56
  136.2 2.9 %collective-permute-done.23 = f32[3]{0:T(128)S(1)} collective-permute-done((f32[3]{0:T(128)S(1)}, f32[3]{0:T(128)S(1)}, u32[]{:S(2)}, u32[]{:S(2)}) %collective-permute-start.23) | collective-permute-done | bytes 44 | tf_op jit(solution)/shard_map/ppermute | solution.py:56
  (64 shorter events, 19.2 us)
Async XLA Ops:
  0.6 0.9 copy-start.2
  1.7 16.2 %collective-permute-start = (bf16[64,1152]{1,0:T(8,128)(2,1)S(1)}, bf16[64,1152]{1,0:T(8,128)(2,1)S(1)}, u32[]{:S(2)}, u32[]{:S(2)}) collective-permute-start(bf16[64,1152]{1,0:T(8,128)(2,1)S(1)} %shard_map.68), channel_id=1, source_target_pairs={{0,16},{1,17},{2,18},{3,19},{4,20},{5,21},{6,22},{7,23},{8,24},{9,... | collective-permute-start | bytes 442376 | tf_op jit(solution)/shard_map/ppermute | solution.py:47
  3.7 14.3 %collective-permute-start.4 = (bf16[64,1152]{1,0:T(8,128)(2,1)S(1)}, bf16[64,1152]{1,0:T(8,128)(2,1)S(1)}, u32[]{:S(2)}, u32[]{:S(2)}) collective-permute-start(bf16[64,1152]{1,0:T(8,128)(2,1)S(1)} %shard_map.68), channel_id=1, source_target_pairs={{0,112},{1,113},{2,114},{3,115},{4,116},{5,117},{6,118},{7,119},{8... | collective-permute-start | bytes 442376 | tf_op jit(solution)/shard_map/ppermute | solution.py:47
  7.7 0.9 copy-start
  10.3 39.9 %all-to-all-start = ((bf16[16,64,1152]{2,1,0:T(8,128)(2,1)}), bf16[16,64,1152]{2,1,0:T(8,128)(2,1)}, u32[]{:S(2)}, u32[]{:S(2)}) async-start(bf16[16,64,1152]{2,1,0:T(8,128)(2,1)} %shard_map.67), calls=%async_computation | async-start | bytes 4718592 | tf_op jit(solution)/shard_map/all_to_all | solution.py:217
  17.8 6.4 %collective-permute-start.1 = (bf16[64,1152]{1,0:T(8,128)(2,1)S(1)}, bf16[64,1152]{1,0:T(8,128)(2,1)S(1)}, u32[]{:S(2)}, u32[]{:S(2)}) collective-permute-start(bf16[64,1152]{1,0:T(8,128)(2,1)S(1)} %collective-permute-done), channel_id=1, source_target_pairs={{0,16},{1,17},{2,18},{3,19},{4,20},{5,21},{6,22},{7,23},{8,24},{9,... | collective-permute-start | bytes 442376 | tf_op jit(solution)/shard_map/ppermute | solution.py:47
  17.9 6.3 %collective-permute-start.5 = (bf16[64,1152]{1,0:T(8,128)(2,1)S(1)}, bf16[64,1152]{1,0:T(8,128)(2,1)S(1)}, u32[]{:S(2)}, u32[]{:S(2)}) collective-permute-start(bf16[64,1152]{1,0:T(8,128)(2,1)S(1)} %collective-permute-done.4), channel_id=1, source_target_pairs={{0,112},{1,113},{2,114},{3,115},{4,116},{5,117},{6,118},{7,119},{8... | collective-permute-start | bytes 442376 | tf_op jit(solution)/shard_map/ppermute | solution.py:47
  24.3 6.4 %collective-permute-start.2 = (bf16[64,1152]{1,0:T(8,128)(2,1)S(1)}, bf16[64,1152]{1,0:T(8,128)(2,1)S(1)}, u32[]{:S(2)}, u32[]{:S(2)}) collective-permute-start(bf16[64,1152]{1,0:T(8,128)(2,1)S(1)} %collective-permute-done.1), channel_id=1, source_target_pairs={{0,16},{1,17},{2,18},{3,19},{4,20},{5,21},{6,22},{7,23},{8,24},{9,... | collective-permute-start | bytes 442376 | tf_op jit(solution)/shard_map/ppermute | solution.py:47
  24.3 12.7 %collective-permute-start.6 = (bf16[64,1152]{1,0:T(8,128)(2,1)S(1)}, bf16[64,1152]{1,0:T(8,128)(2,1)S(1)}, u32[]{:S(2)}, u32[]{:S(2)}) collective-permute-start(bf16[64,1152]{1,0:T(8,128)(2,1)S(1)} %collective-permute-done.5), channel_id=1, source_target_pairs={{0,112},{1,113},{2,114},{3,115},{4,116},{5,117},{6,118},{7,119},{8... | collective-permute-start | bytes 442376 | tf_op jit(solution)/shard_map/ppermute | solution.py:47
  30.6 6.4 %collective-permute-start.3 = (bf16[64,1152]{1,0:T(8,128)(2,1)S(1)}, bf16[64,1152]{1,0:T(8,128)(2,1)S(1)}, u32[]{:S(2)}, u32[]{:S(2)}) collective-permute-start(bf16[64,1152]{1,0:T(8,128)(2,1)S(1)} %collective-permute-done.2), channel_id=1, source_target_pairs={{0,16},{1,17},{2,18},{3,19},{4,20},{5,21},{6,22},{7,23},{8,24},{9,... | collective-permute-start | bytes 442376 | tf_op jit(solution)/shard_map/ppermute | solution.py:47
  37.1 2.9 %collective-permute-start.7 = (bf16[512,1152]{1,0:T(8,128)(2,1)S(1)}, bf16[512,1152]{1,0:T(8,128)(2,1)S(1)}, u32[]{:S(2)}, u32[]{:S(2)}) collective-permute-start(bf16[512,1152]{1,0:T(8,128)(2,1)S(1)} %constant_dynamic-update-slice_fusion.mine_ref), channel_id=1, source_target_pairs={{0,8},{1,9},{2,10},{3,11},{4,12},{5,13},{6,14},{7,15},{8,0},{9,1},... | collective-permute-start | bytes 3538952 | tf_op jit(solution)/shard_map/ppermute | solution.py:47
  61.8 4.8 %collective-permute-start.8 = (f32[512,1152]{1,0:T(8,128)S(1)}, f32[512,1152]{1,0:T(8,128)S(1)}, u32[]{:S(2)}, u32[]{:S(2)}) collective-permute-start(f32[512,1152]{1,0:T(8,128)S(1)} %slice.57), channel_id=1, source_target_pairs={{0,8},{1,9},{2,10},{3,11},{4,12},{5,13},{6,14},{7,15},{8,0},{9,1},... | collective-permute-start | bytes 7077896 | tf_op jit(solution)/shard_map/ppermute | solution.py:47
  66.9 4.3 %copy-start.4 = (f32[512,1152]{1,0:T(8,128)}, f32[512,1152]{1,0:T(8,128)S(1)}, u32[]{:S(2)}) copy-start(f32[512,1152]{1,0:T(8,128)S(1)} %slice_add_fusion) | copy-start | bytes 7077892
  66.9 12.6 %collective-permute-start.9 = (f32[64,1152]{1,0:T(8,128)S(1)}, f32[64,1152]{1,0:T(8,128)S(1)}, u32[]{:S(2)}, u32[]{:S(2)}) collective-permute-start(f32[64,1152]{1,0:T(8,128)S(1)} %slice.59), channel_id=1, source_target_pairs={{0,112},{1,113},{2,114},{3,115},{4,116},{5,117},{6,118},{7,119},{8... | collective-permute-start | bytes 884744 | tf_op jit(solution)/shard_map/ppermute | solution.py:47
  71.1 68.5 %all-to-all-start.1 = ((bf16[16,64,1152]{2,1,0:T(8,128)(2,1)}), bf16[16,64,1152]{2,1,0:T(8,128)(2,1)S(1)}, u32[]{:S(2)}, u32[]{:S(2)}) async-start(bf16[16,64,1152]{2,1,0:T(8,128)(2,1)} %bitcast.9), calls=%async_computation.1 | async-start | bytes 4718592 | tf_op jit(solution)/shard_map/all_to_all | solution.py:235
  80.6 59.0 %copy-start.1 = (bf16[64,1152]{1,0:T(8,128)(2,1)S(1)}, bf16[64,1152]{1,0:T(8,128)(2,1)}, u32[]{:S(2)}) copy-start(bf16[64,1152]{1,0:T(8,128)(2,1)} %rows_ref.6) | copy-start | bytes 442372
  80.6 8.3 %collective-permute-start.10 = (f32[64,1152]{1,0:T(8,128)S(1)}, f32[64,1152]{1,0:T(8,128)S(1)}, u32[]{:S(2)}, u32[]{:S(2)}) collective-permute-start(f32[64,1152]{1,0:T(8,128)S(1)} %get-tuple-element.11), channel_id=1, source_target_pairs={{0,112},{1,113},{2,114},{3,115},{4,116},{5,117},{6,118},{7,119},{8... | collective-permute-start | bytes 884744 | tf_op jit(solution)/shard_map/ppermute | solution.py:47
  81.7 9.1 %collective-permute-start.13 = (f32[64,1152]{1,0:T(8,128)S(1)}, f32[64,1152]{1,0:T(8,128)S(1)}, u32[]{:S(2)}, u32[]{:S(2)}) collective-permute-start(f32[64,1152]{1,0:T(8,128)S(1)} %get-tuple-element.12), channel_id=1, source_target_pairs={{0,16},{1,17},{2,18},{3,19},{4,20},{5,21},{6,22},{7,23},{8,24},{9,... | collective-permute-start | bytes 884744 | tf_op jit(solution)/shard_map/ppermute | solution.py:47
  91.9 7.1 %collective-permute-start.11 = (f32[64,1152]{1,0:T(8,128)S(1)}, f32[64,1152]{1,0:T(8,128)S(1)}, u32[]{:S(2)}, u32[]{:S(2)}) collective-permute-start(f32[64,1152]{1,0:T(8,128)S(1)} %get-tuple-element.9), channel_id=1, source_target_pairs={{0,112},{1,113},{2,114},{3,115},{4,116},{5,117},{6,118},{7,119},{8... | collective-permute-start | bytes 884744 | tf_op jit(solution)/shard_map/ppermute | solution.py:47
  92.3 8.2 %collective-permute-start.14 = (f32[64,1152]{1,0:T(8,128)S(1)}, f32[64,1152]{1,0:T(8,128)S(1)}, u32[]{:S(2)}, u32[]{:S(2)}) collective-permute-start(f32[64,1152]{1,0:T(8,128)S(1)} %get-tuple-element.10), channel_id=1, source_target_pairs={{0,16},{1,17},{2,18},{3,19},{4,20},{5,21},{6,22},{7,23},{8,24},{9,... | collective-permute-start | bytes 884744 | tf_op jit(solution)/shard_map/ppermute | solution.py:47
  101.6 40.3 %copy-start.3 = (bf16[64,1152]{1,0:T(8,128)(2,1)S(1)}, bf16[64,1152]{1,0:T(8,128)(2,1)}, u32[]{:S(2)}) copy-start(bf16[64,1152]{1,0:T(8,128)(2,1)} %rows_ref.7) | copy-start | bytes 442372
  101.6 39.2 %collective-permute-start.15 = (f32[64,1152]{1,0:T(8,128)S(1)}, f32[64,1152]{1,0:T(8,128)S(1)}, u32[]{:S(2)}, u32[]{:S(2)}) collective-permute-start(f32[64,1152]{1,0:T(8,128)S(1)} %get-tuple-element.8), channel_id=1, source_target_pairs={{0,16},{1,17},{2,18},{3,19},{4,20},{5,21},{6,22},{7,23},{8,24},{9,... | collective-permute-start | bytes 884744 | tf_op jit(solution)/shard_map/ppermute | solution.py:47
  102.0 38.8 %collective-permute-start.12 = (f32[64,1152]{1,0:T(8,128)S(1)}, f32[64,1152]{1,0:T(8,128)}, u32[]{:S(2)}, u32[]{:S(2)}) collective-permute-start(f32[64,1152]{1,0:T(8,128)S(1)} %get-tuple-element.7), channel_id=1, source_target_pairs={{0,112},{1,113},{2,114},{3,115},{4,116},{5,117},{6,118},{7,119},{8... | collective-permute-start | bytes 884744 | tf_op jit(solution)/shard_map/ppermute | solution.py:47
  105.3 1.2 collective-permute-start.16
  106.5 7.4 %collective-permute-start.17 = (f32[3]{0:T(128)S(1)}, f32[3]{0:T(128)S(1)}, u32[]{:S(2)}, u32[]{:S(2)}) collective-permute-start(f32[3]{0:T(128)S(1)} %add.68), channel_id=1, source_target_pairs={{0,64},{1,65},{2,66},{3,67},{4,68},{5,69},{6,70},{7,71},{8,72},{9,... | collective-permute-start | bytes 44 | tf_op jit(solution)/shard_map/ppermute | solution.py:56
  113.9 4.4 %collective-permute-start.18 = (f32[3]{0:T(128)S(1)}, f32[3]{0:T(128)S(1)}, u32[]{:S(2)}, u32[]{:S(2)}) collective-permute-start(f32[3]{0:T(128)S(1)} %add.69), channel_id=1, source_target_pairs={{0,32},{1,33},{2,34},{3,35},{4,36},{5,37},{6,38},{7,39},{8,40},{9,... | collective-permute-start | bytes 44 | tf_op jit(solution)/shard_map/ppermute | solution.py:56
  118.4 3.5 %collective-permute-start.19 = (f32[3]{0:T(128)S(1)}, f32[3]{0:T(128)S(1)}, u32[]{:S(2)}, u32[]{:S(2)}) collective-permute-start(f32[3]{0:T(128)S(1)} %add.70), channel_id=1, source_target_pairs={{0,16},{1,17},{2,18},{3,19},{4,20},{5,21},{6,22},{7,23},{8,24},{9,... | collective-permute-start | bytes 44 | tf_op jit(solution)/shard_map/ppermute | solution.py:56
  121.9 5.0 %collective-permute-start.20 = (f32[3]{0:T(128)S(1)}, f32[3]{0:T(128)S(1)}, u32[]{:S(2)}, u32[]{:S(2)}) collective-permute-start(f32[3]{0:T(128)S(1)} %add.71), channel_id=1, source_target_pairs={{0,128},{1,129},{2,130},{3,131},{4,132},{5,133},{6,134},{7,135},{8... | collective-permute-start | bytes 44 | tf_op jit(solution)/shard_map/ppermute | solution.py:56
  127.0 5.0 %collective-permute-start.21 = (f32[3]{0:T(128)S(1)}, f32[3]{0:T(128)S(1)}, u32[]{:S(2)}, u32[]{:S(2)}) collective-permute-start(f32[3]{0:T(128)S(1)} %add.72), channel_id=1, source_target_pairs={{0,4},{1,5},{2,6},{3,7},{4,0},{5,1},{6,2},{7,3},{8,12},{9,13},{10,... | collective-permute-start | bytes 44 | tf_op jit(solution)/shard_map/ppermute | solution.py:56
  132.0 3.5 %collective-permute-start.22 = (f32[3]{0:T(128)S(1)}, f32[3]{0:T(128)S(1)}, u32[]{:S(2)}, u32[]{:S(2)}) collective-permute-start(f32[3]{0:T(128)S(1)} %add.73), channel_id=1, source_target_pairs={{0,2},{1,3},{2,0},{3,1},{4,6},{5,7},{6,4},{7,5},{8,10},{9,11},{10,... | collective-permute-start | bytes 44 | tf_op jit(solution)/shard_map/ppermute | solution.py:56
  135.5 3.5 %collective-permute-start.23 = (f32[3]{0:T(128)S(1)}, f32[3]{0:T(128)S(1)}, u32[]{:S(2)}, u32[]{:S(2)}) collective-permute-start(f32[3]{0:T(128)S(1)} %add.74), channel_id=1, source_target_pairs={{0,1},{1,0},{2,3},{3,2},{4,5},{5,4},{6,7},{7,6},{8,9},{9,8},{10,11... | collective-permute-start | bytes 44 | tf_op jit(solution)/shard_map/ppermute | solution.py:56

commit v2 on v1

--- a/solution.py
+++ b/solution.py
@@ -14,6 +14,7 @@
 DEPTH = 8
 BF16 = jnp.bfloat16
 F32 = jnp.float32
+F16 = jnp.float16
 VMEM = pl.BlockSpec(memory_space=pltpu.VMEM)
 SMEM = pl.BlockSpec(memory_space=pltpu.SMEM)
 PARAMS = pltpu.CompilerParams(vmem_limit_bytes=48 * 1024 * 1024)
@@ -56,6 +57,10 @@
     return lax.ppermute(array, AXES, pairs)
 
 
+def joined(message, arrived):
+    return jnp.concatenate([message[:3] + arrived[:3], message[3:], arrived[3:]])
+
+
 def along_z(array, by):
     return shifted(array, 1, by)
 
@@ -100,7 +105,7 @@
     return out
 
 
-def pair_kernel(first_ref, scale_ref, shift_ref, img_ref, mine_ref, theirs_ref, grad_ref, sums_ref):
+def pair_kernel(first_ref, scale_ref, shift_ref, img_ref, mine_ref, theirs_ref, grad_ref, sums_ref, size_ref, acc_ref):
     tile = pl.program_id(0)
     rows = img_ref.shape[0]
     half = mine_ref.shape[0]
@@ -111,6 +116,7 @@
     loss_sum = jnp.zeros((8, 128), F32)
     scaled_sum = jnp.zeros((8, 128), F32)
     grad_sum = jnp.zeros((8, 128), F32)
+    size_sum = jnp.zeros((8, 128), F32)
     for side, txt_ref in enumerate((mine_ref, theirs_ref)):
         for at in range(0, half, wide):
             cosine = lax.dot_general(
@@ -130,16 +136,25 @@
                 grad = jnp.where(positive, grad - 1.0, grad)
             loss_sum += lanes(fold_sum(jnp.maximum(signed, 0.0)) + jnp.log1p(fold_growth(small)))
             scaled_sum += lanes(fold_sum(grad * scaled))
-            grad_sum += lanes(fold_sum(grad))
+            part = lanes(fold_sum(grad))
+            grad_sum += part
+            size_sum += lanes(fold_sum(jnp.abs(grad))) if side == 0 and at == 0 else part
             grad_ref[:, side * half + at : side * half + at + wide] = grad.astype(BF16)
 
     @pl.when(tile == 0)
     def _():
-        sums_ref[...] = jnp.zeros_like(sums_ref)
-
-    sums_ref[0:8, :] += loss_sum
-    sums_ref[8:16, :] += scaled_sum
-    sums_ref[16:24, :] += grad_sum
+        acc_ref[...] = jnp.zeros_like(acc_ref)
+
+    acc_ref[0] += loss_sum
+    acc_ref[1] += scaled_sum
+    acc_ref[2] += grad_sum
+    acc_ref[3] += size_sum
+
+    @pl.when(tile == pl.num_programs(0) - 1)
+    def _():
+        for k in range(3):
+            sums_ref[k] = jnp.sum(acc_ref[k])
+        size_ref[0] = jnp.sum(acc_ref[3])
 
 
 def pairs(first, scale, shift, imgs, mine, theirs):
@@ -159,28 +174,28 @@
         ],
         out_specs=[
             pl.BlockSpec((rows, 2 * half), lambda i: (i, 0)),
-            pl.BlockSpec((24, 128), lambda i: (0, 0)),
+            SMEM,
+            SMEM,
         ],
         out_shape=[
             jax.ShapeDtypeStruct((count, 2 * half), BF16),
-            jax.ShapeDtypeStruct((24, 128), F32),
+            jax.ShapeDtypeStruct((3,), F32),
+            jax.ShapeDtypeStruct((1,), F32),
         ],
+        scratch_shapes=[pltpu.VMEM((4, 8, 128), F32)],
         compiler_params=PARAMS,
         cost_estimate=cost(2 * count * 2 * half * emb, 8 * 2**20),
     )(first, scale, shift, imgs, mine, theirs)
 
 
-def project_kernel(scale_ref, rows_ref, parts_ref, out_ref):
+def project_kernel(scale_ref, rows_ref, total_ref, out_ref):
     unit, norms = unit_of(rows_ref)
-    total = parts_ref[0].astype(F32)
-    for k in range(1, parts_ref.shape[0]):
-        total = total + parts_ref[k].astype(F32)
-    direction = scale_ref[0] * total
+    direction = scale_ref[0] * total_ref[...]
     along = jnp.sum(direction * unit, axis=-1, keepdims=True)
     out_ref[...] = (direction - unit * along) / norms
 
 
-def projected(scale, rows, parts):
+def projected(scale, rows, total):
     return pl.pallas_call(
         project_kernel,
         in_specs=[SMEM, VMEM, VMEM],
@@ -188,7 +203,7 @@
         out_shape=jax.ShapeDtypeStruct(rows.shape, F32),
         compiler_params=PARAMS,
         cost_estimate=cost(10**6, 4 * 2**20),
-    )(scale, rows, parts)
+    )(scale, rows, total)
 
 
 def on_device(images, texts, log_scale, bias):
@@ -205,6 +220,7 @@
         compiler_params=PARAMS,
         cost_estimate=cost(10**6, 3 * 2**20),
     )(images)
+    copies, texts_later = lax.optimization_barrier((copies, texts))
     txt_low = pl.pallas_call(
         low_kernel,
         in_specs=[VMEM],
@@ -212,7 +228,7 @@
         out_shape=jax.ShapeDtypeStruct((rows, emb), BF16),
         compiler_params=PARAMS,
         cost_estimate=cost(10**6, 2**19),
-    )(texts)
+    )(texts_later)
 
     imgs = lax.all_to_all(copies, PLANE, 0, 0).reshape(PEERS * rows, emb)
     up, down = [txt_low], []
@@ -224,33 +240,62 @@
     mine = jnp.concatenate(up + down[::-1], axis=0)
     theirs = other_core(mine)
 
-    grad_low, sums = pairs(first, scale, bias, imgs, mine, theirs)
+    grad_low, sums, size = pairs(first, scale, bias, imgs, mine, theirs)
+    message = jnp.concatenate([sums, size])
+
     half = DEPTH * rows
+    arrived = flipped(message, 3, 2)
+    factor = 16384.0 / jnp.maximum(size[0], 1e-30)
     img_part = jnp.dot(grad_low[:, :half], mine, preferred_element_type=F32) + jnp.dot(
         grad_low[:, half:], theirs, preferred_element_type=F32
     )
-    img_part = img_part.astype(BF16).reshape(PEERS, rows, emb)
+    img_part = (img_part * factor).astype(F16).reshape(PEERS, rows, emb)
+    img_part, grad_low, arrived = lax.optimization_barrier((img_part, grad_low, arrived))
+    img_recv = lax.all_to_all(img_part, PLANE, 0, 0)
+    message = joined(message, arrived)
+
+    arrived = flipped(message, 3, 1)
     txt_part = lax.dot_general(grad_low, imgs, (((0,), (0,)), ((), ())), preferred_element_type=F32)
-
-    img_recv = lax.all_to_all(img_part, PLANE, 0, 0)
-
-    blocks = (txt_part[:half] + other_core(txt_part[half:])).reshape(DEPTH, rows, emb)
-    left = blocks[4]
-    for k in (3, 2, 1):
-        left = along_z(left, -1) + blocks[k]
+    txt_part, arrived = lax.optimization_barrier((txt_part, arrived))
+    message = joined(message, arrived)
+
+    blocks = other_core(txt_part[half:])
+    arrived = flipped(message, 0, 1)
+    blocks, arrived = lax.optimization_barrier((blocks, arrived))
+    blocks = (txt_part[:half] + blocks).reshape(DEPTH, rows, emb)
+    message = joined(message, arrived)
+
+    left, right = along_z(blocks[4], -1), along_z(blocks[5], 1)
+    arrived = flipped(message, 4, 1)
+    left, right, arrived = lax.optimization_barrier((left, right, arrived))
+    left, right = left + blocks[3], right + blocks[6]
+    message = joined(message, arrived)
+    sums, sizes = message[:3], message[3:]
+
+    left, right = along_z(left, -1), along_z(right, 1)
+    arrived = flipped(sums, 1, 4)
+    left, right, arrived = lax.optimization_barrier((left, right, arrived))
+    left, right, sums = left + blocks[2], right + blocks[7], sums + arrived
+
+    left, right = along_z(left, -1), along_z(right, 1)
+    arrived = flipped(sums, 1, 2)
+    left, right, arrived = lax.optimization_barrier((left, right, arrived))
+    left, sums = left + blocks[1], sums + arrived
+
     left = along_z(left, -1)
-    right = blocks[5]
-    for k in (6, 7):
-        right = along_z(right, 1) + blocks[k]
-    right = along_z(right, 1)
-    txt_total = (blocks[0] + left + right)[None]
-
-    sums = jnp.sum(sums.reshape(3, -1), axis=-1)
-    for axis, by in ((2, 1), (1, 4), (1, 2), (1, 1), (0, 1), (3, 2), (3, 1), (4, 1)):
-        sums = sums + flipped(sums, axis, by)
-    stats = sums / (rows * 256)
-
-    image_grad = projected(scale, images, img_recv)
+    arrived = flipped(sums, 1, 1)
+    left, arrived = lax.optimization_barrier((left, arrived))
+    txt_total, sums = blocks[0] + left + right, sums + arrived
+    stats = (sums + flipped(sums, 2, 1)) / (rows * 256)
+
+    mine_at = (lax.axis_index("x_lo") << 3) | (lax.axis_index("x_hi") << 2) | ((lax.axis_index("y") & 1) << 1) | (lax.axis_index("y") >> 1)
+    peer = jnp.arange(PEERS)
+    peer_at = ((peer & 1) << 3) | ((peer >> 3) << 2) | (((peer >> 1) & 1) << 1) | ((peer >> 2) & 1)
+    chosen = (peer_at ^ mine_at)[:, None] == jnp.arange(PEERS)[None, :]
+    weights = jnp.sum(jnp.where(chosen, jnp.maximum(sizes, 1e-30)[None, :], 0.0), axis=1) / 16384.0
+    img_total = jnp.sum(img_recv.astype(F32) * weights[:, None, None], axis=0)
+
+    image_grad = projected(scale, images, img_total)
     text_grad = projected(scale, texts, txt_total)
     return image_grad, text_grad, stats
 

time: 143 us -> 158 us (1.10)
  the two profiles are of different devices: /device:TPU:2 before, /device:TPU:7 now
where the time goes in v2:
time: 158 us; the launch traced here: 157 us
  starting transfers between devices  63.2 us (40%)
  waiting for transfers between devices  57.8 us (37%)
  Pallas kernels  11.4 us (7%)
  matrix products  9.15 us (6%)
  other arithmetic  7.58 us (5%)
  local copies, waits for them, and re-layouts  5.49 us (3%)
  between operations  2.84 us (2%)
    ppermute x8, waiting for transfers between devices, flipped(): return lax.ppermute(array, AXES, pairs)  37.2 us
    ppermute x16, starting transfers between devices, shifted(): return lax.ppermute(array, AXES, pairs)  29.9 us
    ppermute x8, starting transfers between devices, flipped(): return lax.ppermute(array, AXES, pairs)  22 us
    ppermute x16, waiting for transfers between devices, shifted(): return lax.ppermute(array, AXES, pairs)  15.6 us
    pallas_call x1, Pallas kernels, pairs(): pl.pallas_call(pair_kernel, grid=(count // rows,), in_specs=[SMEM, SMEM,...  7.64 us
    all_to_all x1, starting transfers between devices, on_device(): imgs = lax.all_to_all(copies, PLANE, 0, 0).reshape(PEERS * rows, emb)  6.86 us
    all_to_all x1, waiting for transfers between devices, on_device(): imgs = lax.all_to_all(copies, PLANE, 0, 0).reshape(PEERS * rows, emb)  5.03 us
    dot_general x1, matrix products, on_device(): lax.dot_general(grad_low, imgs, (((0,), (0,)), ((), ())), preferred_eleme...  4.6 us
  transfers between devices with their start and end apart: 26, of which 12 were waited for; matrix products, arithmetic and copies ran while one was open for 11% of the time, Pallas kernels for 1%

profile of v2, /device:TPU:7, one launch (start us, length us, event | category | flops | bytes accessed | tf_op | source)
XLA Modules:
  0.0 157.5 jit_solution(11051974436214607457)
XLA Ops:
  1.5 1.7 %shard_map.67 = bf16[16,64,1152]{2,1,0:T(8,128)(2,1)} custom-call(bf16[64,1152]{1,0:T(8,128)(2,1)S(1)} %copy-done), custom_call_target="tpu_custom_call" | custom-call | flops 1000000 | bytes 3145728 | tf_op jit(solution)/shard_map/pallas_call | solution.py:215
  3.4 5.7 %collective-permute-start.4 = (bf16[64,1152]{1,0:T(8,128)(2,1)S(1)}, bf16[64,1152]{1,0:T(8,128)(2,1)S(1)}, u32[]{:S(2)}, u32[]{:S(2)}) collective-permute-start(bf16[64,1152]{1,0:T(8,128)(2,1)S(1)} %shard_map.68), channel_id=1, source_target_pairs={{0,112},{1,113},{2,114},{3,115},{4,116},{5,117},{6,118},{7,119},{8... | collective-permute-start | bytes 442376 | tf_op jit(solution)/shard_map/ppermute | solution.py:48
  9.1 6.9 %all-to-all-start = ((bf16[16,64,1152]{2,1,0:T(8,128)(2,1)}), bf16[16,64,1152]{2,1,0:T(8,128)(2,1)}, u32[]{:S(2)}, u32[]{:S(2)}) async-start(bf16[16,64,1152]{2,1,0:T(8,128)(2,1)} %shard_map.67), calls=%async_computation | async-start | bytes 4718592 | tf_op jit(solution)/shard_map/all_to_all | solution.py:233
  16.0 2.7 %collective-permute-start.5 = (bf16[64,1152]{1,0:T(8,128)(2,1)S(1)}, bf16[64,1152]{1,0:T(8,128)(2,1)S(1)}, u32[]{:S(2)}, u32[]{:S(2)}) collective-permute-start(bf16[64,1152]{1,0:T(8,128)(2,1)S(1)} %collective-permute-done.4), channel_id=1, source_target_pairs={{0,112},{1,113},{2,114},{3,115},{4,116},{5,117},{6,118},{7,119},{8... | collective-permute-start | bytes 442376 | tf_op jit(solution)/shard_map/ppermute | solution.py:48
  18.7 2.1 %collective-permute-done.5 = bf16[64,1152]{1,0:T(8,128)(2,1)S(1)} collective-permute-done((bf16[64,1152]{1,0:T(8,128)(2,1)S(1)}, bf16[64,1152]{1,0:T(8,128)(2,1)S(1)}, u32[]{:S(2)}, u32[]{:S(2)}) %collective-permute-start.5) | collective-permute-done | bytes 147488 | tf_op jit(solution)/shard_map/ppermute | solution.py:48
  20.8 3.5 %collective-permute-start.6 = (bf16[64,1152]{1,0:T(8,128)(2,1)S(1)}, bf16[64,1152]{1,0:T(8,128)(2,1)S(1)}, u32[]{:S(2)}, u32[]{:S(2)}) collective-permute-start(bf16[64,1152]{1,0:T(8,128)(2,1)S(1)} %collective-permute-done.5), channel_id=1, source_target_pairs={{0,112},{1,113},{2,114},{3,115},{4,116},{5,117},{6,118},{7,119},{8... | collective-permute-start | bytes 442376 | tf_op jit(solution)/shard_map/ppermute | solution.py:48
  24.3 5.6 %collective-permute-done.2 = bf16[64,1152]{1,0:T(8,128)(2,1)S(1)} collective-permute-done((bf16[64,1152]{1,0:T(8,128)(2,1)S(1)}, bf16[64,1152]{1,0:T(8,128)(2,1)S(1)}, u32[]{:S(2)}, u32[]{:S(2)}) %collective-permute-start.2) | collective-permute-done | bytes 147488 | tf_op jit(solution)/shard_map/ppermute | solution.py:48
  29.9 5.6 %collective-permute-done.3 = bf16[64,1152]{1,0:T(8,128)(2,1)S(1)} collective-permute-done((bf16[64,1152]{1,0:T(8,128)(2,1)S(1)}, bf16[64,1152]{1,0:T(8,128)(2,1)S(1)}, u32[]{:S(2)}, u32[]{:S(2)}) %collective-permute-start.3) | collective-permute-done | bytes 147488 | tf_op jit(solution)/shard_map/ppermute | solution.py:48
  35.6 4.4 %collective-permute-start.7 = (bf16[512,1152]{1,0:T(8,128)(2,1)S(1)}, bf16[512,1152]{1,0:T(8,128)(2,1)S(1)}, u32[]{:S(2)}, u32[]{:S(2)}) collective-permute-start(bf16[512,1152]{1,0:T(8,128)(2,1)S(1)} %constant_dynamic-update-slice_fusion.mine_ref), channel_id=1, source_target_pairs={{0,8},{1,9},{2,10},{3,11},{4,12},{5,13},{6,14},{7,15},{8,0},{9,1},... | collective-permute-start | bytes 3538952 | tf_op jit(solution)/shard_map/ppermute | solution.py:48
  42.5 5.0 %all-to-all-done = bf16[16,64,1152]{2,1,0:T(8,128)(2,1)} async-done(((bf16[16,64,1152]{2,1,0:T(8,128)(2,1)}), bf16[16,64,1152]{2,1,0:T(8,128)(2,1)}, u32[]{:S(2)}, u32[]{:S(2)}) %all-to-all-start) | async-done | bytes 2359328 | tf_op jit(solution)/shard_map/all_to_all | solution.py:233
  47.5 7.6 %shard_map.69 = (bf16[1024,1024]{1,0:T(8,128)(2,1)S(1)}, f32[3]{0:T(128)S(1)}, f32[1]{0:T(128)}) custom-call(s32[1]{0:T(128)} %bitcast.first_ref, f32[1]{0:T(128)S(6)} %exp.3.scale_ref, f32[1]{0:T(128)S(6)} %copy.15.shift_ref, bf16[1024,1152]{1,0:T(8,128)(2,1)} %bitcast.1.img_ref, bf16[512,1152]{1,0:T(8,128)(2,1)S(1)} %constant_dynamic-update-slice_fusion.mine_ref, ...), custom_call_target="tpu_custom_call" | custom-call | flops 2415919104 | bytes 8388608 | tf_op jit(solution)/shard_map/pallas_call | solution.py:164
  56.6 1.5 fusion.2
  58.2 3.0 %fusion.1 = f16[1024,1152]{1,0:T(8,128)(2,1)} fusion(f32[1024,1152]{1,0:T(8,128)S(1)} %fusion.2, bf16[512,1152]{1,0:T(8,128)(2,1)S(1)} %constant_dynamic-update-slice_fusion.mine_ref, f32[]{:T(128)} %bitcast.2, bf16[1024,1024]{1,0:T(8,128)(2,1)S(1)} %get-tuple-element.33), kind=kOutput, calls=%fused_computation.3 | convolution fusion | flops 1211498496 | bytes 9306116 | tf_op jit(solution)/shard_map/dot_general | solution.py:249
  61.8 1.4 pad_maximum_fusion.1
  63.2 4.4 %collective-permute-start.9 = (f32[5]{0:T(128)S(1)}, f32[5]{0:T(128)S(1)}, u32[]{:S(2)}, u32[]{:S(2)}) collective-permute-start(f32[5]{0:T(128)S(1)} %pad_maximum_fusion.1), channel_id=1, source_target_pairs={{0,2},{1,3},{2,0},{3,1},{4,6},{5,7},{6,4},{7,5},{8,10},{9,11},{10,... | collective-permute-start | bytes 68 | tf_op jit(solution)/shard_map/ppermute | solution.py:57
  67.6 4.6 %fusion.16 = f32[1024,1152]{1,0:T(8,128)S(1)} fusion(bf16[1024,1024]{1,0:T(8,128)(2,1)S(1)} %get-tuple-element.33, bf16[1024,1152]{1,0:T(8,128)(2,1)} %bitcast.1.img_ref), kind=kOutput, calls=%fused_computation.49 | convolution fusion | flops 2415919104 | bytes 9175040 | tf_op jit(solution)/shard_map/dot_general | solution.py:258
  72.4 2.9 %collective-permute-start.10 = (f32[512,1152]{1,0:T(8,128)S(1)}, f32[512,1152]{1,0:T(8,128)S(1)}, u32[]{:S(2)}, u32[]{:S(2)}) collective-permute-start(f32[512,1152]{1,0:T(8,128)S(1)} %slice.79), channel_id=1, source_target_pairs={{0,8},{1,9},{2,10},{3,11},{4,12},{5,13},{6,14},{7,15},{8,0},{9,1},... | collective-permute-start | bytes 7077896 | tf_op jit(solution)/shard_map/ppermute | solution.py:48
  75.4 1.4 pad_maximum_fusion.2
  76.7 1.6 %collective-permute-start.11 = (f32[7]{0:T(128)S(1)}, f32[7]{0:T(128)S(1)}, u32[]{:S(2)}, u32[]{:S(2)}) collective-permute-start(f32[7]{0:T(128)S(1)} %pad_maximum_fusion.2), channel_id=1, source_target_pairs={{0,128},{1,129},{2,130},{3,131},{4,132},{5,133},{6,134},{7,135},{8... | collective-permute-start | bytes 92 | tf_op jit(solution)/shard_map/ppermute | solution.py:57
  78.4 2.3 %collective-permute-done.11 = f32[7]{0:T(128)S(1)} collective-permute-done((f32[7]{0:T(128)S(1)}, f32[7]{0:T(128)S(1)}, u32[]{:S(2)}, u32[]{:S(2)}) %collective-permute-start.11) | collective-permute-done | bytes 60 | tf_op jit(solution)/shard_map/ppermute | solution.py:57
  81.6 2.7 %collective-permute-start.12 = (f32[64,1152]{1,0:T(8,128)S(1)}, f32[64,1152]{1,0:T(8,128)S(1)}, u32[]{:S(2)}, u32[]{:S(2)}) collective-permute-start(f32[64,1152]{1,0:T(8,128)S(1)} %get-tuple-element.54), channel_id=1, source_target_pairs={{0,112},{1,113},{2,114},{3,115},{4,116},{5,117},{6,118},{7,119},{8... | collective-permute-start | bytes 884744 | tf_op jit(solution)/shard_map/ppermute | solution.py:48
  84.3 4.5 %all-to-all-start.1 = ((f16[16,64,1152]{2,1,0:T(8,128)(2,1)}), f16[16,64,1152]{2,1,0:T(8,128)(2,1)}, u32[]{:S(2)}, u32[]{:S(2)}) async-start(f16[16,64,1152]{2,1,0:T(8,128)(2,1)} %bitcast.3), calls=%async_computation.1 | async-start | bytes 4718592 | tf_op jit(solution)/shard_map/all_to_all | solution.py:254
  90.8 24.8 %collective-permute-done.14 = f32[11]{0:T(128)S(1)} collective-permute-done((f32[11]{0:T(128)S(1)}, f32[11]{0:T(128)S(1)}, u32[]{:S(2)}, u32[]{:S(2)}) %collective-permute-start.14) | collective-permute-done | bytes 76 | tf_op jit(solution)/shard_map/ppermute | solution.py:57
  116.4 1.6 %collective-permute-start.16 = (f32[64,1152]{1,0:T(8,128)}, f32[64,1152]{1,0:T(8,128)S(1)}, u32[]{:S(2)}, u32[]{:S(2)}) collective-permute-start(f32[64,1152]{1,0:T(8,128)} %get-tuple-element.51), channel_id=1, source_target_pairs={{0,16},{1,17},{2,18},{3,19},{4,20},{5,21},{6,22},{7,23},{8,24},{9,... | collective-permute-start | bytes 884744 | tf_op jit(solution)/shard_map/ppermute | solution.py:48
  120.5 3.4 %collective-permute-start.17 = (f32[3]{0:T(128)S(1)}, f32[3]{0:T(128)S(1)}, u32[]{:S(2)}, u32[]{:S(2)}) collective-permute-start(f32[3]{0:T(128)S(1)} %slice_add_fusion.7), channel_id=1, source_target_pairs={{0,64},{1,65},{2,66},{3,67},{4,68},{5,69},{6,70},{7,71},{8,72},{9,... | collective-permute-start | bytes 44 | tf_op jit(solution)/shard_map/ppermute | solution.py:57
  123.9 3.0 %collective-permute-done.17 = f32[3]{0:T(128)S(1)} collective-permute-done((f32[3]{0:T(128)S(1)}, f32[3]{0:T(128)S(1)}, u32[]{:S(2)}, u32[]{:S(2)}) %collective-permute-start.17) | collective-permute-done | bytes 44 | tf_op jit(solution)/shard_map/ppermute | solution.py:57
  127.4 2.3 %collective-permute-start.18 = (f32[64,1152]{1,0:T(8,128)S(1)}, f32[64,1152]{1,0:T(8,128)S(1)}, u32[]{:S(2)}, u32[]{:S(2)}) collective-permute-start(f32[64,1152]{1,0:T(8,128)S(1)} %get-tuple-element.50), channel_id=1, source_target_pairs={{0,112},{1,113},{2,114},{3,115},{4,116},{5,117},{6,118},{7,119},{8... | collective-permute-start | bytes 884744 | tf_op jit(solution)/shard_map/ppermute | solution.py:48
  130.0 3.5 %collective-permute-done.20 = f32[3]{0:T(128)S(1)} collective-permute-done((f32[3]{0:T(128)S(1)}, f32[3]{0:T(128)S(1)}, u32[]{:S(2)}, u32[]{:S(2)}) %collective-permute-start.20) | collective-permute-done | bytes 44 | tf_op jit(solution)/shard_map/ppermute | solution.py:57
  134.8 2.5 %collective-permute-start.21 = (f32[64,1152]{1,0:T(8,128)S(1)}, f32[64,1152]{1,0:T(8,128)S(1)}, u32[]{:S(2)}, u32[]{:S(2)}) collective-permute-start(f32[64,1152]{1,0:T(8,128)S(1)} %slice_add_fusion.1), channel_id=1, source_target_pairs={{0,112},{1,113},{2,114},{3,115},{4,116},{5,117},{6,118},{7,119},{8... | collective-permute-start | bytes 884744 | tf_op jit(solution)/shard_map/ppermute | solution.py:48
  137.4 2.2 %multiply_reduce_fusion.total_ref = f32[64,1152]{1,0:T(8,128)S(1)} fusion(f16[16,64,1152]{2,1,0:T(8,128)(2,1)} %all-to-all-done.1, f32[16]{0:T(128)S(1)} %broadcast_multiply_fusion), kind=kLoop, calls=%fused_computation.2 | loop fusion | flops 3465216 | bytes 2654272 | tf_op jit(solution)/shard_map/reduce_sum | solution.py:296
  140.6 2.7 %collective-permute-done.22 = f32[3]{0:T(128)S(1)} collective-permute-done((f32[3]{0:T(128)S(1)}, f32[3]{0:T(128)S(1)}, u32[]{:S(2)}, u32[]{:S(2)}) %collective-permute-start.22) | collective-permute-done | bytes 44 | tf_op jit(solution)/shard_map/ppermute | solution.py:57
  144.3 11.8 %collective-permute-start.23 = (f32[3]{0:T(128)S(1)}, f32[3]{0:T(128)S(1)}, u32[]{:S(2)}, u32[]{:S(2)}) collective-permute-start(f32[3]{0:T(128)S(1)} %add.74), channel_id=1, source_target_pairs={{0,8},{1,9},{2,10},{3,11},{4,12},{5,13},{6,14},{7,15},{8,0},{9,1},... | collective-permute-start | bytes 44 | tf_op jit(solution)/shard_map/ppermute | solution.py:57
  (71 shorter events, 15.7 us)
Async XLA Ops:
  0.6 0.9 copy-start
  1.5 1.7 %copy-start.2 = (bf16[64,1152]{1,0:T(8,128)(2,1)S(1)}, bf16[64,1152]{1,0:T(8,128)(2,1)}, u32[]{:S(2)}) copy-start(bf16[64,1152]{1,0:T(8,128)(2,1)} %rows_ref.6) | copy-start | bytes 442372
  3.4 12.5 %collective-permute-start.4 = (bf16[64,1152]{1,0:T(8,128)(2,1)S(1)}, bf16[64,1152]{1,0:T(8,128)(2,1)S(1)}, u32[]{:S(2)}, u32[]{:S(2)}) collective-permute-start(bf16[64,1152]{1,0:T(8,128)(2,1)S(1)} %shard_map.68), channel_id=1, source_target_pairs={{0,112},{1,113},{2,114},{3,115},{4,116},{5,117},{6,118},{7,119},{8... | collective-permute-start | bytes 442376 | tf_op jit(solution)/shard_map/ppermute | solution.py:48
  9.1 9.6 %collective-permute-start = (bf16[64,1152]{1,0:T(8,128)(2,1)S(1)}, bf16[64,1152]{1,0:T(8,128)(2,1)S(1)}, u32[]{:S(2)}, u32[]{:S(2)}) collective-permute-start(bf16[64,1152]{1,0:T(8,128)(2,1)S(1)} %shard_map.68), channel_id=1, source_target_pairs={{0,16},{1,17},{2,18},{3,19},{4,20},{5,21},{6,22},{7,23},{8,24},{9,... | collective-permute-start | bytes 442376 | tf_op jit(solution)/shard_map/ppermute | solution.py:48
  9.1 38.5 %all-to-all-start = ((bf16[16,64,1152]{2,1,0:T(8,128)(2,1)}), bf16[16,64,1152]{2,1,0:T(8,128)(2,1)}, u32[]{:S(2)}, u32[]{:S(2)}) async-start(bf16[16,64,1152]{2,1,0:T(8,128)(2,1)} %shard_map.67), calls=%async_computation | async-start | bytes 4718592 | tf_op jit(solution)/shard_map/all_to_all | solution.py:233
  16.0 4.9 %collective-permute-start.5 = (bf16[64,1152]{1,0:T(8,128)(2,1)S(1)}, bf16[64,1152]{1,0:T(8,128)(2,1)S(1)}, u32[]{:S(2)}, u32[]{:S(2)}) collective-permute-start(bf16[64,1152]{1,0:T(8,128)(2,1)S(1)} %collective-permute-done.4), channel_id=1, source_target_pairs={{0,112},{1,113},{2,114},{3,115},{4,116},{5,117},{6,118},{7,119},{8... | collective-permute-start | bytes 442376 | tf_op jit(solution)/shard_map/ppermute | solution.py:48
  18.7 5.6 %collective-permute-start.1 = (bf16[64,1152]{1,0:T(8,128)(2,1)S(1)}, bf16[64,1152]{1,0:T(8,128)(2,1)S(1)}, u32[]{:S(2)}, u32[]{:S(2)}) collective-permute-start(bf16[64,1152]{1,0:T(8,128)(2,1)S(1)} %collective-permute-done), channel_id=1, source_target_pairs={{0,16},{1,17},{2,18},{3,19},{4,20},{5,21},{6,22},{7,23},{8,24},{9,... | collective-permute-start | bytes 442376 | tf_op jit(solution)/shard_map/ppermute | solution.py:48
  20.8 14.7 %collective-permute-start.6 = (bf16[64,1152]{1,0:T(8,128)(2,1)S(1)}, bf16[64,1152]{1,0:T(8,128)(2,1)S(1)}, u32[]{:S(2)}, u32[]{:S(2)}) collective-permute-start(bf16[64,1152]{1,0:T(8,128)(2,1)S(1)} %collective-permute-done.5), channel_id=1, source_target_pairs={{0,112},{1,113},{2,114},{3,115},{4,116},{5,117},{6,118},{7,119},{8... | collective-permute-start | bytes 442376 | tf_op jit(solution)/shard_map/ppermute | solution.py:48
  24.3 5.6 %collective-permute-start.2 = (bf16[64,1152]{1,0:T(8,128)(2,1)S(1)}, bf16[64,1152]{1,0:T(8,128)(2,1)S(1)}, u32[]{:S(2)}, u32[]{:S(2)}) collective-permute-start(bf16[64,1152]{1,0:T(8,128)(2,1)S(1)} %collective-permute-done.1), channel_id=1, source_target_pairs={{0,16},{1,17},{2,18},{3,19},{4,20},{5,21},{6,22},{7,23},{8,24},{9,... | collective-permute-start | bytes 442376 | tf_op jit(solution)/shard_map/ppermute | solution.py:48
  29.9 5.6 %collective-permute-start.3 = (bf16[64,1152]{1,0:T(8,128)(2,1)S(1)}, bf16[64,1152]{1,0:T(8,128)(2,1)S(1)}, u32[]{:S(2)}, u32[]{:S(2)}) collective-permute-start(bf16[64,1152]{1,0:T(8,128)(2,1)S(1)} %collective-permute-done.2), channel_id=1, source_target_pairs={{0,16},{1,17},{2,18},{3,19},{4,20},{5,21},{6,22},{7,23},{8,24},{9,... | collective-permute-start | bytes 442376 | tf_op jit(solution)/shard_map/ppermute | solution.py:48
  35.6 6.9 %collective-permute-start.7 = (bf16[512,1152]{1,0:T(8,128)(2,1)S(1)}, bf16[512,1152]{1,0:T(8,128)(2,1)S(1)}, u32[]{:S(2)}, u32[]{:S(2)}) collective-permute-start(bf16[512,1152]{1,0:T(8,128)(2,1)S(1)} %constant_dynamic-update-slice_fusion.mine_ref), channel_id=1, source_target_pairs={{0,8},{1,9},{2,10},{3,11},{4,12},{5,13},{6,14},{7,15},{8,0},{9,1},... | collective-permute-start | bytes 3538952 | tf_op jit(solution)/shard_map/ppermute | solution.py:48
  56.5 4.7 %collective-permute-start.8 = (f32[4]{0:T(128)S(1)}, f32[4]{0:T(128)S(1)}, u32[]{:S(2)}, u32[]{:S(2)}) collective-permute-start(f32[4]{0:T(128)S(1)} %pad_maximum_fusion), channel_id=1, source_target_pairs={{0,4},{1,5},{2,6},{3,7},{4,0},{5,1},{6,2},{7,3},{8,12},{9,13},{10,... | collective-permute-start | bytes 56 | tf_op jit(solution)/shard_map/ppermute | solution.py:57
  63.2 9.0 %collective-permute-start.9 = (f32[5]{0:T(128)S(1)}, f32[5]{0:T(128)S(1)}, u32[]{:S(2)}, u32[]{:S(2)}) collective-permute-start(f32[5]{0:T(128)S(1)} %pad_maximum_fusion.1), channel_id=1, source_target_pairs={{0,2},{1,3},{2,0},{3,1},{4,6},{5,7},{6,4},{7,5},{8,10},{9,11},{10,... | collective-permute-start | bytes 68 | tf_op jit(solution)/shard_map/ppermute | solution.py:57
  72.4 8.3 %collective-permute-start.10 = (f32[512,1152]{1,0:T(8,128)S(1)}, f32[512,1152]{1,0:T(8,128)S(1)}, u32[]{:S(2)}, u32[]{:S(2)}) collective-permute-start(f32[512,1152]{1,0:T(8,128)S(1)} %slice.79), channel_id=1, source_target_pairs={{0,8},{1,9},{2,10},{3,11},{4,12},{5,13},{6,14},{7,15},{8,0},{9,1},... | collective-permute-start | bytes 7077896 | tf_op jit(solution)/shard_map/ppermute | solution.py:48
  76.7 3.9 %collective-permute-start.11 = (f32[7]{0:T(128)S(1)}, f32[7]{0:T(128)S(1)}, u32[]{:S(2)}, u32[]{:S(2)}) collective-permute-start(f32[7]{0:T(128)S(1)} %pad_maximum_fusion.2), channel_id=1, source_target_pairs={{0,128},{1,129},{2,130},{3,131},{4,132},{5,133},{6,134},{7,135},{8... | collective-permute-start | bytes 92 | tf_op jit(solution)/shard_map/ppermute | solution.py:57
  81.6 34.0 %collective-permute-start.13 = (f32[64,1152]{1,0:T(8,128)}, f32[64,1152]{1,0:T(8,128)S(1)}, u32[]{:S(2)}, u32[]{:S(2)}) collective-permute-start(f32[64,1152]{1,0:T(8,128)} %get-tuple-element.53), channel_id=1, source_target_pairs={{0,16},{1,17},{2,18},{3,19},{4,20},{5,21},{6,22},{7,23},{8,24},{9,... | collective-permute-start | bytes 884744 | tf_op jit(solution)/shard_map/ppermute | solution.py:48
  81.6 34.0 %collective-permute-start.12 = (f32[64,1152]{1,0:T(8,128)S(1)}, f32[64,1152]{1,0:T(8,128)S(1)}, u32[]{:S(2)}, u32[]{:S(2)}) collective-permute-start(f32[64,1152]{1,0:T(8,128)S(1)} %get-tuple-element.54), channel_id=1, source_target_pairs={{0,112},{1,113},{2,114},{3,115},{4,116},{5,117},{6,118},{7,119},{8... | collective-permute-start | bytes 884744 | tf_op jit(solution)/shard_map/ppermute | solution.py:48
  84.3 53.0 %all-to-all-start.1 = ((f16[16,64,1152]{2,1,0:T(8,128)(2,1)}), f16[16,64,1152]{2,1,0:T(8,128)(2,1)}, u32[]{:S(2)}, u32[]{:S(2)}) async-start(f16[16,64,1152]{2,1,0:T(8,128)(2,1)} %bitcast.3), calls=%async_computation.1 | async-start | bytes 4718592 | tf_op jit(solution)/shard_map/all_to_all | solution.py:254
  90.2 25.4 %collective-permute-start.14 = (f32[11]{0:T(128)S(1)}, f32[11]{0:T(128)S(1)}, u32[]{:S(2)}, u32[]{:S(2)}) collective-permute-start(f32[11]{0:T(128)S(1)} %concatenate.34), channel_id=1, source_target_pairs={{0,1},{1,0},{2,3},{3,2},{4,5},{5,4},{6,7},{7,6},{8,9},{9,8},{10,11... | collective-permute-start | bytes 140 | tf_op jit(solution)/shard_map/ppermute | solution.py:57
  116.4 10.5 %collective-permute-start.16 = (f32[64,1152]{1,0:T(8,128)}, f32[64,1152]{1,0:T(8,128)S(1)}, u32[]{:S(2)}, u32[]{:S(2)}) collective-permute-start(f32[64,1152]{1,0:T(8,128)} %get-tuple-element.51), channel_id=1, source_target_pairs={{0,16},{1,17},{2,18},{3,19},{4,20},{5,21},{6,22},{7,23},{8,24},{9,... | collective-permute-start | bytes 884744 | tf_op jit(solution)/shard_map/ppermute | solution.py:48
  118.0 8.9 %collective-permute-start.15 = (f32[64,1152]{1,0:T(8,128)S(1)}, f32[64,1152]{1,0:T(8,128)S(1)}, u32[]{:S(2)}, u32[]{:S(2)}) collective-permute-start(f32[64,1152]{1,0:T(8,128)S(1)} %get-tuple-element.52), channel_id=1, source_target_pairs={{0,112},{1,113},{2,114},{3,115},{4,116},{5,117},{6,118},{7,119},{8... | collective-permute-start | bytes 884744 | tf_op jit(solution)/shard_map/ppermute | solution.py:48
  120.5 6.4 %collective-permute-start.17 = (f32[3]{0:T(128)S(1)}, f32[3]{0:T(128)S(1)}, u32[]{:S(2)}, u32[]{:S(2)}) collective-permute-start(f32[3]{0:T(128)S(1)} %slice_add_fusion.7), channel_id=1, source_target_pairs={{0,64},{1,65},{2,66},{3,67},{4,68},{5,69},{6,70},{7,71},{8,72},{9,... | collective-permute-start | bytes 44 | tf_op jit(solution)/shard_map/ppermute | solution.py:57
  127.0 12.6 %copy-start.1 = (bf16[64,1152]{1,0:T(8,128)(2,1)S(1)}, bf16[64,1152]{1,0:T(8,128)(2,1)}, u32[]{:S(2)}) copy-start(bf16[64,1152]{1,0:T(8,128)(2,1)} %rows_ref.5) | copy-start | bytes 442372
  127.0 7.8 %collective-permute-start.19 = (f32[64,1152]{1,0:T(8,128)S(1)}, f32[64,1152]{1,0:T(8,128)S(1)}, u32[]{:S(2)}, u32[]{:S(2)}) collective-permute-start(f32[64,1152]{1,0:T(8,128)S(1)} %get-tuple-element.49), channel_id=1, source_target_pairs={{0,16},{1,17},{2,18},{3,19},{4,20},{5,21},{6,22},{7,23},{8,24},{9,... | collective-permute-start | bytes 884744 | tf_op jit(solution)/shard_map/ppermute | solution.py:48
  127.4 7.3 %collective-permute-start.18 = (f32[64,1152]{1,0:T(8,128)S(1)}, f32[64,1152]{1,0:T(8,128)S(1)}, u32[]{:S(2)}, u32[]{:S(2)}) collective-permute-start(f32[64,1152]{1,0:T(8,128)S(1)} %get-tuple-element.50), channel_id=1, source_target_pairs={{0,112},{1,113},{2,114},{3,115},{4,116},{5,117},{6,118},{7,119},{8... | collective-permute-start | bytes 884744 | tf_op jit(solution)/shard_map/ppermute | solution.py:48
  129.9 3.6 %collective-permute-start.20 = (f32[3]{0:T(128)S(1)}, f32[3]{0:T(128)S(1)}, u32[]{:S(2)}, u32[]{:S(2)}) collective-permute-start(f32[3]{0:T(128)S(1)} %add.69), channel_id=1, source_target_pairs={{0,32},{1,33},{2,34},{3,35},{4,36},{5,37},{6,38},{7,39},{8,40},{9,... | collective-permute-start | bytes 44 | tf_op jit(solution)/shard_map/ppermute | solution.py:57
  134.8 8.5 %collective-permute-start.21 = (f32[64,1152]{1,0:T(8,128)S(1)}, f32[64,1152]{1,0:T(8,128)S(1)}, u32[]{:S(2)}, u32[]{:S(2)}) collective-permute-start(f32[64,1152]{1,0:T(8,128)S(1)} %slice_add_fusion.1), channel_id=1, source_target_pairs={{0,112},{1,113},{2,114},{3,115},{4,116},{5,117},{6,118},{7,119},{8... | collective-permute-start | bytes 884744 | tf_op jit(solution)/shard_map/ppermute | solution.py:48
  140.6 2.8 %collective-permute-start.22 = (f32[3]{0:T(128)S(1)}, f32[3]{0:T(128)S(1)}, u32[]{:S(2)}, u32[]{:S(2)}) collective-permute-start(f32[3]{0:T(128)S(1)} %add.71), channel_id=1, source_target_pairs={{0,16},{1,17},{2,18},{3,19},{4,20},{5,21},{6,22},{7,23},{8,24},{9,... | collective-permute-start | bytes 44 | tf_op jit(solution)/shard_map/ppermute | solution.py:57
  144.3 12.6 %collective-permute-start.23 = (f32[3]{0:T(128)S(1)}, f32[3]{0:T(128)S(1)}, u32[]{:S(2)}, u32[]{:S(2)}) collective-permute-start(f32[3]{0:T(128)S(1)} %add.74), channel_id=1, source_target_pairs={{0,8},{1,9},{2,10},{3,11},{4,12},{5,13},{6,14},{7,15},{8,0},{9,1},... | collective-permute-start | bytes 44 | tf_op jit(solution)/shard_map/ppermute | solution.py:57

commit v3 on v2

--- a/solution.py
+++ b/solution.py
@@ -57,8 +57,20 @@
     return lax.ppermute(array, AXES, pairs)
 
 
+def moved(array, dx, dy):
+    pairs = []
+    for source in range(256):
+        x_hi, z, core, y, x_lo = place(source)
+        x = (x_hi * 2 + x_lo + dx) % 4
+        pairs.append((source, number((x // 2, z, core, (y + dy) % 4, x % 2))))
+    return lax.ppermute(array, AXES, pairs)
+
+
 def joined(message, arrived):
-    return jnp.concatenate([message[:3] + arrived[:3], message[3:], arrived[3:]])
+    sums = message[:3]
+    for other in arrived:
+        sums = sums + other[:3]
+    return jnp.concatenate([sums, message[3:]] + [other[3:] for other in arrived])
 
 
 def along_z(array, by):
@@ -241,57 +253,50 @@
     theirs = other_core(mine)
 
     grad_low, sums, size = pairs(first, scale, bias, imgs, mine, theirs)
+    half = DEPTH * rows
+
     message = jnp.concatenate([sums, size])
-
-    half = DEPTH * rows
-    arrived = flipped(message, 3, 2)
+    arrived = [moved(message, by, 0) for by in (1, 2, 3)]
+    txt_part = lax.dot_general(grad_low, imgs, (((0,), (0,)), ((), ())), preferred_element_type=F32)
+    txt_part, grad_low, *arrived = lax.optimization_barrier((txt_part, grad_low, *arrived))
+    message = joined(message, arrived)
+
+    arrived = [moved(message, 0, by) for by in (1, 2, 3)]
     factor = 16384.0 / jnp.maximum(size[0], 1e-30)
     img_part = jnp.dot(grad_low[:, :half], mine, preferred_element_type=F32) + jnp.dot(
         grad_low[:, half:], theirs, preferred_element_type=F32
     )
     img_part = (img_part * factor).astype(F16).reshape(PEERS, rows, emb)
-    img_part, grad_low, arrived = lax.optimization_barrier((img_part, grad_low, arrived))
+    img_part, *arrived = lax.optimization_barrier((img_part, *arrived))
     img_recv = lax.all_to_all(img_part, PLANE, 0, 0)
     message = joined(message, arrived)
-
-    arrived = flipped(message, 3, 1)
-    txt_part = lax.dot_general(grad_low, imgs, (((0,), (0,)), ((), ())), preferred_element_type=F32)
-    txt_part, arrived = lax.optimization_barrier((txt_part, arrived))
-    message = joined(message, arrived)
-
-    blocks = other_core(txt_part[half:])
-    arrived = flipped(message, 0, 1)
-    blocks, arrived = lax.optimization_barrier((blocks, arrived))
-    blocks = (txt_part[:half] + blocks).reshape(DEPTH, rows, emb)
-    message = joined(message, arrived)
-
+    sums, sizes = message[:3], message[3:]
+
+    blocks = (txt_part[:half] + other_core(txt_part[half:])).reshape(DEPTH, rows, emb)
     left, right = along_z(blocks[4], -1), along_z(blocks[5], 1)
-    arrived = flipped(message, 4, 1)
-    left, right, arrived = lax.optimization_barrier((left, right, arrived))
-    left, right = left + blocks[3], right + blocks[6]
-    message = joined(message, arrived)
-    sums, sizes = message[:3], message[3:]
-
-    left, right = along_z(left, -1), along_z(right, 1)
     arrived = flipped(sums, 1, 4)
     left, right, arrived = lax.optimization_barrier((left, right, arrived))
-    left, right, sums = left + blocks[2], right + blocks[7], sums + arrived
+    left, right, sums = left + blocks[3], right + blocks[6], sums + arrived
 
     left, right = along_z(left, -1), along_z(right, 1)
     arrived = flipped(sums, 1, 2)
     left, right, arrived = lax.optimization_barrier((left, right, arrived))
+    left, right, sums = left + blocks[2], right + blocks[7], sums + arrived
+
+    left, right = along_z(left, -1), along_z(right, 1)
+    arrived = flipped(sums, 1, 1)
+    left, right, arrived = lax.optimization_barrier((left, right, arrived))
     left, sums = left + blocks[1], sums + arrived
 
     left = along_z(left, -1)
-    arrived = flipped(sums, 1, 1)
-    left, arrived = lax.optimization_barrier((left, arrived))
-    txt_total, sums = blocks[0] + left + right, sums + arrived
+    txt_total = blocks[0] + left + right
     stats = (sums + flipped(sums, 2, 1)) / (rows * 256)
 
-    mine_at = (lax.axis_index("x_lo") << 3) | (lax.axis_index("x_hi") << 2) | ((lax.axis_index("y") & 1) << 1) | (lax.axis_index("y") >> 1)
+    x, y = lax.axis_index("x_hi") * 2 + lax.axis_index("x_lo"), lax.axis_index("y")
     peer = jnp.arange(PEERS)
-    peer_at = ((peer & 1) << 3) | ((peer >> 3) << 2) | (((peer >> 1) & 1) << 1) | ((peer >> 2) & 1)
-    chosen = (peer_at ^ mine_at)[:, None] == jnp.arange(PEERS)[None, :]
+    peer_x, peer_y = (peer >> 3) * 2 + (peer & 1), (peer >> 1) & 3
+    entry = ((y - peer_y) & 3) * 4 + ((x - peer_x) & 3)
+    chosen = entry[:, None] == peer[None, :]
     weights = jnp.sum(jnp.where(chosen, jnp.maximum(sizes, 1e-30)[None, :], 0.0), axis=1) / 16384.0
     img_total = jnp.sum(img_recv.astype(F32) * weights[:, None, None], axis=0)
 

time: 158 us -> 143 us (0.905)
  the two profiles are of different devices: /device:TPU:7 before, /device:TPU:2 now
where the time goes in v3:
time: 143 us; the launch traced here: 141 us
  starting transfers between devices  52.7 us (37%)
  waiting for transfers between devices  37.4 us (26%)
  local copies, waits for them, and re-layouts  15.8 us (11%)
  Pallas kernels  11.4 us (8%)
  other arithmetic  10.6 us (7%)
  matrix products  10.5 us (7%)
  between operations  2.83 us (2%)
    ppermute x16, starting transfers between devices, shifted(): return lax.ppermute(array, AXES, pairs)  26.2 us
    ppermute x16, waiting for transfers between devices, shifted(): return lax.ppermute(array, AXES, pairs)  17.7 us
    ppermute x4, waiting for transfers between devices, flipped(): return lax.ppermute(array, AXES, pairs)  13.7 us
    ppermute x6, starting transfers between devices, moved(): return lax.ppermute(array, AXES, pairs)  9.58 us
    pallas_call x1, Pallas kernels, pairs(): pl.pallas_call(pair_kernel, grid=(count // rows,), in_specs=[SMEM, SMEM,...  7.64 us
    all_to_all x1, starting transfers between devices, on_device(): imgs = lax.all_to_all(copies, PLANE, 0, 0).reshape(PEERS * rows, emb)  7.48 us
    all_to_all x1, starting transfers between devices, on_device(): img_recv = lax.all_to_all(img_part, PLANE, 0, 0)  6.37 us
    unnamed x21, local copies, waits for them, and re-layouts  5.98 us
  transfers between devices with their start and end apart: 28, of which 10 were waited for; matrix products, arithmetic and copies ran while one was open for 20% of the time, Pallas kernels for 1%

profile of v3, /device:TPU:2, one launch (start us, length us, event | category | flops | bytes accessed | tf_op | source)
XLA Modules:
  0.0 141.2 jit_solution(14994500457691151763)
XLA Ops:
  1.5 1.7 %shard_map.67 = bf16[16,64,1152]{2,1,0:T(8,128)(2,1)} custom-call(bf16[64,1152]{1,0:T(8,128)(2,1)S(1)} %copy-done), custom_call_target="tpu_custom_call" | custom-call | flops 1000000 | bytes 3145728 | tf_op jit(solution)/shard_map/pallas_call | solution.py:227
  3.4 5.9 %collective-permute-start.4 = (bf16[64,1152]{1,0:T(8,128)(2,1)S(1)}, bf16[64,1152]{1,0:T(8,128)(2,1)S(1)}, u32[]{:S(2)}, u32[]{:S(2)}) collective-permute-start(bf16[64,1152]{1,0:T(8,128)(2,1)S(1)} %shard_map.68), channel_id=1, source_target_pairs={{0,112},{1,113},{2,114},{3,115},{4,116},{5,117},{6,118},{7,119},{8... | collective-permute-start | bytes 442376 | tf_op jit(solution)/shard_map/ppermute | solution.py:48
  9.3 7.5 %all-to-all-start = ((bf16[16,64,1152]{2,1,0:T(8,128)(2,1)}), bf16[16,64,1152]{2,1,0:T(8,128)(2,1)}, u32[]{:S(2)}, u32[]{:S(2)}) async-start(bf16[16,64,1152]{2,1,0:T(8,128)(2,1)} %shard_map.67), calls=%async_computation | async-start | bytes 4718592 | tf_op jit(solution)/shard_map/all_to_all | solution.py:245
  16.8 3.3 %collective-permute-start.5 = (bf16[64,1152]{1,0:T(8,128)(2,1)S(1)}, bf16[64,1152]{1,0:T(8,128)(2,1)S(1)}, u32[]{:S(2)}, u32[]{:S(2)}) collective-permute-start(bf16[64,1152]{1,0:T(8,128)(2,1)S(1)} %collective-permute-done.4), channel_id=1, source_target_pairs={{0,112},{1,113},{2,114},{3,115},{4,116},{5,117},{6,118},{7,119},{8... | collective-permute-start | bytes 442376 | tf_op jit(solution)/shard_map/ppermute | solution.py:48
  20.2 2.6 %collective-permute-done.5 = bf16[64,1152]{1,0:T(8,128)(2,1)S(1)} collective-permute-done((bf16[64,1152]{1,0:T(8,128)(2,1)S(1)}, bf16[64,1152]{1,0:T(8,128)(2,1)S(1)}, u32[]{:S(2)}, u32[]{:S(2)}) %collective-permute-start.5) | collective-permute-done | bytes 147488 | tf_op jit(solution)/shard_map/ppermute | solution.py:48
  22.8 3.7 %collective-permute-start.6 = (bf16[64,1152]{1,0:T(8,128)(2,1)S(1)}, bf16[64,1152]{1,0:T(8,128)(2,1)S(1)}, u32[]{:S(2)}, u32[]{:S(2)}) collective-permute-start(bf16[64,1152]{1,0:T(8,128)(2,1)S(1)} %collective-permute-done.5), channel_id=1, source_target_pairs={{0,112},{1,113},{2,114},{3,115},{4,116},{5,117},{6,118},{7,119},{8... | collective-permute-start | bytes 442376 | tf_op jit(solution)/shard_map/ppermute | solution.py:48
  26.5 6.3 %collective-permute-done.2 = bf16[64,1152]{1,0:T(8,128)(2,1)S(1)} collective-permute-done((bf16[64,1152]{1,0:T(8,128)(2,1)S(1)}, bf16[64,1152]{1,0:T(8,128)(2,1)S(1)}, u32[]{:S(2)}, u32[]{:S(2)}) %collective-permute-start.2) | collective-permute-done | bytes 147488 | tf_op jit(solution)/shard_map/ppermute | solution.py:48
  32.9 6.3 %collective-permute-done.3 = bf16[64,1152]{1,0:T(8,128)(2,1)S(1)} collective-permute-done((bf16[64,1152]{1,0:T(8,128)(2,1)S(1)}, bf16[64,1152]{1,0:T(8,128)(2,1)S(1)}, u32[]{:S(2)}, u32[]{:S(2)}) %collective-permute-start.3) | collective-permute-done | bytes 147488 | tf_op jit(solution)/shard_map/ppermute | solution.py:48
  40.8 1.5 %collective-permute-done.7.theirs_ref = bf16[512,1152]{1,0:T(8,128)(2,1)S(1)} collective-permute-done((bf16[512,1152]{1,0:T(8,128)(2,1)S(1)}, bf16[512,1152]{1,0:T(8,128)(2,1)S(1)}, u32[]{:S(2)}, u32[]{:S(2)}) %collective-permute-start.7) | collective-permute-done | bytes 1179680 | tf_op jit(solution)/shard_map/ppermute | solution.py:48
  43.3 6.0 %all-to-all-done = bf16[16,64,1152]{2,1,0:T(8,128)(2,1)} async-done(((bf16[16,64,1152]{2,1,0:T(8,128)(2,1)}), bf16[16,64,1152]{2,1,0:T(8,128)(2,1)}, u32[]{:S(2)}, u32[]{:S(2)}) %all-to-all-start) | async-done | bytes 2359328 | tf_op jit(solution)/shard_map/all_to_all | solution.py:245
  50.5 7.6 %shard_map.69 = (bf16[1024,1024]{1,0:T(8,128)(2,1)S(1)}, f32[3]{0:T(128)S(1)}, f32[1]{0:T(128)}) custom-call(s32[1]{0:T(128)} %bitcast.first_ref, f32[1]{0:T(128)S(6)} %exp.3.scale_ref, f32[1]{0:T(128)S(6)} %copy.15.shift_ref, bf16[1024,1152]{1,0:T(8,128)(2,1)} %bitcast.1.img_ref, bf16[512,1152]{1,0:T(8,128)(2,1)S(1)} %constant_dynamic-update-slice_fusion.mine_ref, ...), custom_call_target="tpu_custom_call" | custom-call | flops 2415919104 | bytes 8388608 | tf_op jit(solution)/shard_map/pallas_call | solution.py:176
  58.8 1.6 %collective-permute-start.10 = (f32[4]{0:T(128)S(1)}, f32[4]{0:T(128)S(1)}, u32[]{:S(2)}, u32[]{:S(2)}) collective-permute-start(f32[4]{0:T(128)S(1)} %pad_maximum_fusion), channel_id=1, source_target_pairs={{0,129},{1,0},{2,131},{3,2},{4,133},{5,4},{6,135},{7,6},{8,137},{9... | collective-permute-start | bytes 56 | tf_op jit(solution)/shard_map/ppermute | solution.py:66
  61.6 2.0 %collective-permute-start.8 = (f32[4]{0:T(128)S(1)}, f32[4]{0:T(128)S(1)}, u32[]{:S(2)}, u32[]{:S(2)}) collective-permute-start(f32[4]{0:T(128)S(1)} %pad_maximum_fusion), channel_id=1, source_target_pairs={{0,1},{1,128},{2,3},{3,130},{4,5},{5,132},{6,7},{7,134},{8,9},{9,1... | collective-permute-start | bytes 56 | tf_op jit(solution)/shard_map/ppermute | solution.py:66
  63.6 4.7 %fusion.12 = f32[1024,1152]{1,0:T(8,128)S(1)} fusion(bf16[1024,1024]{1,0:T(8,128)(2,1)S(1)} %get-tuple-element.31, bf16[1024,1152]{1,0:T(8,128)(2,1)} %bitcast.1.img_ref), kind=kOutput, calls=%fused_computation.39 | convolution fusion | flops 2415919104 | bytes 9175040 | tf_op jit(solution)/shard_map/dot_general | solution.py:260
  68.3 1.8 %slice.94 = f32[512,1152]{1,0:T(8,128)} slice(f32[1024,1152]{1,0:T(8,128)S(1)} %fusion.12), slice={[512:1024], [0:1152]} | slice | bytes 4718592 | tf_op jit(solution)/shard_map/slice | solution.py:275
  73.8 2.5 %concatenate.20 = f32[7]{0:T(128)S(1)} concatenate(f32[3]{0:T(128)S(1)} %slice_add_fusion.8, f32[1]{0:T(128)} %get-tuple-element.30, f32[1]{0:T(128)} %slice.87, f32[1]{0:T(128)} %slice.88, f32[1]{0:T(128)} %slice.89), dimensions={0} | concatenate | bytes 56 | tf_op jit(solution)/shard_map/concatenate | solution.py:73
  76.3 3.8 %collective-permute-start.13 = (f32[7]{0:T(128)S(1)}, f32[7]{0:T(128)S(1)}, u32[]{:S(2)}, u32[]{:S(2)}) collective-permute-start(f32[7]{0:T(128)S(1)} %concatenate.20), channel_id=1, source_target_pairs={{0,6},{1,7},{2,0},{3,1},{4,2},{5,3},{6,4},{7,5},{8,14},{9,15},{10,... | collective-permute-start | bytes 92 | tf_op jit(solution)/shard_map/ppermute | solution.py:66
  81.1 2.8 %fusion.2 = f32[1024,1152]{1,0:T(8,128)S(1)} fusion(bf16[512,1152]{1,0:T(8,128)(2,1)} %copy-done.3, bf16[1024,1024]{1,0:T(8,128)(2,1)S(1)} %get-tuple-element.31), kind=kOutput, calls=%fused_computation.5 | convolution fusion | flops 1207959552 | bytes 6946816 | tf_op jit(solution)/shard_map/dot_general | solution.py:266
  83.9 2.6 %slice_add_fusion = f32[512,1152]{1,0:T(8,128)S(1)} fusion(f32[512,1152]{1,0:T(8,128)} %collective-permute-done.14, f32[1024,1152]{1,0:T(8,128)} %copy-done.6), kind=kLoop, calls=%fused_computation.4 | loop fusion | flops 589824 | bytes 7077888 | tf_op jit(solution)/shard_map/add | solution.py:275
  86.6 1.4 copy-done.5
  88.8 3.2 %collective-permute-start.15 = (f32[64,1152]{1,0:T(8,128)}, f32[64,1152]{1,0:T(8,128)}, u32[]{:S(2)}, u32[]{:S(2)}) collective-permute-start(f32[64,1152]{1,0:T(8,128)} %get-tuple-element.54), channel_id=1, source_target_pairs={{0,112},{1,113},{2,114},{3,115},{4,116},{5,117},{6,118},{7,119},{8... | collective-permute-start | bytes 884744 | tf_op jit(solution)/shard_map/ppermute | solution.py:48
  92.1 3.0 %fusion.1 = f16[1024,1152]{1,0:T(8,128)(2,1)} fusion(f32[1024,1152]{1,0:T(8,128)S(1)} %fusion.2, bf16[512,1152]{1,0:T(8,128)(2,1)S(1)} %constant_dynamic-update-slice_fusion.mine_ref, f32[]{:T(128)} %bitcast.2, bf16[1024,1024]{1,0:T(8,128)(2,1)S(1)} %get-tuple-element.31), kind=kOutput, calls=%fused_computation.3 | convolution fusion | flops 1211498496 | bytes 9306116 | tf_op jit(solution)/shard_map/dot_general | solution.py:266
  95.1 6.4 %all-to-all-start.1 = ((f16[16,64,1152]{2,1,0:T(8,128)(2,1)}), f16[16,64,1152]{2,1,0:T(8,128)(2,1)}, u32[]{:S(2)}, u32[]{:S(2)}) async-start(f16[16,64,1152]{2,1,0:T(8,128)(2,1)} %bitcast.8), calls=%async_computation.1 | async-start | bytes 4718592 | tf_op jit(solution)/shard_map/all_to_all | solution.py:271
  101.5 2.9 %collective-permute-start.17 = (f32[3]{0:T(128)S(1)}, f32[3]{0:T(128)S(1)}, u32[]{:S(2)}, u32[]{:S(2)}) collective-permute-start(f32[3]{0:T(128)S(1)} %slice_add_fusion.7), channel_id=1, source_target_pairs={{0,64},{1,65},{2,66},{3,67},{4,68},{5,69},{6,70},{7,71},{8,72},{9,... | collective-permute-start | bytes 44 | tf_op jit(solution)/shard_map/ppermute | solution.py:57
  104.3 4.7 %collective-permute-done.17 = f32[3]{0:T(128)S(1)} collective-permute-done((f32[3]{0:T(128)S(1)}, f32[3]{0:T(128)S(1)}, u32[]{:S(2)}, u32[]{:S(2)}) %collective-permute-start.17) | collective-permute-done | bytes 44 | tf_op jit(solution)/shard_map/ppermute | solution.py:57
  110.4 3.2 %collective-permute-start.18 = (f32[64,1152]{1,0:T(8,128)S(1)}, f32[64,1152]{1,0:T(8,128)S(1)}, u32[]{:S(2)}, u32[]{:S(2)}) collective-permute-start(f32[64,1152]{1,0:T(8,128)S(1)} %get-tuple-element.52), channel_id=1, source_target_pairs={{0,112},{1,113},{2,114},{3,115},{4,116},{5,117},{6,118},{7,119},{8... | collective-permute-start | bytes 884744 | tf_op jit(solution)/shard_map/ppermute | solution.py:48
  113.8 2.5 %concatenate.21 = f32[16]{0:T(128)S(1)} concatenate(f32[1]{0:T(128)} %get-tuple-element.30, f32[1]{0:T(128)} %slice.87, f32[1]{0:T(128)} %slice.88, f32[1]{0:T(128)} %slice.89, f32[4]{0:T(128)S(1)} %slice.90, f32[4]{0:T(128)S(1)} %slice.91, f32[4]{0:T(128)S(1)} %slice.92), dimensions={0} | concatenate | bytes 128 | tf_op jit(solution)/shard_map/concatenate | solution.py:73
  116.5 4.4 %collective-permute-done.20 = f32[3]{0:T(128)S(1)} collective-permute-done((f32[3]{0:T(128)S(1)}, f32[3]{0:T(128)S(1)}, u32[]{:S(2)}, u32[]{:S(2)}) %collective-permute-start.20) | collective-permute-done | bytes 44 | tf_op jit(solution)/shard_map/ppermute | solution.py:57
  122.2 3.2 %collective-permute-start.21 = (f32[64,1152]{1,0:T(8,128)S(1)}, f32[64,1152]{1,0:T(8,128)S(1)}, u32[]{:S(2)}, u32[]{:S(2)}) collective-permute-start(f32[64,1152]{1,0:T(8,128)S(1)} %get-tuple-element.50), channel_id=1, source_target_pairs={{0,112},{1,113},{2,114},{3,115},{4,116},{5,117},{6,118},{7,119},{8... | collective-permute-start | bytes 884744 | tf_op jit(solution)/shard_map/ppermute | solution.py:48
  125.7 3.5 %collective-permute-done.23 = f32[3]{0:T(128)S(1)} collective-permute-done((f32[3]{0:T(128)S(1)}, f32[3]{0:T(128)S(1)}, u32[]{:S(2)}, u32[]{:S(2)}) %collective-permute-start.23) | collective-permute-done | bytes 44 | tf_op jit(solution)/shard_map/ppermute | solution.py:57
  131.1 3.3 %collective-permute-start.24 = (f32[64,1152]{1,0:T(8,128)S(1)}, f32[64,1152]{1,0:T(8,128)S(1)}, u32[]{:S(2)}, u32[]{:S(2)}) collective-permute-start(f32[64,1152]{1,0:T(8,128)S(1)} %slice_add_fusion.1), channel_id=1, source_target_pairs={{0,112},{1,113},{2,114},{3,115},{4,116},{5,117},{6,118},{7,119},{8... | collective-permute-start | bytes 884744 | tf_op jit(solution)/shard_map/ppermute | solution.py:48
  134.4 2.2 %multiply_reduce_fusion.total_ref = f32[64,1152]{1,0:T(8,128)S(1)} fusion(f16[16,64,1152]{2,1,0:T(8,128)(2,1)} %all-to-all-done.1, f32[16]{0:T(128)S(1)} %broadcast_multiply_fusion), kind=kLoop, calls=%fused_computation.2 | loop fusion | flops 3465216 | bytes 2654272 | tf_op jit(solution)/shard_map/reduce_sum | solution.py:301
  (81 shorter events, 20.0 us)
Async XLA Ops:
  1.5 1.7 %copy-start.2 = (bf16[64,1152]{1,0:T(8,128)(2,1)S(1)}, bf16[64,1152]{1,0:T(8,128)(2,1)}, u32[]{:S(2)}) copy-start(bf16[64,1152]{1,0:T(8,128)(2,1)} %rows_ref.6) | copy-start | bytes 442372
  3.4 13.4 %collective-permute-start.4 = (bf16[64,1152]{1,0:T(8,128)(2,1)S(1)}, bf16[64,1152]{1,0:T(8,128)(2,1)S(1)}, u32[]{:S(2)}, u32[]{:S(2)}) collective-permute-start(bf16[64,1152]{1,0:T(8,128)(2,1)S(1)} %shard_map.68), channel_id=1, source_target_pairs={{0,112},{1,113},{2,114},{3,115},{4,116},{5,117},{6,118},{7,119},{8... | collective-permute-start | bytes 442376 | tf_op jit(solution)/shard_map/ppermute | solution.py:48
  9.3 10.8 %collective-permute-start = (bf16[64,1152]{1,0:T(8,128)(2,1)S(1)}, bf16[64,1152]{1,0:T(8,128)(2,1)S(1)}, u32[]{:S(2)}, u32[]{:S(2)}) collective-permute-start(bf16[64,1152]{1,0:T(8,128)(2,1)S(1)} %shard_map.68), channel_id=1, source_target_pairs={{0,16},{1,17},{2,18},{3,19},{4,20},{5,21},{6,22},{7,23},{8,24},{9,... | collective-permute-start | bytes 442376 | tf_op jit(solution)/shard_map/ppermute | solution.py:48
  9.3 39.9 %all-to-all-start = ((bf16[16,64,1152]{2,1,0:T(8,128)(2,1)}), bf16[16,64,1152]{2,1,0:T(8,128)(2,1)}, u32[]{:S(2)}, u32[]{:S(2)}) async-start(bf16[16,64,1152]{2,1,0:T(8,128)(2,1)} %shard_map.67), calls=%async_computation | async-start | bytes 4718592 | tf_op jit(solution)/shard_map/all_to_all | solution.py:245
  16.8 6.0 %collective-permute-start.5 = (bf16[64,1152]{1,0:T(8,128)(2,1)S(1)}, bf16[64,1152]{1,0:T(8,128)(2,1)S(1)}, u32[]{:S(2)}, u32[]{:S(2)}) collective-permute-start(bf16[64,1152]{1,0:T(8,128)(2,1)S(1)} %collective-permute-done.4), channel_id=1, source_target_pairs={{0,112},{1,113},{2,114},{3,115},{4,116},{5,117},{6,118},{7,119},{8... | collective-permute-start | bytes 442376 | tf_op jit(solution)/shard_map/ppermute | solution.py:48
  20.1 6.4 %collective-permute-start.1 = (bf16[64,1152]{1,0:T(8,128)(2,1)S(1)}, bf16[64,1152]{1,0:T(8,128)(2,1)S(1)}, u32[]{:S(2)}, u32[]{:S(2)}) collective-permute-start(bf16[64,1152]{1,0:T(8,128)(2,1)S(1)} %collective-permute-done), channel_id=1, source_target_pairs={{0,16},{1,17},{2,18},{3,19},{4,20},{5,21},{6,22},{7,23},{8,24},{9,... | collective-permute-start | bytes 442376 | tf_op jit(solution)/shard_map/ppermute | solution.py:48
  22.8 16.4 %collective-permute-start.6 = (bf16[64,1152]{1,0:T(8,128)(2,1)S(1)}, bf16[64,1152]{1,0:T(8,128)(2,1)S(1)}, u32[]{:S(2)}, u32[]{:S(2)}) collective-permute-start(bf16[64,1152]{1,0:T(8,128)(2,1)S(1)} %collective-permute-done.5), channel_id=1, source_target_pairs={{0,112},{1,113},{2,114},{3,115},{4,116},{5,117},{6,118},{7,119},{8... | collective-permute-start | bytes 442376 | tf_op jit(solution)/shard_map/ppermute | solution.py:48
  26.5 6.4 %collective-permute-start.2 = (bf16[64,1152]{1,0:T(8,128)(2,1)S(1)}, bf16[64,1152]{1,0:T(8,128)(2,1)S(1)}, u32[]{:S(2)}, u32[]{:S(2)}) collective-permute-start(bf16[64,1152]{1,0:T(8,128)(2,1)S(1)} %collective-permute-done.1), channel_id=1, source_target_pairs={{0,16},{1,17},{2,18},{3,19},{4,20},{5,21},{6,22},{7,23},{8,24},{9,... | collective-permute-start | bytes 442376 | tf_op jit(solution)/shard_map/ppermute | solution.py:48
  32.9 6.4 %collective-permute-start.3 = (bf16[64,1152]{1,0:T(8,128)(2,1)S(1)}, bf16[64,1152]{1,0:T(8,128)(2,1)S(1)}, u32[]{:S(2)}, u32[]{:S(2)}) collective-permute-start(bf16[64,1152]{1,0:T(8,128)(2,1)S(1)} %collective-permute-done.2), channel_id=1, source_target_pairs={{0,16},{1,17},{2,18},{3,19},{4,20},{5,21},{6,22},{7,23},{8,24},{9,... | collective-permute-start | bytes 442376 | tf_op jit(solution)/shard_map/ppermute | solution.py:48
  39.3 2.9 %collective-permute-start.7 = (bf16[512,1152]{1,0:T(8,128)(2,1)S(1)}, bf16[512,1152]{1,0:T(8,128)(2,1)S(1)}, u32[]{:S(2)}, u32[]{:S(2)}) collective-permute-start(bf16[512,1152]{1,0:T(8,128)(2,1)S(1)} %constant_dynamic-update-slice_fusion.mine_ref), channel_id=1, source_target_pairs={{0,8},{1,9},{2,10},{3,11},{4,12},{5,13},{6,14},{7,15},{8,0},{9,1},... | collective-permute-start | bytes 3538952 | tf_op jit(solution)/shard_map/ppermute | solution.py:48
  58.8 9.5 %collective-permute-start.10 = (f32[4]{0:T(128)S(1)}, f32[4]{0:T(128)S(1)}, u32[]{:S(2)}, u32[]{:S(2)}) collective-permute-start(f32[4]{0:T(128)S(1)} %pad_maximum_fusion), channel_id=1, source_target_pairs={{0,129},{1,0},{2,131},{3,2},{4,133},{5,4},{6,135},{7,6},{8,137},{9... | collective-permute-start | bytes 56 | tf_op jit(solution)/shard_map/ppermute | solution.py:66
  60.3 8.0 %collective-permute-start.9 = (f32[4]{0:T(128)S(1)}, f32[4]{0:T(128)S(1)}, u32[]{:S(2)}, u32[]{:S(2)}) collective-permute-start(f32[4]{0:T(128)S(1)} %pad_maximum_fusion), channel_id=1, source_target_pairs={{0,128},{1,129},{2,130},{3,131},{4,132},{5,133},{6,134},{7,135},{8... | collective-permute-start | bytes 56 | tf_op jit(solution)/shard_map/ppermute | solution.py:66
  61.6 6.7 %collective-permute-start.8 = (f32[4]{0:T(128)S(1)}, f32[4]{0:T(128)S(1)}, u32[]{:S(2)}, u32[]{:S(2)}) collective-permute-start(f32[4]{0:T(128)S(1)} %pad_maximum_fusion), channel_id=1, source_target_pairs={{0,1},{1,128},{2,3},{3,130},{4,5},{5,132},{6,7},{7,134},{8,9},{9,1... | collective-permute-start | bytes 56 | tf_op jit(solution)/shard_map/ppermute | solution.py:66
  68.3 3.0 %copy-start.6 = (f32[1024,1152]{1,0:T(8,128)}, f32[1024,1152]{1,0:T(8,128)S(1)}, u32[]{:S(2)}) copy-start(f32[1024,1152]{1,0:T(8,128)S(1)} %fusion.12) | copy-start | bytes 14155780
  71.3 12.6 %collective-permute-start.14 = (f32[512,1152]{1,0:T(8,128)}, f32[512,1152]{1,0:T(8,128)}, u32[]{:S(2)}, u32[]{:S(2)}) collective-permute-start(f32[512,1152]{1,0:T(8,128)} %slice.94), channel_id=1, source_target_pairs={{0,8},{1,9},{2,10},{3,11},{4,12},{5,13},{6,14},{7,15},{8,0},{9,1},... | collective-permute-start | bytes 7077896 | tf_op jit(solution)/shard_map/ppermute | solution.py:48
  76.3 18.7 %collective-permute-start.13 = (f32[7]{0:T(128)S(1)}, f32[7]{0:T(128)S(1)}, u32[]{:S(2)}, u32[]{:S(2)}) collective-permute-start(f32[7]{0:T(128)S(1)} %concatenate.20), channel_id=1, source_target_pairs={{0,6},{1,7},{2,0},{3,1},{4,2},{5,3},{6,4},{7,5},{8,14},{9,15},{10,... | collective-permute-start | bytes 92 | tf_op jit(solution)/shard_map/ppermute | solution.py:66
  80.2 14.9 %collective-permute-start.12 = (f32[7]{0:T(128)S(1)}, f32[7]{0:T(128)S(1)}, u32[]{:S(2)}, u32[]{:S(2)}) collective-permute-start(f32[7]{0:T(128)S(1)} %concatenate.20), channel_id=1, source_target_pairs={{0,4},{1,5},{2,6},{3,7},{4,0},{5,1},{6,2},{7,3},{8,12},{9,13},{10,... | collective-permute-start | bytes 92 | tf_op jit(solution)/shard_map/ppermute | solution.py:66
  80.2 14.9 %collective-permute-start.11 = (f32[7]{0:T(128)S(1)}, f32[7]{0:T(128)S(1)}, u32[]{:S(2)}, u32[]{:S(2)}) collective-permute-start(f32[7]{0:T(128)S(1)} %concatenate.20), channel_id=1, source_target_pairs={{0,2},{1,3},{2,4},{3,5},{4,6},{5,7},{6,0},{7,1},{8,10},{9,11},{10,... | collective-permute-start | bytes 92 | tf_op jit(solution)/shard_map/ppermute | solution.py:66
  86.5 1.4 %copy-start.5 = (f32[512,1152]{1,0:T(8,128)}, f32[512,1152]{1,0:T(8,128)S(1)}, u32[]{:S(2)}) copy-start(f32[512,1152]{1,0:T(8,128)S(1)} %slice_add_fusion) | copy-start | bytes 7077892
  88.8 20.2 %collective-permute-start.16 = (f32[64,1152]{1,0:T(8,128)}, f32[64,1152]{1,0:T(8,128)}, u32[]{:S(2)}, u32[]{:S(2)}) collective-permute-start(f32[64,1152]{1,0:T(8,128)} %get-tuple-element.53), channel_id=1, source_target_pairs={{0,16},{1,17},{2,18},{3,19},{4,20},{5,21},{6,22},{7,23},{8,24},{9,... | collective-permute-start | bytes 884744 | tf_op jit(solution)/shard_map/ppermute | solution.py:48
  88.8 20.2 %collective-permute-start.15 = (f32[64,1152]{1,0:T(8,128)}, f32[64,1152]{1,0:T(8,128)}, u32[]{:S(2)}, u32[]{:S(2)}) collective-permute-start(f32[64,1152]{1,0:T(8,128)} %get-tuple-element.54), channel_id=1, source_target_pairs={{0,112},{1,113},{2,114},{3,115},{4,116},{5,117},{6,118},{7,119},{8... | collective-permute-start | bytes 884744 | tf_op jit(solution)/shard_map/ppermute | solution.py:48
  95.1 39.3 %all-to-all-start.1 = ((f16[16,64,1152]{2,1,0:T(8,128)(2,1)}), f16[16,64,1152]{2,1,0:T(8,128)(2,1)}, u32[]{:S(2)}, u32[]{:S(2)}) async-start(f16[16,64,1152]{2,1,0:T(8,128)(2,1)} %bitcast.8), calls=%async_computation.1 | async-start | bytes 4718592 | tf_op jit(solution)/shard_map/all_to_all | solution.py:271
  101.5 7.5 %collective-permute-start.17 = (f32[3]{0:T(128)S(1)}, f32[3]{0:T(128)S(1)}, u32[]{:S(2)}, u32[]{:S(2)}) collective-permute-start(f32[3]{0:T(128)S(1)} %slice_add_fusion.7), channel_id=1, source_target_pairs={{0,64},{1,65},{2,66},{3,67},{4,68},{5,69},{6,70},{7,71},{8,72},{9,... | collective-permute-start | bytes 44 | tf_op jit(solution)/shard_map/ppermute | solution.py:57
  110.3 10.6 %collective-permute-start.19 = (f32[64,1152]{1,0:T(8,128)S(1)}, f32[64,1152]{1,0:T(8,128)S(1)}, u32[]{:S(2)}, u32[]{:S(2)}) collective-permute-start(f32[64,1152]{1,0:T(8,128)S(1)} %get-tuple-element.51), channel_id=1, source_target_pairs={{0,16},{1,17},{2,18},{3,19},{4,20},{5,21},{6,22},{7,23},{8,24},{9,... | collective-permute-start | bytes 884744 | tf_op jit(solution)/shard_map/ppermute | solution.py:48
  110.4 10.5 %collective-permute-start.18 = (f32[64,1152]{1,0:T(8,128)S(1)}, f32[64,1152]{1,0:T(8,128)S(1)}, u32[]{:S(2)}, u32[]{:S(2)}) collective-permute-start(f32[64,1152]{1,0:T(8,128)S(1)} %get-tuple-element.52), channel_id=1, source_target_pairs={{0,112},{1,113},{2,114},{3,115},{4,116},{5,117},{6,118},{7,119},{8... | collective-permute-start | bytes 884744 | tf_op jit(solution)/shard_map/ppermute | solution.py:48
  116.4 4.5 %collective-permute-start.20 = (f32[3]{0:T(128)S(1)}, f32[3]{0:T(128)S(1)}, u32[]{:S(2)}, u32[]{:S(2)}) collective-permute-start(f32[3]{0:T(128)S(1)} %add.95), channel_id=1, source_target_pairs={{0,32},{1,33},{2,34},{3,35},{4,36},{5,37},{6,38},{7,39},{8,40},{9,... | collective-permute-start | bytes 44 | tf_op jit(solution)/shard_map/ppermute | solution.py:57
  122.1 14.6 %copy-start.1 = (bf16[64,1152]{1,0:T(8,128)(2,1)S(1)}, bf16[64,1152]{1,0:T(8,128)(2,1)}, u32[]{:S(2)}) copy-start(bf16[64,1152]{1,0:T(8,128)(2,1)} %rows_ref.5) | copy-start | bytes 442372
  122.1 8.0 %collective-permute-start.22 = (f32[64,1152]{1,0:T(8,128)S(1)}, f32[64,1152]{1,0:T(8,128)S(1)}, u32[]{:S(2)}, u32[]{:S(2)}) collective-permute-start(f32[64,1152]{1,0:T(8,128)S(1)} %get-tuple-element.49), channel_id=1, source_target_pairs={{0,16},{1,17},{2,18},{3,19},{4,20},{5,21},{6,22},{7,23},{8,24},{9,... | collective-permute-start | bytes 884744 | tf_op jit(solution)/shard_map/ppermute | solution.py:48
  122.2 7.9 %collective-permute-start.21 = (f32[64,1152]{1,0:T(8,128)S(1)}, f32[64,1152]{1,0:T(8,128)S(1)}, u32[]{:S(2)}, u32[]{:S(2)}) collective-permute-start(f32[64,1152]{1,0:T(8,128)S(1)} %get-tuple-element.50), channel_id=1, source_target_pairs={{0,112},{1,113},{2,114},{3,115},{4,116},{5,117},{6,118},{7,119},{8... | collective-permute-start | bytes 884744 | tf_op jit(solution)/shard_map/ppermute | solution.py:48
  125.6 3.6 %collective-permute-start.23 = (f32[3]{0:T(128)S(1)}, f32[3]{0:T(128)S(1)}, u32[]{:S(2)}, u32[]{:S(2)}) collective-permute-start(f32[3]{0:T(128)S(1)} %add.98), channel_id=1, source_target_pairs={{0,16},{1,17},{2,18},{3,19},{4,20},{5,21},{6,22},{7,23},{8,24},{9,... | collective-permute-start | bytes 44 | tf_op jit(solution)/shard_map/ppermute | solution.py:57
  131.1 8.1 %collective-permute-start.24 = (f32[64,1152]{1,0:T(8,128)S(1)}, f32[64,1152]{1,0:T(8,128)S(1)}, u32[]{:S(2)}, u32[]{:S(2)}) collective-permute-start(f32[64,1152]{1,0:T(8,128)S(1)} %slice_add_fusion.1), channel_id=1, source_target_pairs={{0,112},{1,113},{2,114},{3,115},{4,116},{5,117},{6,118},{7,119},{8... | collective-permute-start | bytes 884744 | tf_op jit(solution)/shard_map/ppermute | solution.py:48
  137.6 1.1 collective-permute-start.25
  (3 other events, 3.2 us)

commit v4 on v3

--- a/solution.py
+++ b/solution.py
@@ -12,6 +12,7 @@
 PLANE = ("x_hi", "y", "x_lo")
 PEERS = 16
 DEPTH = 8
+CODE = 1024.0
 BF16 = jnp.bfloat16
 F32 = jnp.float32
 F16 = jnp.float16
@@ -66,11 +67,13 @@
     return lax.ppermute(array, AXES, pairs)
 
 
-def joined(message, arrived):
-    sums = message[:3]
-    for other in arrived:
-        sums = sums + other[:3]
-    return jnp.concatenate([sums, message[3:]] + [other[3:] for other in arrived])
+def coded(array):
+    return (array * lax.rsqrt(jnp.maximum(jnp.abs(array), 1e-36)) * CODE).astype(F16)
+
+
+def decoded(array):
+    wide = array.astype(F32) * (1.0 / CODE)
+    return wide * jnp.abs(wide)
 
 
 def along_z(array, by):
@@ -117,7 +120,7 @@
     return out
 
 
-def pair_kernel(first_ref, scale_ref, shift_ref, img_ref, mine_ref, theirs_ref, grad_ref, sums_ref, size_ref, acc_ref):
+def pair_kernel(first_ref, scale_ref, shift_ref, img_ref, mine_ref, theirs_ref, grad_ref, sums_ref, acc_ref):
     tile = pl.program_id(0)
     rows = img_ref.shape[0]
     half = mine_ref.shape[0]
@@ -128,7 +131,6 @@
     loss_sum = jnp.zeros((8, 128), F32)
     scaled_sum = jnp.zeros((8, 128), F32)
     grad_sum = jnp.zeros((8, 128), F32)
-    size_sum = jnp.zeros((8, 128), F32)
     for side, txt_ref in enumerate((mine_ref, theirs_ref)):
         for at in range(0, half, wide):
             cosine = lax.dot_general(
@@ -148,9 +150,7 @@
                 grad = jnp.where(positive, grad - 1.0, grad)
             loss_sum += lanes(fold_sum(jnp.maximum(signed, 0.0)) + jnp.log1p(fold_growth(small)))
             scaled_sum += lanes(fold_sum(grad * scaled))
-            part = lanes(fold_sum(grad))
-            grad_sum += part
-            size_sum += lanes(fold_sum(jnp.abs(grad))) if side == 0 and at == 0 else part
+            grad_sum += lanes(fold_sum(grad))
             grad_ref[:, side * half + at : side * half + at + wide] = grad.astype(BF16)
 
     @pl.when(tile == 0)
@@ -160,13 +160,11 @@
     acc_ref[0] += loss_sum
     acc_ref[1] += scaled_sum
     acc_ref[2] += grad_sum
-    acc_ref[3] += size_sum
 
     @pl.when(tile == pl.num_programs(0) - 1)
     def _():
         for k in range(3):
             sums_ref[k] = jnp.sum(acc_ref[k])
-        size_ref[0] = jnp.sum(acc_ref[3])
 
 
 def pairs(first, scale, shift, imgs, mine, theirs):
@@ -187,14 +185,12 @@
         out_specs=[
             pl.BlockSpec((rows, 2 * half), lambda i: (i, 0)),
             SMEM,
-            SMEM,
         ],
         out_shape=[
             jax.ShapeDtypeStruct((count, 2 * half), BF16),
             jax.ShapeDtypeStruct((3,), F32),
-            jax.ShapeDtypeStruct((1,), F32),
         ],
-        scratch_shapes=[pltpu.VMEM((4, 8, 128), F32)],
+        scratch_shapes=[pltpu.VMEM((3, 8, 128), F32)],
         compiler_params=PARAMS,
         cost_estimate=cost(2 * count * 2 * half * emb, 8 * 2**20),
     )(first, scale, shift, imgs, mine, theirs)
@@ -252,53 +248,52 @@
     mine = jnp.concatenate(up + down[::-1], axis=0)
     theirs = other_core(mine)
 
-    grad_low, sums, size = pairs(first, scale, bias, imgs, mine, theirs)
+    grad_low, sums = pairs(first, scale, bias, imgs, mine, theirs)
     half = DEPTH * rows
 
-    message = jnp.concatenate([sums, size])
-    arrived = [moved(message, by, 0) for by in (1, 2, 3)]
-    txt_part = lax.dot_general(grad_low, imgs, (((0,), (0,)), ((), ())), preferred_element_type=F32)
-    txt_part, grad_low, *arrived = lax.optimization_barrier((txt_part, grad_low, *arrived))
-    message = joined(message, arrived)
-
-    arrived = [moved(message, 0, by) for by in (1, 2, 3)]
-    factor = 16384.0 / jnp.maximum(size[0], 1e-30)
+    txt_part = lax.dot_general(grad_low[:, half:], imgs, (((0,), (0,)), ((), ())), preferred_element_type=F32)
+    theirs_part = other_core(coded(txt_part))
+    mine_part = lax.dot_general(grad_low[:, :half], imgs, (((0,), (0,)), ((), ())), preferred_element_type=F32)
+
+    arrived = [moved(sums, by, 0) for by in (1, 2, 3)]
     img_part = jnp.dot(grad_low[:, :half], mine, preferred_element_type=F32) + jnp.dot(
         grad_low[:, half:], theirs, preferred_element_type=F32
     )
-    img_part = (img_part * factor).astype(F16).reshape(PEERS, rows, emb)
+    img_part = coded(img_part).reshape(PEERS, rows, emb)
     img_part, *arrived = lax.optimization_barrier((img_part, *arrived))
     img_recv = lax.all_to_all(img_part, PLANE, 0, 0)
-    message = joined(message, arrived)
-    sums, sizes = message[:3], message[3:]
-
-    blocks = (txt_part[:half] + other_core(txt_part[half:])).reshape(DEPTH, rows, emb)
-    left, right = along_z(blocks[4], -1), along_z(blocks[5], 1)
+    sums = sums + arrived[0] + arrived[1] + arrived[2]
+
+    mine_part = mine_part.reshape(DEPTH, rows, emb)
+    theirs_part = theirs_part.reshape(DEPTH, rows, emb)
+    block = lambda k: mine_part[k] + decoded(theirs_part[k])
+    left, right = along_z(coded(block(4)), -1), along_z(coded(block(5)), 1)
     arrived = flipped(sums, 1, 4)
     left, right, arrived = lax.optimization_barrier((left, right, arrived))
-    left, right, sums = left + blocks[3], right + blocks[6], sums + arrived
-
-    left, right = along_z(left, -1), along_z(right, 1)
+    left, right, sums = decoded(left) + block(3), decoded(right) + block(6), sums + arrived
+
+    left, right = along_z(coded(left), -1), along_z(coded(right), 1)
     arrived = flipped(sums, 1, 2)
     left, right, arrived = lax.optimization_barrier((left, right, arrived))
-    left, right, sums = left + blocks[2], right + blocks[7], sums + arrived
-
-    left, right = along_z(left, -1), along_z(right, 1)
+    left, right, sums = decoded(left) + block(2), decoded(right) + block(7), sums + arrived
+
+    left, right = along_z(coded(left), -1), along_z(coded(right), 1)
     arrived = flipped(sums, 1, 1)
     left, right, arrived = lax.optimization_barrier((left, right, arrived))
-    left, sums = left + blocks[1], sums + arrived
-
-    left = along_z(left, -1)
-    txt_total = blocks[0] + left + right
-    stats = (sums + flipped(sums, 2, 1)) / (rows * 256)
-
-    x, y = lax.axis_index("x_hi") * 2 + lax.axis_index("x_lo"), lax.axis_index("y")
-    peer = jnp.arange(PEERS)
-    peer_x, peer_y = (peer >> 3) * 2 + (peer & 1), (peer >> 1) & 3
-    entry = ((y - peer_y) & 3) * 4 + ((x - peer_x) & 3)
-    chosen = entry[:, None] == peer[None, :]
-    weights = jnp.sum(jnp.where(chosen, jnp.maximum(sizes, 1e-30)[None, :], 0.0), axis=1) / 16384.0
-    img_total = jnp.sum(img_recv.astype(F32) * weights[:, None, None], axis=0)
+    left, sums = decoded(left) + block(1), sums + arrived
+
+    left = along_z(coded(left), -1)
+    arrived = flipped(sums, 2, 1)
+    left, arrived = lax.optimization_barrier((left, arrived))
+    txt_total = block(0) + decoded(left) + decoded(right)
+    sums = sums + arrived
+
+    img_recv, sums = lax.optimization_barrier((img_recv, sums))
+    for by in (1, 2, 3):
+        arrived = moved(sums, 0, by)
+        stats = arrived + (sums if by == 1 else stats)
+    stats = stats / (rows * 256)
+    img_total = jnp.sum(decoded(img_recv), axis=0)
 
     image_grad = projected(scale, images, img_total)
     text_grad = projected(scale, texts, txt_total)

time: 143 us -> 131 us (0.916)
  local copies, waits for them, and re-layouts: 15.8 us -> 1.06 us
  waiting for transfers between devices: 37.4 us -> 45.6 us
  starting transfers between devices: 52.7 us -> 48.7 us
  matrix products: 10.5 us -> 13.9 us
  other arithmetic: 10.6 us -> 7.78 us
    add x11 -> x6, other arithmetic: 7.06 us -> 1.12 us  [the longest x1 1.1 us: on_device(): txt_total = block(0) + decoded(left) + decoded(right)]
    ppermute x16, starting transfers between devices: 26.2 us -> 20.4 us  [shifted(): return lax.ppermute(array, AXES, pairs)]
    convert_element_type x0 -> x4, other arithmetic: none -> 5.37 us  [coded(): (array * lax.rsqrt(jnp.maximum(jnp.abs(array), 1e-36)) * CODE).astype(F16)]
    concatenate x2 -> x0, local copies, waits for them, and re-layouts: 5.09 us -> none  [joined(): jnp.concatenate([sums, message[3:]] + [other[3:] for other in arrived])]
    unnamed x21 -> x15, local copies, waits for them, and re-layouts: 5.98 us -> 1.04 us
    slice x8 -> x0, local copies, waits for them, and re-layouts: 4.68 us -> none  [the longest x6 2.07 us: joined(): other[3:]]
    dot_general x1 -> x2, matrix products: 4.69 us -> 9.1 us  [the longest x1 4.66 us: on_device(): lax.dot_general(grad_low[:, :half], imgs, (((0,), (0,)), ((), ())), prefe...]
    all_to_all x1, waiting for transfers between devices: 5.96 us -> 10.2 us  [on_device(): imgs = lax.all_to_all(copies, PLANE, 0, 0).reshape(PEERS * rows, emb)]
  transfers between devices with their start and end apart: 28 -> 28, of which waited for: 10 -> 14; matrix products, arithmetic and copies ran while one was open for 20% -> 16% of each run, Pallas kernels for 1% -> 1%
where the time goes in v4:
time: 131 us
  starting transfers between devices  48.7 us (37%)
  waiting for transfers between devices  45.6 us (35%)
  matrix products  13.9 us (11%)
  Pallas kernels  11.3 us (9%)
  other arithmetic  7.78 us (6%)
  between operations  2.12 us (2%)
    ppermute x16, waiting for transfers between devices, shifted(): return lax.ppermute(array, AXES, pairs)  21.6 us
    ppermute x16, starting transfers between devices, shifted(): return lax.ppermute(array, AXES, pairs)  20.4 us
    ppermute x4, waiting for transfers between devices, flipped(): return lax.ppermute(array, AXES, pairs)  11.6 us
    all_to_all x1, waiting for transfers between devices, on_device(): imgs = lax.all_to_all(copies, PLANE, 0, 0).reshape(PEERS * rows, emb)  10.2 us
    ppermute x6, starting transfers between devices, moved(): return lax.ppermute(array, AXES, pairs)  9.22 us
    pallas_call x1, Pallas kernels, pairs(): pl.pallas_call(pair_kernel, grid=(count // rows,), in_specs=[SMEM, SMEM,...  7.6 us
    all_to_all x1, starting transfers between devices, on_device(): imgs = lax.all_to_all(copies, PLANE, 0, 0).reshape(PEERS * rows, emb)  7.48 us
    all_to_all x1, starting transfers between devices, on_device(): img_recv = lax.all_to_all(img_part, PLANE, 0, 0)  6.57 us
  transfers between devices with their start and end apart: 28, of which 14 were waited for; matrix products, arithmetic and copies ran while one was open for 16% of the time, Pallas kernels for 1%

profile of v4, /device:TPU:2, one launch (start us, length us, event | category | flops | bytes accessed | tf_op | source)
XLA Modules:
  0.0 130.6 jit_solution(7598701944989767041)
XLA Ops:
  1.5 1.7 %shard_map.67 = bf16[16,64,1152]{2,1,0:T(8,128)(2,1)} custom-call(bf16[64,1152]{1,0:T(8,128)(2,1)S(1)} %copy-done), custom_call_target="tpu_custom_call" | custom-call | flops 1000000 | bytes 3145728 | tf_op jit(solution)/shard_map/pallas_call | solution.py:223
  3.4 2.0 %collective-permute-start = (bf16[64,1152]{1,0:T(8,128)(2,1)S(1)}, bf16[64,1152]{1,0:T(8,128)(2,1)S(1)}, u32[]{:S(2)}, u32[]{:S(2)}) collective-permute-start(bf16[64,1152]{1,0:T(8,128)(2,1)S(1)} %shard_map.68), channel_id=1, source_target_pairs={{0,16},{1,17},{2,18},{3,19},{4,20},{5,21},{6,22},{7,23},{8,24},{9,... | collective-permute-start | bytes 442376 | tf_op jit(solution)/shard_map/ppermute | solution.py:49
  5.4 4.0 %collective-permute-start.4 = (bf16[64,1152]{1,0:T(8,128)(2,1)S(1)}, bf16[64,1152]{1,0:T(8,128)(2,1)S(1)}, u32[]{:S(2)}, u32[]{:S(2)}) collective-permute-start(bf16[64,1152]{1,0:T(8,128)(2,1)S(1)} %shard_map.68), channel_id=1, source_target_pairs={{0,112},{1,113},{2,114},{3,115},{4,116},{5,117},{6,118},{7,119},{8... | collective-permute-start | bytes 442376 | tf_op jit(solution)/shard_map/ppermute | solution.py:49
  9.4 7.5 %all-to-all-start = ((bf16[16,64,1152]{2,1,0:T(8,128)(2,1)}), bf16[16,64,1152]{2,1,0:T(8,128)(2,1)}, u32[]{:S(2)}, u32[]{:S(2)}) async-start(bf16[16,64,1152]{2,1,0:T(8,128)(2,1)} %shard_map.67), calls=%async_computation | async-start | bytes 4718592 | tf_op jit(solution)/shard_map/all_to_all | solution.py:241
  17.0 3.2 %collective-permute-start.5 = (bf16[64,1152]{1,0:T(8,128)(2,1)S(1)}, bf16[64,1152]{1,0:T(8,128)(2,1)S(1)}, u32[]{:S(2)}, u32[]{:S(2)}) collective-permute-start(bf16[64,1152]{1,0:T(8,128)(2,1)S(1)} %collective-permute-done.4), channel_id=1, source_target_pairs={{0,112},{1,113},{2,114},{3,115},{4,116},{5,117},{6,118},{7,119},{8... | collective-permute-start | bytes 442376 | tf_op jit(solution)/shard_map/ppermute | solution.py:49
  20.3 3.1 %collective-permute-done.1 = bf16[64,1152]{1,0:T(8,128)(2,1)S(1)} collective-permute-done((bf16[64,1152]{1,0:T(8,128)(2,1)S(1)}, bf16[64,1152]{1,0:T(8,128)(2,1)S(1)}, u32[]{:S(2)}, u32[]{:S(2)}) %collective-permute-start.1) | collective-permute-done | bytes 147488 | tf_op jit(solution)/shard_map/ppermute | solution.py:49
  23.4 3.2 %collective-permute-start.6 = (bf16[64,1152]{1,0:T(8,128)(2,1)S(1)}, bf16[64,1152]{1,0:T(8,128)(2,1)S(1)}, u32[]{:S(2)}, u32[]{:S(2)}) collective-permute-start(bf16[64,1152]{1,0:T(8,128)(2,1)S(1)} %collective-permute-done.5), channel_id=1, source_target_pairs={{0,112},{1,113},{2,114},{3,115},{4,116},{5,117},{6,118},{7,119},{8... | collective-permute-start | bytes 442376 | tf_op jit(solution)/shard_map/ppermute | solution.py:49
  26.6 3.1 %collective-permute-done.2 = bf16[64,1152]{1,0:T(8,128)(2,1)S(1)} collective-permute-done((bf16[64,1152]{1,0:T(8,128)(2,1)S(1)}, bf16[64,1152]{1,0:T(8,128)(2,1)S(1)}, u32[]{:S(2)}, u32[]{:S(2)}) %collective-permute-start.2) | collective-permute-done | bytes 147488 | tf_op jit(solution)/shard_map/ppermute | solution.py:49
  29.7 6.3 %collective-permute-done.3 = bf16[64,1152]{1,0:T(8,128)(2,1)S(1)} collective-permute-done((bf16[64,1152]{1,0:T(8,128)(2,1)S(1)}, bf16[64,1152]{1,0:T(8,128)(2,1)S(1)}, u32[]{:S(2)}, u32[]{:S(2)}) %collective-permute-start.3) | collective-permute-done | bytes 147488 | tf_op jit(solution)/shard_map/ppermute | solution.py:49
  37.6 1.5 %collective-permute-done.7.theirs_ref = bf16[512,1152]{1,0:T(8,128)(2,1)S(1)} collective-permute-done((bf16[512,1152]{1,0:T(8,128)(2,1)S(1)}, bf16[512,1152]{1,0:T(8,128)(2,1)S(1)}, u32[]{:S(2)}, u32[]{:S(2)}) %collective-permute-start.7) | collective-permute-done | bytes 1179680 | tf_op jit(solution)/shard_map/ppermute | solution.py:49
  39.1 10.2 %all-to-all-done = bf16[16,64,1152]{2,1,0:T(8,128)(2,1)} async-done(((bf16[16,64,1152]{2,1,0:T(8,128)(2,1)}), bf16[16,64,1152]{2,1,0:T(8,128)(2,1)}, u32[]{:S(2)}, u32[]{:S(2)}) %all-to-all-start) | async-done | bytes 2359328 | tf_op jit(solution)/shard_map/all_to_all | solution.py:241
  49.3 7.6 %shard_map.69 = (bf16[1024,1024]{1,0:T(8,128)(2,1)S(1)}, f32[3]{0:T(128)S(1)}) custom-call(s32[1]{0:T(128)} %bitcast.first_ref, f32[1]{0:T(128)S(6)} %exp.3.scale_ref, f32[1]{0:T(128)S(6)} %copy.15.shift_ref, bf16[1024,1152]{1,0:T(8,128)(2,1)} %bitcast.1.img_ref, bf16[512,1152]{1,0:T(8,128)(2,1)S(1)} %constant_dynamic-update-slice_fusion.mine_ref, ...), custom_call_target="tpu_custom_call" | custom-call | flops 2415919104 | bytes 8388608 | tf_op jit(solution)/shard_map/pallas_call | solution.py:174
  58.3 2.3 %collective-permute-start.9 = (f32[3]{0:T(128)S(1)}, f32[3]{0:T(128)S(1)}, u32[]{:S(2)}, u32[]{:S(2)}) collective-permute-start(f32[3]{0:T(128)S(1)} %get-tuple-element.27), channel_id=1, source_target_pairs={{0,128},{1,129},{2,130},{3,131},{4,132},{5,133},{6,134},{7,135},{8... | collective-permute-start | bytes 44 | tf_op jit(solution)/shard_map/ppermute | solution.py:67
  61.8 4.4 %multiply_convert_fusion.1 = f16[512,1152]{1,0:T(8,128)(2,1)} fusion(bf16[1024,1152]{1,0:T(8,128)(2,1)} %bitcast.1.img_ref, bf16[1024,1024]{1,0:T(8,128)(2,1)S(1)} %get-tuple-element.26), kind=kOutput, calls=%fused_computation.4 | convolution fusion | flops 1210908672 | bytes 4587520 | tf_op jit(solution)/shard_map/dot_general | solution.py:254
  66.2 4.7 %fusion.7 = f32[512,1152]{1,0:T(8,128)} fusion(bf16[1024,1152]{1,0:T(8,128)(2,1)} %bitcast.1.img_ref, bf16[1024,1024]{1,0:T(8,128)(2,1)S(1)} %get-tuple-element.26), kind=kOutput, calls=%fused_computation.9 | convolution fusion | flops 1207959552 | bytes 5767168 | tf_op jit(solution)/shard_map/dot_general | solution.py:256
  70.9 1.5 %fusion.3 = f32[1024,1152]{1,0:T(8,128)S(1)} fusion(bf16[512,1152]{1,0:T(8,128)(2,1)S(1)} %collective-permute-done.7.theirs_ref, bf16[1024,1024]{1,0:T(8,128)(2,1)S(1)} %get-tuple-element.26), kind=kOutput, calls=%fused_computation.7 | convolution fusion | flops 1207959552 | bytes 6946816 | tf_op jit(solution)/shard_map/dot_general | solution.py:259
  72.4 3.3 %multiply_convert_fusion = f16[1024,1152]{1,0:T(8,128)(2,1)} fusion(f32[1024,1152]{1,0:T(8,128)S(1)} %fusion.3, bf16[512,1152]{1,0:T(8,128)(2,1)S(1)} %constant_dynamic-update-slice_fusion.mine_ref, bf16[1024,1024]{1,0:T(8,128)(2,1)S(1)} %get-tuple-element.26), kind=kOutput, calls=%fused_computation.3 | convolution fusion | flops 1215037440 | bytes 9306112 | tf_op jit(solution)/shard_map/dot_general | solution.py:259
  75.7 6.6 %all-to-all-start.1 = ((f16[16,64,1152]{2,1,0:T(8,128)(2,1)}), f16[16,64,1152]{2,1,0:T(8,128)(2,1)S(1)}, u32[]{:S(2)}, u32[]{:S(2)}) async-start(f16[16,64,1152]{2,1,0:T(8,128)(2,1)} %bitcast.7), calls=%async_computation.1 | async-start | bytes 4718592 | tf_op jit(solution)/shard_map/all_to_all | solution.py:264
  82.3 1.5 %multiply_convert_fusion.7 = (f16[64,1152]{1,0:T(8,128)(2,1)S(1)}, f16[64,1152]{1,0:T(8,128)(2,1)S(1)}) fusion(f32[512,1152]{1,0:T(8,128)} %fusion.7, f16[512,1152]{1,0:T(8,128)(2,1)} %collective-permute-done.11), kind=kLoop, calls=%fused_computation.47 | loop fusion | flops 1474560 | bytes 1179648 | tf_op jit(solution)/shard_map/convert_element_type | solution.py:71
  83.8 1.7 %collective-permute-start.12 = (f16[64,1152]{1,0:T(8,128)(2,1)S(1)}, f16[64,1152]{1,0:T(8,128)(2,1)S(1)}, u32[]{:S(2)}, u32[]{:S(2)}) collective-permute-start(f16[64,1152]{1,0:T(8,128)(2,1)S(1)} %get-tuple-element.50), channel_id=1, source_target_pairs={{0,112},{1,113},{2,114},{3,115},{4,116},{5,117},{6,118},{7,119},{8... | collective-permute-start | bytes 442376 | tf_op jit(solution)/shard_map/ppermute | solution.py:49
  85.9 4.2 %collective-permute-start.14 = (f32[3]{0:T(128)S(1)}, f32[3]{0:T(128)S(1)}, u32[]{:S(2)}, u32[]{:S(2)}) collective-permute-start(f32[3]{0:T(128)S(1)} %add_add_fusion), channel_id=1, source_target_pairs={{0,64},{1,65},{2,66},{3,67},{4,68},{5,69},{6,70},{7,71},{8,72},{9,... | collective-permute-start | bytes 44 | tf_op jit(solution)/shard_map/ppermute | solution.py:58
  90.1 3.4 %collective-permute-done.14 = f32[3]{0:T(128)S(1)} collective-permute-done((f32[3]{0:T(128)S(1)}, f32[3]{0:T(128)S(1)}, u32[]{:S(2)}, u32[]{:S(2)}) %collective-permute-start.14) | collective-permute-done | bytes 44 | tf_op jit(solution)/shard_map/ppermute | solution.py:58
  93.5 1.5 %multiply_convert_fusion.5 = (f16[64,1152]{1,0:T(8,128)(2,1)S(1)}, f16[64,1152]{1,0:T(8,128)(2,1)S(1)}) fusion(f32[512,1152]{1,0:T(8,128)} %fusion.7, f16[64,1152]{1,0:T(8,128)(2,1)S(1)} %collective-permute-done.13, f16[512,1152]{1,0:T(8,128)(2,1)} %collective-permute-done.11, f16[64,1152]{1,0:T(8,128)(2,1)S(1)} %collective-permute-done.12), kind=kLoop, calls=%fused_computation.45 | loop fusion | flops 2211840 | bytes 1474560 | tf_op jit(solution)/shard_map/convert_element_type | solution.py:71
  94.9 2.8 %collective-permute-start.15 = (f16[64,1152]{1,0:T(8,128)(2,1)S(1)}, f16[64,1152]{1,0:T(8,128)(2,1)S(1)}, u32[]{:S(2)}, u32[]{:S(2)}) collective-permute-start(f16[64,1152]{1,0:T(8,128)(2,1)S(1)} %get-tuple-element.48), channel_id=1, source_target_pairs={{0,112},{1,113},{2,114},{3,115},{4,116},{5,117},{6,118},{7,119},{8... | collective-permute-start | bytes 442376 | tf_op jit(solution)/shard_map/ppermute | solution.py:49
  98.6 3.6 %collective-permute-done.17 = f32[3]{0:T(128)S(1)} collective-permute-done((f32[3]{0:T(128)S(1)}, f32[3]{0:T(128)S(1)}, u32[]{:S(2)}, u32[]{:S(2)}) %collective-permute-start.17) | collective-permute-done | bytes 44 | tf_op jit(solution)/shard_map/ppermute | solution.py:58
  102.2 1.9 %collective-permute-done.16 = f16[64,1152]{1,0:T(8,128)(2,1)S(1)} collective-permute-done((f16[64,1152]{1,0:T(8,128)(2,1)S(1)}, f16[64,1152]{1,0:T(8,128)(2,1)S(1)}, u32[]{:S(2)}, u32[]{:S(2)}) %collective-permute-start.16) | collective-permute-done | bytes 147488 | tf_op jit(solution)/shard_map/ppermute | solution.py:49
  105.4 1.4 %collective-permute-start.18 = (f16[64,1152]{1,0:T(8,128)(2,1)S(1)}, f16[64,1152]{1,0:T(8,128)(2,1)S(1)}, u32[]{:S(2)}, u32[]{:S(2)}) collective-permute-start(f16[64,1152]{1,0:T(8,128)(2,1)S(1)} %get-tuple-element.46), channel_id=1, source_target_pairs={{0,112},{1,113},{2,114},{3,115},{4,116},{5,117},{6,118},{7,119},{8... | collective-permute-start | bytes 442376 | tf_op jit(solution)/shard_map/ppermute | solution.py:49
  107.5 3.5 %collective-permute-done.20 = f32[3]{0:T(128)S(1)} collective-permute-done((f32[3]{0:T(128)S(1)}, f32[3]{0:T(128)S(1)}, u32[]{:S(2)}, u32[]{:S(2)}) %collective-permute-start.20) | collective-permute-done | bytes 44 | tf_op jit(solution)/shard_map/ppermute | solution.py:58
  111.1 2.1 %collective-permute-done.19 = f16[64,1152]{1,0:T(8,128)(2,1)S(1)} collective-permute-done((f16[64,1152]{1,0:T(8,128)(2,1)S(1)}, f16[64,1152]{1,0:T(8,128)(2,1)S(1)}, u32[]{:S(2)}, u32[]{:S(2)}) %collective-permute-start.19) | collective-permute-done | bytes 147488 | tf_op jit(solution)/shard_map/ppermute | solution.py:49
  116.1 3.6 %collective-permute-done.21 = f16[64,1152]{1,0:T(8,128)(2,1)S(1)} collective-permute-done((f16[64,1152]{1,0:T(8,128)(2,1)S(1)}, f16[64,1152]{1,0:T(8,128)(2,1)S(1)}, u32[]{:S(2)}, u32[]{:S(2)}) %collective-permute-start.21) | collective-permute-done | bytes 147488 | tf_op jit(solution)/shard_map/ppermute | solution.py:49
  121.8 2.7 %collective-permute-start.23 = (f32[3]{0:T(128)S(1)}, f32[3]{0:T(128)S(1)}, u32[]{:S(2)}, u32[]{:S(2)}) collective-permute-start(f32[3]{0:T(128)S(1)} %add.105), channel_id=1, source_target_pairs={{0,6},{1,7},{2,0},{3,1},{4,2},{5,3},{6,4},{7,5},{8,14},{9,15},{10,... | collective-permute-start | bytes 44 | tf_op jit(solution)/shard_map/ppermute | solution.py:67
  127.9 1.6 %collective-permute-done.24 = f32[3]{0:T(128)S(1)} collective-permute-done((f32[3]{0:T(128)S(1)}, f32[3]{0:T(128)S(1)}, u32[]{:S(2)}, u32[]{:S(2)}) %collective-permute-start.24) | collective-permute-done | bytes 44 | tf_op jit(solution)/shard_map/ppermute | solution.py:67
  (61 shorter events, 16.8 us)
Async XLA Ops:
  0.6 0.9 copy-start
  1.5 1.7 %copy-start.2 = (bf16[64,1152]{1,0:T(8,128)(2,1)S(1)}, bf16[64,1152]{1,0:T(8,128)(2,1)}, u32[]{:S(2)}) copy-start(bf16[64,1152]{1,0:T(8,128)(2,1)} %rows_ref.6) | copy-start | bytes 442372
  3.4 13.5 %collective-permute-start = (bf16[64,1152]{1,0:T(8,128)(2,1)S(1)}, bf16[64,1152]{1,0:T(8,128)(2,1)S(1)}, u32[]{:S(2)}, u32[]{:S(2)}) collective-permute-start(bf16[64,1152]{1,0:T(8,128)(2,1)S(1)} %shard_map.68), channel_id=1, source_target_pairs={{0,16},{1,17},{2,18},{3,19},{4,20},{5,21},{6,22},{7,23},{8,24},{9,... | collective-permute-start | bytes 442376 | tf_op jit(solution)/shard_map/ppermute | solution.py:49
  5.4 11.6 %collective-permute-start.4 = (bf16[64,1152]{1,0:T(8,128)(2,1)S(1)}, bf16[64,1152]{1,0:T(8,128)(2,1)S(1)}, u32[]{:S(2)}, u32[]{:S(2)}) collective-permute-start(bf16[64,1152]{1,0:T(8,128)(2,1)S(1)} %shard_map.68), channel_id=1, source_target_pairs={{0,112},{1,113},{2,114},{3,115},{4,116},{5,117},{6,118},{7,119},{8... | collective-permute-start | bytes 442376 | tf_op jit(solution)/shard_map/ppermute | solution.py:49
  9.4 39.9 %all-to-all-start = ((bf16[16,64,1152]{2,1,0:T(8,128)(2,1)}), bf16[16,64,1152]{2,1,0:T(8,128)(2,1)}, u32[]{:S(2)}, u32[]{:S(2)}) async-start(bf16[16,64,1152]{2,1,0:T(8,128)(2,1)} %shard_map.67), calls=%async_computation | async-start | bytes 4718592 | tf_op jit(solution)/shard_map/all_to_all | solution.py:241
  16.9 6.4 %collective-permute-start.1 = (bf16[64,1152]{1,0:T(8,128)(2,1)S(1)}, bf16[64,1152]{1,0:T(8,128)(2,1)S(1)}, u32[]{:S(2)}, u32[]{:S(2)}) collective-permute-start(bf16[64,1152]{1,0:T(8,128)(2,1)S(1)} %collective-permute-done), channel_id=1, source_target_pairs={{0,16},{1,17},{2,18},{3,19},{4,20},{5,21},{6,22},{7,23},{8,24},{9,... | collective-permute-start | bytes 442376 | tf_op jit(solution)/shard_map/ppermute | solution.py:49
  17.0 6.3 %collective-permute-start.5 = (bf16[64,1152]{1,0:T(8,128)(2,1)S(1)}, bf16[64,1152]{1,0:T(8,128)(2,1)S(1)}, u32[]{:S(2)}, u32[]{:S(2)}) collective-permute-start(bf16[64,1152]{1,0:T(8,128)(2,1)S(1)} %collective-permute-done.4), channel_id=1, source_target_pairs={{0,112},{1,113},{2,114},{3,115},{4,116},{5,117},{6,118},{7,119},{8... | collective-permute-start | bytes 442376 | tf_op jit(solution)/shard_map/ppermute | solution.py:49
  23.4 6.4 %collective-permute-start.2 = (bf16[64,1152]{1,0:T(8,128)(2,1)S(1)}, bf16[64,1152]{1,0:T(8,128)(2,1)S(1)}, u32[]{:S(2)}, u32[]{:S(2)}) collective-permute-start(bf16[64,1152]{1,0:T(8,128)(2,1)S(1)} %collective-permute-done.1), channel_id=1, source_target_pairs={{0,16},{1,17},{2,18},{3,19},{4,20},{5,21},{6,22},{7,23},{8,24},{9,... | collective-permute-start | bytes 442376 | tf_op jit(solution)/shard_map/ppermute | solution.py:49
  23.4 12.7 %collective-permute-start.6 = (bf16[64,1152]{1,0:T(8,128)(2,1)S(1)}, bf16[64,1152]{1,0:T(8,128)(2,1)S(1)}, u32[]{:S(2)}, u32[]{:S(2)}) collective-permute-start(bf16[64,1152]{1,0:T(8,128)(2,1)S(1)} %collective-permute-done.5), channel_id=1, source_target_pairs={{0,112},{1,113},{2,114},{3,115},{4,116},{5,117},{6,118},{7,119},{8... | collective-permute-start | bytes 442376 | tf_op jit(solution)/shard_map/ppermute | solution.py:49
  29.7 6.4 %collective-permute-start.3 = (bf16[64,1152]{1,0:T(8,128)(2,1)S(1)}, bf16[64,1152]{1,0:T(8,128)(2,1)S(1)}, u32[]{:S(2)}, u32[]{:S(2)}) collective-permute-start(bf16[64,1152]{1,0:T(8,128)(2,1)S(1)} %collective-permute-done.2), channel_id=1, source_target_pairs={{0,16},{1,17},{2,18},{3,19},{4,20},{5,21},{6,22},{7,23},{8,24},{9,... | collective-permute-start | bytes 442376 | tf_op jit(solution)/shard_map/ppermute | solution.py:49
  36.2 2.9 %collective-permute-start.7 = (bf16[512,1152]{1,0:T(8,128)(2,1)S(1)}, bf16[512,1152]{1,0:T(8,128)(2,1)S(1)}, u32[]{:S(2)}, u32[]{:S(2)}) collective-permute-start(bf16[512,1152]{1,0:T(8,128)(2,1)S(1)} %constant_dynamic-update-slice_fusion.mine_ref), channel_id=1, source_target_pairs={{0,8},{1,9},{2,10},{3,11},{4,12},{5,13},{6,14},{7,15},{8,0},{9,1},... | collective-permute-start | bytes 3538952 | tf_op jit(solution)/shard_map/ppermute | solution.py:49
  56.9 18.8 %collective-permute-start.8 = (f32[3]{0:T(128)S(1)}, f32[3]{0:T(128)S(1)}, u32[]{:S(2)}, u32[]{:S(2)}) collective-permute-start(f32[3]{0:T(128)S(1)} %get-tuple-element.27), channel_id=1, source_target_pairs={{0,1},{1,128},{2,3},{3,130},{4,5},{5,132},{6,7},{7,134},{8,9},{9,1... | collective-permute-start | bytes 44 | tf_op jit(solution)/shard_map/ppermute | solution.py:67
  58.3 17.4 %collective-permute-start.9 = (f32[3]{0:T(128)S(1)}, f32[3]{0:T(128)S(1)}, u32[]{:S(2)}, u32[]{:S(2)}) collective-permute-start(f32[3]{0:T(128)S(1)} %get-tuple-element.27), channel_id=1, source_target_pairs={{0,128},{1,129},{2,130},{3,131},{4,132},{5,133},{6,134},{7,135},{8... | collective-permute-start | bytes 44 | tf_op jit(solution)/shard_map/ppermute | solution.py:67
  60.6 15.1 %collective-permute-start.10 = (f32[3]{0:T(128)S(1)}, f32[3]{0:T(128)S(1)}, u32[]{:S(2)}, u32[]{:S(2)}) collective-permute-start(f32[3]{0:T(128)S(1)} %get-tuple-element.27), channel_id=1, source_target_pairs={{0,129},{1,0},{2,131},{3,2},{4,133},{5,4},{6,135},{7,6},{8,137},{9... | collective-permute-start | bytes 44 | tf_op jit(solution)/shard_map/ppermute | solution.py:67
  66.2 16.1 %collective-permute-start.11 = (f16[512,1152]{1,0:T(8,128)(2,1)}, f16[512,1152]{1,0:T(8,128)(2,1)}, u32[]{:S(2)}, u32[]{:S(2)}) collective-permute-start(f16[512,1152]{1,0:T(8,128)(2,1)} %multiply_convert_fusion.1), channel_id=1, source_target_pairs={{0,8},{1,9},{2,10},{3,11},{4,12},{5,13},{6,14},{7,15},{8,0},{9,1},... | collective-permute-start | bytes 3538952 | tf_op jit(solution)/shard_map/ppermute | solution.py:49
  75.7 46.0 %all-to-all-start.1 = ((f16[16,64,1152]{2,1,0:T(8,128)(2,1)}), f16[16,64,1152]{2,1,0:T(8,128)(2,1)S(1)}, u32[]{:S(2)}, u32[]{:S(2)}) async-start(f16[16,64,1152]{2,1,0:T(8,128)(2,1)} %bitcast.7), calls=%async_computation.1 | async-start | bytes 4718592 | tf_op jit(solution)/shard_map/all_to_all | solution.py:264
  82.3 21.8 %copy-start.3 = (f32[512,1152]{1,0:T(8,128)S(1)}, f32[512,1152]{1,0:T(8,128)}, u32[]{:S(2)}) copy-start(f32[512,1152]{1,0:T(8,128)} %fusion.7) | copy-start | bytes 7077892
  83.8 9.6 %collective-permute-start.12 = (f16[64,1152]{1,0:T(8,128)(2,1)S(1)}, f16[64,1152]{1,0:T(8,128)(2,1)S(1)}, u32[]{:S(2)}, u32[]{:S(2)}) collective-permute-start(f16[64,1152]{1,0:T(8,128)(2,1)S(1)} %get-tuple-element.50), channel_id=1, source_target_pairs={{0,112},{1,113},{2,114},{3,115},{4,116},{5,117},{6,118},{7,119},{8... | collective-permute-start | bytes 442376 | tf_op jit(solution)/shard_map/ppermute | solution.py:49
  85.5 8.0 %collective-permute-start.13 = (f16[64,1152]{1,0:T(8,128)(2,1)S(1)}, f16[64,1152]{1,0:T(8,128)(2,1)S(1)}, u32[]{:S(2)}, u32[]{:S(2)}) collective-permute-start(f16[64,1152]{1,0:T(8,128)(2,1)S(1)} %get-tuple-element.49), channel_id=1, source_target_pairs={{0,16},{1,17},{2,18},{3,19},{4,20},{5,21},{6,22},{7,23},{8,24},{9,... | collective-permute-start | bytes 442376 | tf_op jit(solution)/shard_map/ppermute | solution.py:49
  85.9 7.5 %collective-permute-start.14 = (f32[3]{0:T(128)S(1)}, f32[3]{0:T(128)S(1)}, u32[]{:S(2)}, u32[]{:S(2)}) collective-permute-start(f32[3]{0:T(128)S(1)} %add_add_fusion), channel_id=1, source_target_pairs={{0,64},{1,65},{2,66},{3,67},{4,68},{5,69},{6,70},{7,71},{8,72},{9,... | collective-permute-start | bytes 44 | tf_op jit(solution)/shard_map/ppermute | solution.py:58
  94.9 7.3 %collective-permute-start.15 = (f16[64,1152]{1,0:T(8,128)(2,1)S(1)}, f16[64,1152]{1,0:T(8,128)(2,1)S(1)}, u32[]{:S(2)}, u32[]{:S(2)}) collective-permute-start(f16[64,1152]{1,0:T(8,128)(2,1)S(1)} %get-tuple-element.48), channel_id=1, source_target_pairs={{0,112},{1,113},{2,114},{3,115},{4,116},{5,117},{6,118},{7,119},{8... | collective-permute-start | bytes 442376 | tf_op jit(solution)/shard_map/ppermute | solution.py:49
  97.7 6.4 %collective-permute-start.16 = (f16[64,1152]{1,0:T(8,128)(2,1)S(1)}, f16[64,1152]{1,0:T(8,128)(2,1)S(1)}, u32[]{:S(2)}, u32[]{:S(2)}) collective-permute-start(f16[64,1152]{1,0:T(8,128)(2,1)S(1)} %get-tuple-element.47), channel_id=1, source_target_pairs={{0,16},{1,17},{2,18},{3,19},{4,20},{5,21},{6,22},{7,23},{8,24},{9,... | collective-permute-start | bytes 442376 | tf_op jit(solution)/shard_map/ppermute | solution.py:49
  97.8 4.4 %collective-permute-start.17 = (f32[3]{0:T(128)S(1)}, f32[3]{0:T(128)S(1)}, u32[]{:S(2)}, u32[]{:S(2)}) collective-permute-start(f32[3]{0:T(128)S(1)} %add.92), channel_id=1, source_target_pairs={{0,32},{1,33},{2,34},{3,35},{4,36},{5,37},{6,38},{7,39},{8,40},{9,... | collective-permute-start | bytes 44 | tf_op jit(solution)/shard_map/ppermute | solution.py:58
  105.4 5.7 %collective-permute-start.18 = (f16[64,1152]{1,0:T(8,128)(2,1)S(1)}, f16[64,1152]{1,0:T(8,128)(2,1)S(1)}, u32[]{:S(2)}, u32[]{:S(2)}) collective-permute-start(f16[64,1152]{1,0:T(8,128)(2,1)S(1)} %get-tuple-element.46), channel_id=1, source_target_pairs={{0,112},{1,113},{2,114},{3,115},{4,116},{5,117},{6,118},{7,119},{8... | collective-permute-start | bytes 442376 | tf_op jit(solution)/shard_map/ppermute | solution.py:49
  106.8 6.4 %collective-permute-start.19 = (f16[64,1152]{1,0:T(8,128)(2,1)S(1)}, f16[64,1152]{1,0:T(8,128)(2,1)S(1)}, u32[]{:S(2)}, u32[]{:S(2)}) collective-permute-start(f16[64,1152]{1,0:T(8,128)(2,1)S(1)} %get-tuple-element.45), channel_id=1, source_target_pairs={{0,16},{1,17},{2,18},{3,19},{4,20},{5,21},{6,22},{7,23},{8,24},{9,... | collective-permute-start | bytes 442376 | tf_op jit(solution)/shard_map/ppermute | solution.py:49
  107.5 3.5 %collective-permute-start.20 = (f32[3]{0:T(128)S(1)}, f32[3]{0:T(128)S(1)}, u32[]{:S(2)}, u32[]{:S(2)}) collective-permute-start(f32[3]{0:T(128)S(1)} %add.97), channel_id=1, source_target_pairs={{0,16},{1,17},{2,18},{3,19},{4,20},{5,21},{6,22},{7,23},{8,24},{9,... | collective-permute-start | bytes 44 | tf_op jit(solution)/shard_map/ppermute | solution.py:58
  114.3 5.4 %collective-permute-start.21 = (f16[64,1152]{1,0:T(8,128)(2,1)S(1)}, f16[64,1152]{1,0:T(8,128)(2,1)S(1)}, u32[]{:S(2)}, u32[]{:S(2)}) collective-permute-start(f16[64,1152]{1,0:T(8,128)(2,1)S(1)} %multiply_convert_fusion.2), channel_id=1, source_target_pairs={{0,112},{1,113},{2,114},{3,115},{4,116},{5,117},{6,118},{7,119},{8... | collective-permute-start | bytes 442376 | tf_op jit(solution)/shard_map/ppermute | solution.py:49
  115.0 1.1 collective-permute-start.22
  119.7 7.2 %copy-start.1 = (bf16[64,1152]{1,0:T(8,128)(2,1)S(1)}, bf16[64,1152]{1,0:T(8,128)(2,1)}, u32[]{:S(2)}) copy-start(bf16[64,1152]{1,0:T(8,128)(2,1)} %rows_ref.5) | copy-start | bytes 442372
  121.8 6.1 %collective-permute-start.23 = (f32[3]{0:T(128)S(1)}, f32[3]{0:T(128)S(1)}, u32[]{:S(2)}, u32[]{:S(2)}) collective-permute-start(f32[3]{0:T(128)S(1)} %add.105), channel_id=1, source_target_pairs={{0,6},{1,7},{2,0},{3,1},{4,2},{5,3},{6,4},{7,5},{8,14},{9,15},{10,... | collective-permute-start | bytes 44 | tf_op jit(solution)/shard_map/ppermute | solution.py:67
  124.4 5.0 %collective-permute-start.24 = (f32[3]{0:T(128)S(1)}, f32[3]{0:T(128)S(1)}, u32[]{:S(2)}, u32[]{:S(2)}) collective-permute-start(f32[3]{0:T(128)S(1)} %add.105), channel_id=1, source_target_pairs={{0,4},{1,5},{2,6},{3,7},{4,0},{5,1},{6,2},{7,3},{8,12},{9,13},{10,... | collective-permute-start | bytes 44 | tf_op jit(solution)/shard_map/ppermute | solution.py:67
  125.3 4.8 %collective-permute-start.25 = (f32[3]{0:T(128)S(1)}, f32[3]{0:T(128)S(1)}, u32[]{:S(2)}, u32[]{:S(2)}) collective-permute-start(f32[3]{0:T(128)S(1)} %add.105), channel_id=1, source_target_pairs={{0,2},{1,3},{2,4},{3,5},{4,6},{5,7},{6,0},{7,1},{8,10},{9,11},{10,... | collective-permute-start | bytes 44 | tf_op jit(solution)/shard_map/ppermute | solution.py:67

commit v5 on v4

--- a/solution.py
+++ b/solution.py
@@ -13,6 +13,8 @@
 PEERS = 16
 DEPTH = 8
 CODE = 1024.0
+EXTRA = 8
+PAIRS = 1024.0 * 1024.0
 BF16 = jnp.bfloat16
 F32 = jnp.float32
 F16 = jnp.float16
@@ -251,11 +253,14 @@
     grad_low, sums = pairs(first, scale, bias, imgs, mine, theirs)
     half = DEPTH * rows
 
-    txt_part = lax.dot_general(grad_low[:, half:], imgs, (((0,), (0,)), ((), ())), preferred_element_type=F32)
-    theirs_part = other_core(coded(txt_part))
-    mine_part = lax.dot_general(grad_low[:, :half], imgs, (((0,), (0,)), ((), ())), preferred_element_type=F32)
-
     arrived = [moved(sums, by, 0) for by in (1, 2, 3)]
+    txt_part = lax.dot_general(grad_low, imgs, (((0,), (0,)), ((), ())), preferred_element_type=F32)
+    txt_part, grad_low, *arrived = lax.optimization_barrier((txt_part, grad_low, *arrived))
+    theirs_part = other_core(coded(txt_part[half:])).reshape(DEPTH, rows, emb)
+    mine_part = txt_part[:half].reshape(DEPTH, rows, emb)
+    sums = sums + arrived[0] + arrived[1] + arrived[2]
+
+    arrived = [moved(sums, 0, by) for by in (1, 2, 3)]
     img_part = jnp.dot(grad_low[:, :half], mine, preferred_element_type=F32) + jnp.dot(
         grad_low[:, half:], theirs, preferred_element_type=F32
     )
@@ -263,36 +268,23 @@
     img_part, *arrived = lax.optimization_barrier((img_part, *arrived))
     img_recv = lax.all_to_all(img_part, PLANE, 0, 0)
     sums = sums + arrived[0] + arrived[1] + arrived[2]
-
-    mine_part = mine_part.reshape(DEPTH, rows, emb)
-    theirs_part = theirs_part.reshape(DEPTH, rows, emb)
-    block = lambda k: mine_part[k] + decoded(theirs_part[k])
-    left, right = along_z(coded(block(4)), -1), along_z(coded(block(5)), 1)
-    arrived = flipped(sums, 1, 4)
-    left, right, arrived = lax.optimization_barrier((left, right, arrived))
-    left, right, sums = decoded(left) + block(3), decoded(right) + block(6), sums + arrived
-
-    left, right = along_z(coded(left), -1), along_z(coded(right), 1)
-    arrived = flipped(sums, 1, 2)
-    left, right, arrived = lax.optimization_barrier((left, right, arrived))
-    left, right, sums = decoded(left) + block(2), decoded(right) + block(7), sums + arrived
-
-    left, right = along_z(coded(left), -1), along_z(coded(right), 1)
-    arrived = flipped(sums, 1, 1)
-    left, right, arrived = lax.optimization_barrier((left, right, arrived))
-    left, sums = decoded(left) + block(1), sums + arrived
-
-    left = along_z(coded(left), -1)
-    arrived = flipped(sums, 2, 1)
-    left, arrived = lax.optimization_barrier((left, arrived))
-    txt_total = block(0) + decoded(left) + decoded(right)
-    sums = sums + arrived
-
-    img_recv, sums = lax.optimization_barrier((img_recv, sums))
-    for by in (1, 2, 3):
-        arrived = moved(sums, 0, by)
-        stats = arrived + (sums if by == 1 else stats)
-    stats = stats / (rows * 256)
+    sums = (sums + flipped(sums, 2, 1)) / (PAIRS * PEERS)
+
+    riding = jnp.broadcast_to(jnp.pad(sums, (0, EXTRA - 3))[:, None], (EXTRA, emb))
+
+    def block(k):
+        return jnp.concatenate([mine_part[k] + decoded(theirs_part[k]), riding], axis=0)
+
+    far = [along_z(coded(block(4)), -2), along_z(coded(block(5)), 2), along_z(coded(block(3)), -2)]
+    near = [
+        along_z(coded(block(6)), 2),
+        along_z(coded(block(2) + decoded(far[0])), -2),
+        along_z(coded(block(7) + decoded(far[1])), 1),
+        along_z(coded(block(1) + decoded(far[2])), -1),
+    ]
+    total = block(0) + decoded(near[0]) + decoded(near[1]) + decoded(near[2]) + decoded(near[3])
+    txt_total = total[:rows]
+    stats = total[rows : rows + 3, 0] * (PAIRS * PEERS / (rows * 256))
     img_total = jnp.sum(decoded(img_recv), axis=0)
 
     image_grad = projected(scale, images, img_total)

time: 131 us -> 123 us (0.939)
  waiting for transfers between devices: 45.6 us -> 40.5 us
  matrix products: 13.9 us -> 9.46 us
  starting transfers between devices: 48.7 us -> 52 us
    ppermute x4 -> x1, waiting for transfers between devices: 11.6 us -> 1.11 us  [flipped(): return lax.ppermute(array, AXES, pairs)]
    ppermute x16, waiting for transfers between devices: 21.6 us -> 31.8 us  [shifted(): return lax.ppermute(array, AXES, pairs)]
    ppermute x16, starting transfers between devices: 20.4 us -> 28.3 us  [shifted(): return lax.ppermute(array, AXES, pairs)]
    ppermute x4 -> x1, starting transfers between devices: 5.05 us -> 0.09 us  [flipped(): return lax.ppermute(array, AXES, pairs)]
    dot_general x2 -> x1, matrix products: 9.1 us -> 4.59 us  [on_device(): lax.dot_general(grad_low, imgs, (((0,), (0,)), ((), ())), preferred_eleme...]
    all_to_all x1, waiting for transfers between devices: 10.2 us -> 6.98 us  [on_device(): imgs = lax.all_to_all(copies, PLANE, 0, 0).reshape(PEERS * rows, emb)]
    convert_element_type x4 -> x3, other arithmetic: 5.37 us -> 2.43 us  [coded(): (array * lax.rsqrt(jnp.maximum(jnp.abs(array), 1e-36)) * CODE).astype(F16)]
    ppermute x6, waiting for transfers between devices: 2.17 us -> 0.02 us  [moved(): return lax.ppermute(array, AXES, pairs)]
  transfers between devices with their start and end apart: 28 -> 25, of which waited for: 14 -> 12; matrix products, arithmetic and copies ran while one was open for 16% -> 12% of each run, Pallas kernels for 1% -> 1%
where the time goes in v5:
time: 123 us
  starting transfers between devices  52 us (42%)
  waiting for transfers between devices  40.5 us (33%)
  Pallas kernels  11.3 us (9%)
  matrix products  9.46 us (8%)
  other arithmetic  6.52 us (5%)
  between operations  2.19 us (2%)
    ppermute x16, waiting for transfers between devices, shifted(): return lax.ppermute(array, AXES, pairs)  31.8 us
    ppermute x16, starting transfers between devices, shifted(): return lax.ppermute(array, AXES, pairs)  28.3 us
    ppermute x6, starting transfers between devices, moved(): return lax.ppermute(array, AXES, pairs)  9.72 us
    pallas_call x1, Pallas kernels, pairs(): pl.pallas_call(pair_kernel, grid=(count // rows,), in_specs=[SMEM, SMEM,...  7.59 us
    all_to_all x1, starting transfers between devices, on_device(): imgs = lax.all_to_all(copies, PLANE, 0, 0).reshape(PEERS * rows, emb)  7.48 us
    all_to_all x1, waiting for transfers between devices, on_device(): imgs = lax.all_to_all(copies, PLANE, 0, 0).reshape(PEERS * rows, emb)  6.98 us
    all_to_all x1, starting transfers between devices, on_device(): img_recv = lax.all_to_all(img_part, PLANE, 0, 0)  6.36 us
    dot_general x1, matrix products, on_device(): lax.dot_general(grad_low, imgs, (((0,), (0,)), ((), ())), preferred_eleme...  4.59 us
  transfers between devices with their start and end apart: 25, of which 12 were waited for; matrix products, arithmetic and copies ran while one was open for 12% of the time, Pallas kernels for 1%

profile of v5, /device:TPU:2, one launch (start us, length us, event | category | flops | bytes accessed | tf_op | source)
XLA Modules:
  0.0 123.1 jit_solution(12309130557667524539)
XLA Ops:
  1.5 1.7 %shard_map.67 = bf16[16,64,1152]{2,1,0:T(8,128)(2,1)} custom-call(bf16[64,1152]{1,0:T(8,128)(2,1)S(1)} %copy-done), custom_call_target="tpu_custom_call" | custom-call | flops 1000000 | bytes 3145728 | tf_op jit(solution)/shard_map/pallas_call | solution.py:225
  3.4 5.9 %collective-permute-start.4 = (bf16[64,1152]{1,0:T(8,128)(2,1)S(1)}, bf16[64,1152]{1,0:T(8,128)(2,1)S(1)}, u32[]{:S(2)}, u32[]{:S(2)}) collective-permute-start(bf16[64,1152]{1,0:T(8,128)(2,1)S(1)} %shard_map.68), channel_id=1, source_target_pairs={{0,112},{1,113},{2,114},{3,115},{4,116},{5,117},{6,118},{7,119},{8... | collective-permute-start | bytes 442376 | tf_op jit(solution)/shard_map/ppermute | solution.py:51
  9.3 7.5 %all-to-all-start = ((bf16[16,64,1152]{2,1,0:T(8,128)(2,1)}), bf16[16,64,1152]{2,1,0:T(8,128)(2,1)}, u32[]{:S(2)}, u32[]{:S(2)}) async-start(bf16[16,64,1152]{2,1,0:T(8,128)(2,1)} %shard_map.67), calls=%async_computation | async-start | bytes 4718592 | tf_op jit(solution)/shard_map/all_to_all | solution.py:243
  16.8 3.3 %collective-permute-start.5 = (bf16[64,1152]{1,0:T(8,128)(2,1)S(1)}, bf16[64,1152]{1,0:T(8,128)(2,1)S(1)}, u32[]{:S(2)}, u32[]{:S(2)}) collective-permute-start(bf16[64,1152]{1,0:T(8,128)(2,1)S(1)} %collective-permute-done.4), channel_id=1, source_target_pairs={{0,112},{1,113},{2,114},{3,115},{4,116},{5,117},{6,118},{7,119},{8... | collective-permute-start | bytes 442376 | tf_op jit(solution)/shard_map/ppermute | solution.py:51
  20.2 2.6 %collective-permute-done.5 = bf16[64,1152]{1,0:T(8,128)(2,1)S(1)} collective-permute-done((bf16[64,1152]{1,0:T(8,128)(2,1)S(1)}, bf16[64,1152]{1,0:T(8,128)(2,1)S(1)}, u32[]{:S(2)}, u32[]{:S(2)}) %collective-permute-start.5) | collective-permute-done | bytes 147488 | tf_op jit(solution)/shard_map/ppermute | solution.py:51
  22.8 3.7 %collective-permute-start.6 = (bf16[64,1152]{1,0:T(8,128)(2,1)S(1)}, bf16[64,1152]{1,0:T(8,128)(2,1)S(1)}, u32[]{:S(2)}, u32[]{:S(2)}) collective-permute-start(bf16[64,1152]{1,0:T(8,128)(2,1)S(1)} %collective-permute-done.5), channel_id=1, source_target_pairs={{0,112},{1,113},{2,114},{3,115},{4,116},{5,117},{6,118},{7,119},{8... | collective-permute-start | bytes 442376 | tf_op jit(solution)/shard_map/ppermute | solution.py:51
  26.5 6.3 %collective-permute-done.2 = bf16[64,1152]{1,0:T(8,128)(2,1)S(1)} collective-permute-done((bf16[64,1152]{1,0:T(8,128)(2,1)S(1)}, bf16[64,1152]{1,0:T(8,128)(2,1)S(1)}, u32[]{:S(2)}, u32[]{:S(2)}) %collective-permute-start.2) | collective-permute-done | bytes 147488 | tf_op jit(solution)/shard_map/ppermute | solution.py:51
  32.9 6.3 %collective-permute-done.3 = bf16[64,1152]{1,0:T(8,128)(2,1)S(1)} collective-permute-done((bf16[64,1152]{1,0:T(8,128)(2,1)S(1)}, bf16[64,1152]{1,0:T(8,128)(2,1)S(1)}, u32[]{:S(2)}, u32[]{:S(2)}) %collective-permute-start.3) | collective-permute-done | bytes 147488 | tf_op jit(solution)/shard_map/ppermute | solution.py:51
  40.8 1.5 %collective-permute-done.7.theirs_ref = bf16[512,1152]{1,0:T(8,128)(2,1)S(1)} collective-permute-done((bf16[512,1152]{1,0:T(8,128)(2,1)S(1)}, bf16[512,1152]{1,0:T(8,128)(2,1)S(1)}, u32[]{:S(2)}, u32[]{:S(2)}) %collective-permute-start.7) | collective-permute-done | bytes 1179680 | tf_op jit(solution)/shard_map/ppermute | solution.py:51
  42.3 7.0 %all-to-all-done = bf16[16,64,1152]{2,1,0:T(8,128)(2,1)} async-done(((bf16[16,64,1152]{2,1,0:T(8,128)(2,1)}), bf16[16,64,1152]{2,1,0:T(8,128)(2,1)}, u32[]{:S(2)}, u32[]{:S(2)}) %all-to-all-start) | async-done | bytes 2359328 | tf_op jit(solution)/shard_map/all_to_all | solution.py:243
  49.2 7.6 %shard_map.69 = (bf16[1024,1024]{1,0:T(8,128)(2,1)S(1)}, f32[3]{0:T(128)S(1)}) custom-call(s32[1]{0:T(128)} %bitcast.first_ref, f32[1]{0:T(128)S(6)} %exp.3.scale_ref, f32[1]{0:T(128)S(6)} %copy.15.shift_ref, bf16[1024,1152]{1,0:T(8,128)(2,1)} %bitcast.1.img_ref, bf16[512,1152]{1,0:T(8,128)(2,1)S(1)} %constant_dynamic-update-slice_fusion.mine_ref, ...), custom_call_target="tpu_custom_call" | custom-call | flops 2415919104 | bytes 8388608 | tf_op jit(solution)/shard_map/pallas_call | solution.py:176
  56.8 1.6 %collective-permute-start.10 = (f32[3]{0:T(128)S(1)}, f32[3]{0:T(128)S(1)}, u32[]{:S(2)}, u32[]{:S(2)}) collective-permute-start(f32[3]{0:T(128)S(1)} %get-tuple-element.19), channel_id=1, source_target_pairs={{0,129},{1,0},{2,131},{3,2},{4,133},{5,4},{6,135},{7,6},{8,137},{9... | collective-permute-start | bytes 44 | tf_op jit(solution)/shard_map/ppermute | solution.py:69
  58.5 1.3 %collective-permute-start.9 = (f32[3]{0:T(128)S(1)}, f32[3]{0:T(128)S(1)}, u32[]{:S(2)}, u32[]{:S(2)}) collective-permute-start(f32[3]{0:T(128)S(1)} %get-tuple-element.19), channel_id=1, source_target_pairs={{0,128},{1,129},{2,130},{3,131},{4,132},{5,133},{6,134},{7,135},{8... | collective-permute-start | bytes 44 | tf_op jit(solution)/shard_map/ppermute | solution.py:69
  59.7 2.0 %collective-permute-start.8 = (f32[3]{0:T(128)S(1)}, f32[3]{0:T(128)S(1)}, u32[]{:S(2)}, u32[]{:S(2)}) collective-permute-start(f32[3]{0:T(128)S(1)} %get-tuple-element.19), channel_id=1, source_target_pairs={{0,1},{1,128},{2,3},{3,130},{4,5},{5,132},{6,7},{7,134},{8,9},{9,1... | collective-permute-start | bytes 44 | tf_op jit(solution)/shard_map/ppermute | solution.py:69
  61.7 4.6 %fusion.20 = f32[1024,1152]{1,0:T(8,128)S(1)} fusion(bf16[1024,1024]{1,0:T(8,128)(2,1)S(1)} %get-tuple-element.20, bf16[1024,1152]{1,0:T(8,128)(2,1)} %bitcast.1.img_ref), kind=kOutput, calls=%fused_computation.63 | convolution fusion | flops 2415919104 | bytes 9175040 | tf_op jit(solution)/shard_map/dot_general | solution.py:257
  66.3 3.9 %collective-permute-start.13 = (f32[3]{0:T(128)S(1)}, f32[3]{0:T(128)S(1)}, u32[]{:S(2)}, u32[]{:S(2)}) collective-permute-start(f32[3]{0:T(128)S(1)} %add_add_fusion.1), channel_id=1, source_target_pairs={{0,6},{1,7},{2,0},{3,1},{4,2},{5,3},{6,4},{7,5},{8,14},{9,15},{10,... | collective-permute-start | bytes 44 | tf_op jit(solution)/shard_map/ppermute | solution.py:69
  71.2 1.6 %multiply_convert_fusion.1 = f16[512,1152]{1,0:T(8,128)(2,1)} fusion(f32[1024,1152]{1,0:T(8,128)S(1)} %fusion.20), kind=kLoop, calls=%fused_computation.4 | loop fusion | flops 2949120 | bytes 3538944 | tf_op jit(solution)/shard_map/convert_element_type | solution.py:73
  72.8 1.5 %fusion.1 = f32[1024,1152]{1,0:T(8,128)S(1)} fusion(bf16[512,1152]{1,0:T(8,128)(2,1)S(1)} %collective-permute-done.7.theirs_ref, bf16[1024,1024]{1,0:T(8,128)(2,1)S(1)} %get-tuple-element.20), kind=kOutput, calls=%fused_computation.5 | convolution fusion | flops 1207959552 | bytes 6946816 | tf_op jit(solution)/shard_map/dot_general | solution.py:264
  74.4 3.3 %multiply_convert_fusion = f16[1024,1152]{1,0:T(8,128)(2,1)} fusion(f32[1024,1152]{1,0:T(8,128)S(1)} %fusion.1, bf16[512,1152]{1,0:T(8,128)(2,1)S(1)} %constant_dynamic-update-slice_fusion.mine_ref, bf16[1024,1024]{1,0:T(8,128)(2,1)S(1)} %get-tuple-element.20), kind=kOutput, calls=%fused_computation.3 | convolution fusion | flops 1215037440 | bytes 9306112 | tf_op jit(solution)/shard_map/dot_general | solution.py:264
  77.7 6.4 %all-to-all-start.1 = ((f16[16,64,1152]{2,1,0:T(8,128)(2,1)}), f16[16,64,1152]{2,1,0:T(8,128)(2,1)S(1)}, u32[]{:S(2)}, u32[]{:S(2)}) async-start(f16[16,64,1152]{2,1,0:T(8,128)(2,1)} %bitcast.7), calls=%async_computation.1 | async-start | bytes 4718592 | tf_op jit(solution)/shard_map/all_to_all | solution.py:269
  84.2 1.1 collective-permute-done.15
  85.4 2.3 %fusion.12 = (f32[64,1152]{1,0:T(8,128)S(1)}, f32[64,1152]{1,0:T(8,128)S(1)}, f32[64,1152]{1,0:T(8,128)S(1)}, f32[64,1152]{1,0:T(8,128)S(1)}, f32[64,1152]{1,0:T...) fusion(f32[1024,1152]{1,0:T(8,128)} %copy-done.3, ...), kind=kLoop, calls=%fused_computation.42 | loop fusion | flops 2949120 | bytes 5898240 | tf_op jit(solution)/shard_map/add | solution.py:276
  88.1 2.0 %collective-permute-start.17 = (f16[72,1152]{1,0:T(8,128)(2,1)S(1)}, f16[72,1152]{1,0:T(8,128)(2,1)S(1)}, u32[]{:S(2)}, u32[]{:S(2)}) collective-permute-start(f16[72,1152]{1,0:T(8,128)(2,1)S(1)} %get-tuple-element.41), channel_id=1, source_target_pairs={{0,96},{1,97},{2,98},{3,99},{4,100},{5,101},{6,102},{7,103},{8,104... | collective-permute-start | bytes 497672 | tf_op jit(solution)/shard_map/ppermute | solution.py:51
  90.0 1.0 collective-permute-start.19
  91.1 3.1 %collective-permute-start.21 = (f16[72,1152]{1,0:T(8,128)(2,1)S(1)}, f16[72,1152]{1,0:T(8,128)(2,1)S(1)}, u32[]{:S(2)}, u32[]{:S(2)}) collective-permute-start(f16[72,1152]{1,0:T(8,128)(2,1)S(1)} %get-tuple-element.43), channel_id=1, source_target_pairs={{0,96},{1,97},{2,98},{3,99},{4,100},{5,101},{6,102},{7,103},{8,104... | collective-permute-start | bytes 497672 | tf_op jit(solution)/shard_map/ppermute | solution.py:51
  94.2 3.8 %collective-permute-done.17 = f16[72,1152]{1,0:T(8,128)(2,1)S(1)} collective-permute-done((f16[72,1152]{1,0:T(8,128)(2,1)S(1)}, f16[72,1152]{1,0:T(8,128)(2,1)S(1)}, u32[]{:S(2)}, u32[]{:S(2)}) %collective-permute-start.17) | collective-permute-done | bytes 165920 | tf_op jit(solution)/shard_map/ppermute | solution.py:51
  98.0 3.5 %collective-permute-done.19 = f16[72,1152]{1,0:T(8,128)(2,1)S(1)} collective-permute-done((f16[72,1152]{1,0:T(8,128)(2,1)S(1)}, f16[72,1152]{1,0:T(8,128)(2,1)S(1)}, u32[]{:S(2)}, u32[]{:S(2)}) %collective-permute-start.19) | collective-permute-done | bytes 165920 | tf_op jit(solution)/shard_map/ppermute | solution.py:51
  101.5 1.3 %collective-permute-done.21 = f16[72,1152]{1,0:T(8,128)(2,1)S(1)} collective-permute-done((f16[72,1152]{1,0:T(8,128)(2,1)S(1)}, f16[72,1152]{1,0:T(8,128)(2,1)S(1)}, u32[]{:S(2)}, u32[]{:S(2)}) %collective-permute-start.21) | collective-permute-done | bytes 165920 | tf_op jit(solution)/shard_map/ppermute | solution.py:51
  103.9 3.7 %collective-permute-start.18 = (f16[72,1152]{1,0:T(8,128)(2,1)S(1)}, f16[72,1152]{1,0:T(8,128)(2,1)S(1)}, u32[]{:S(2)}, u32[]{:S(2)}) collective-permute-start(f16[72,1152]{1,0:T(8,128)(2,1)S(1)} %get-tuple-element.38), channel_id=1, source_target_pairs={{0,96},{1,97},{2,98},{3,99},{4,100},{5,101},{6,102},{7,103},{8,104... | collective-permute-start | bytes 497672 | tf_op jit(solution)/shard_map/ppermute | solution.py:51
  107.5 3.6 %collective-permute-start.20 = (f16[72,1152]{1,0:T(8,128)(2,1)S(1)}, f16[72,1152]{1,0:T(8,128)(2,1)S(1)}, u32[]{:S(2)}, u32[]{:S(2)}) collective-permute-start(f16[72,1152]{1,0:T(8,128)(2,1)S(1)} %get-tuple-element.39), channel_id=1, source_target_pairs={{0,16},{1,17},{2,18},{3,19},{4,20},{5,21},{6,22},{7,23},{8,24},{9,... | collective-permute-start | bytes 497672 | tf_op jit(solution)/shard_map/ppermute | solution.py:51
  111.2 1.4 %collective-permute-start.22 = (f16[72,1152]{1,0:T(8,128)(2,1)S(1)}, f16[72,1152]{1,0:T(8,128)(2,1)S(1)}, u32[]{:S(2)}, u32[]{:S(2)}) collective-permute-start(f16[72,1152]{1,0:T(8,128)(2,1)S(1)} %get-tuple-element.40), channel_id=1, source_target_pairs={{0,112},{1,113},{2,114},{3,115},{4,116},{5,117},{6,118},{7,119},{8... | collective-permute-start | bytes 497672 | tf_op jit(solution)/shard_map/ppermute | solution.py:51
  112.5 5.7 %collective-permute-done.20 = f16[72,1152]{1,0:T(8,128)(2,1)S(1)} collective-permute-done((f16[72,1152]{1,0:T(8,128)(2,1)S(1)}, f16[72,1152]{1,0:T(8,128)(2,1)S(1)}, u32[]{:S(2)}, u32[]{:S(2)}) %collective-permute-start.20) | collective-permute-done | bytes 165920 | tf_op jit(solution)/shard_map/ppermute | solution.py:51
  (54 shorter events, 8.6 us)
Async XLA Ops:
  0.6 0.9 copy-start
  1.5 1.7 %copy-start.2 = (bf16[64,1152]{1,0:T(8,128)(2,1)S(1)}, bf16[64,1152]{1,0:T(8,128)(2,1)}, u32[]{:S(2)}) copy-start(bf16[64,1152]{1,0:T(8,128)(2,1)} %rows_ref.6) | copy-start | bytes 442372
  3.4 13.4 %collective-permute-start.4 = (bf16[64,1152]{1,0:T(8,128)(2,1)S(1)}, bf16[64,1152]{1,0:T(8,128)(2,1)S(1)}, u32[]{:S(2)}, u32[]{:S(2)}) collective-permute-start(bf16[64,1152]{1,0:T(8,128)(2,1)S(1)} %shard_map.68), channel_id=1, source_target_pairs={{0,112},{1,113},{2,114},{3,115},{4,116},{5,117},{6,118},{7,119},{8... | collective-permute-start | bytes 442376 | tf_op jit(solution)/shard_map/ppermute | solution.py:51
  9.3 10.8 %collective-permute-start = (bf16[64,1152]{1,0:T(8,128)(2,1)S(1)}, bf16[64,1152]{1,0:T(8,128)(2,1)S(1)}, u32[]{:S(2)}, u32[]{:S(2)}) collective-permute-start(bf16[64,1152]{1,0:T(8,128)(2,1)S(1)} %shard_map.68), channel_id=1, source_target_pairs={{0,16},{1,17},{2,18},{3,19},{4,20},{5,21},{6,22},{7,23},{8,24},{9,... | collective-permute-start | bytes 442376 | tf_op jit(solution)/shard_map/ppermute | solution.py:51
  9.3 39.9 %all-to-all-start = ((bf16[16,64,1152]{2,1,0:T(8,128)(2,1)}), bf16[16,64,1152]{2,1,0:T(8,128)(2,1)}, u32[]{:S(2)}, u32[]{:S(2)}) async-start(bf16[16,64,1152]{2,1,0:T(8,128)(2,1)} %shard_map.67), calls=%async_computation | async-start | bytes 4718592 | tf_op jit(solution)/shard_map/all_to_all | solution.py:243
  16.8 6.0 %collective-permute-start.5 = (bf16[64,1152]{1,0:T(8,128)(2,1)S(1)}, bf16[64,1152]{1,0:T(8,128)(2,1)S(1)}, u32[]{:S(2)}, u32[]{:S(2)}) collective-permute-start(bf16[64,1152]{1,0:T(8,128)(2,1)S(1)} %collective-permute-done.4), channel_id=1, source_target_pairs={{0,112},{1,113},{2,114},{3,115},{4,116},{5,117},{6,118},{7,119},{8... | collective-permute-start | bytes 442376 | tf_op jit(solution)/shard_map/ppermute | solution.py:51
  20.2 6.4 %collective-permute-start.1 = (bf16[64,1152]{1,0:T(8,128)(2,1)S(1)}, bf16[64,1152]{1,0:T(8,128)(2,1)S(1)}, u32[]{:S(2)}, u32[]{:S(2)}) collective-permute-start(bf16[64,1152]{1,0:T(8,128)(2,1)S(1)} %collective-permute-done), channel_id=1, source_target_pairs={{0,16},{1,17},{2,18},{3,19},{4,20},{5,21},{6,22},{7,23},{8,24},{9,... | collective-permute-start | bytes 442376 | tf_op jit(solution)/shard_map/ppermute | solution.py:51
  22.8 16.4 %collective-permute-start.6 = (bf16[64,1152]{1,0:T(8,128)(2,1)S(1)}, bf16[64,1152]{1,0:T(8,128)(2,1)S(1)}, u32[]{:S(2)}, u32[]{:S(2)}) collective-permute-start(bf16[64,1152]{1,0:T(8,128)(2,1)S(1)} %collective-permute-done.5), channel_id=1, source_target_pairs={{0,112},{1,113},{2,114},{3,115},{4,116},{5,117},{6,118},{7,119},{8... | collective-permute-start | bytes 442376 | tf_op jit(solution)/shard_map/ppermute | solution.py:51
  26.5 6.4 %collective-permute-start.2 = (bf16[64,1152]{1,0:T(8,128)(2,1)S(1)}, bf16[64,1152]{1,0:T(8,128)(2,1)S(1)}, u32[]{:S(2)}, u32[]{:S(2)}) collective-permute-start(bf16[64,1152]{1,0:T(8,128)(2,1)S(1)} %collective-permute-done.1), channel_id=1, source_target_pairs={{0,16},{1,17},{2,18},{3,19},{4,20},{5,21},{6,22},{7,23},{8,24},{9,... | collective-permute-start | bytes 442376 | tf_op jit(solution)/shard_map/ppermute | solution.py:51
  32.9 6.4 %collective-permute-start.3 = (bf16[64,1152]{1,0:T(8,128)(2,1)S(1)}, bf16[64,1152]{1,0:T(8,128)(2,1)S(1)}, u32[]{:S(2)}, u32[]{:S(2)}) collective-permute-start(bf16[64,1152]{1,0:T(8,128)(2,1)S(1)} %collective-permute-done.2), channel_id=1, source_target_pairs={{0,16},{1,17},{2,18},{3,19},{4,20},{5,21},{6,22},{7,23},{8,24},{9,... | collective-permute-start | bytes 442376 | tf_op jit(solution)/shard_map/ppermute | solution.py:51
  39.3 2.9 %collective-permute-start.7 = (bf16[512,1152]{1,0:T(8,128)(2,1)S(1)}, bf16[512,1152]{1,0:T(8,128)(2,1)S(1)}, u32[]{:S(2)}, u32[]{:S(2)}) collective-permute-start(bf16[512,1152]{1,0:T(8,128)(2,1)S(1)} %constant_dynamic-update-slice_fusion.mine_ref), channel_id=1, source_target_pairs={{0,8},{1,9},{2,10},{3,11},{4,12},{5,13},{6,14},{7,15},{8,0},{9,1},... | collective-permute-start | bytes 3538952 | tf_op jit(solution)/shard_map/ppermute | solution.py:51
  56.8 9.5 %collective-permute-start.10 = (f32[3]{0:T(128)S(1)}, f32[3]{0:T(128)S(1)}, u32[]{:S(2)}, u32[]{:S(2)}) collective-permute-start(f32[3]{0:T(128)S(1)} %get-tuple-element.19), channel_id=1, source_target_pairs={{0,129},{1,0},{2,131},{3,2},{4,133},{5,4},{6,135},{7,6},{8,137},{9... | collective-permute-start | bytes 44 | tf_op jit(solution)/shard_map/ppermute | solution.py:69
  58.5 7.9 %collective-permute-start.9 = (f32[3]{0:T(128)S(1)}, f32[3]{0:T(128)S(1)}, u32[]{:S(2)}, u32[]{:S(2)}) collective-permute-start(f32[3]{0:T(128)S(1)} %get-tuple-element.19), channel_id=1, source_target_pairs={{0,128},{1,129},{2,130},{3,131},{4,132},{5,133},{6,134},{7,135},{8... | collective-permute-start | bytes 44 | tf_op jit(solution)/shard_map/ppermute | solution.py:69
  59.7 6.6 %collective-permute-start.8 = (f32[3]{0:T(128)S(1)}, f32[3]{0:T(128)S(1)}, u32[]{:S(2)}, u32[]{:S(2)}) collective-permute-start(f32[3]{0:T(128)S(1)} %get-tuple-element.19), channel_id=1, source_target_pairs={{0,1},{1,128},{2,3},{3,130},{4,5},{5,132},{6,7},{7,134},{8,9},{9,1... | collective-permute-start | bytes 44 | tf_op jit(solution)/shard_map/ppermute | solution.py:69
  66.3 8.1 %copy-start.3 = (f32[1024,1152]{1,0:T(8,128)}, f32[1024,1152]{1,0:T(8,128)S(1)}, u32[]{:S(2)}) copy-start(f32[1024,1152]{1,0:T(8,128)S(1)} %fusion.20) | copy-start | bytes 14155780
  66.3 11.4 %collective-permute-start.13 = (f32[3]{0:T(128)S(1)}, f32[3]{0:T(128)S(1)}, u32[]{:S(2)}, u32[]{:S(2)}) collective-permute-start(f32[3]{0:T(128)S(1)} %add_add_fusion.1), channel_id=1, source_target_pairs={{0,6},{1,7},{2,0},{3,1},{4,2},{5,3},{6,4},{7,5},{8,14},{9,15},{10,... | collective-permute-start | bytes 44 | tf_op jit(solution)/shard_map/ppermute | solution.py:69
  70.3 7.5 %collective-permute-start.12 = (f32[3]{0:T(128)S(1)}, f32[3]{0:T(128)S(1)}, u32[]{:S(2)}, u32[]{:S(2)}) collective-permute-start(f32[3]{0:T(128)S(1)} %add_add_fusion.1), channel_id=1, source_target_pairs={{0,4},{1,5},{2,6},{3,7},{4,0},{5,1},{6,2},{7,3},{8,12},{9,13},{10,... | collective-permute-start | bytes 44 | tf_op jit(solution)/shard_map/ppermute | solution.py:69
  70.3 7.5 %collective-permute-start.11 = (f32[3]{0:T(128)S(1)}, f32[3]{0:T(128)S(1)}, u32[]{:S(2)}, u32[]{:S(2)}) collective-permute-start(f32[3]{0:T(128)S(1)} %add_add_fusion.1), channel_id=1, source_target_pairs={{0,2},{1,3},{2,4},{3,5},{4,6},{5,7},{6,0},{7,1},{8,10},{9,11},{10,... | collective-permute-start | bytes 44 | tf_op jit(solution)/shard_map/ppermute | solution.py:69
  72.8 12.6 %collective-permute-start.14 = (f16[512,1152]{1,0:T(8,128)(2,1)}, f16[512,1152]{1,0:T(8,128)(2,1)}, u32[]{:S(2)}, u32[]{:S(2)}) collective-permute-start(f16[512,1152]{1,0:T(8,128)(2,1)} %multiply_convert_fusion.1), channel_id=1, source_target_pairs={{0,8},{1,9},{2,10},{3,11},{4,12},{5,13},{6,14},{7,15},{8,0},{9,1},... | collective-permute-start | bytes 3538952 | tf_op jit(solution)/shard_map/ppermute | solution.py:51
  77.7 43.6 %all-to-all-start.1 = ((f16[16,64,1152]{2,1,0:T(8,128)(2,1)}), f16[16,64,1152]{2,1,0:T(8,128)(2,1)S(1)}, u32[]{:S(2)}, u32[]{:S(2)}) async-start(f16[16,64,1152]{2,1,0:T(8,128)(2,1)} %bitcast.7), calls=%async_computation.1 | async-start | bytes 4718592 | tf_op jit(solution)/shard_map/all_to_all | solution.py:269
  84.1 1.2 collective-permute-start.15
  88.1 9.9 %collective-permute-start.17 = (f16[72,1152]{1,0:T(8,128)(2,1)S(1)}, f16[72,1152]{1,0:T(8,128)(2,1)S(1)}, u32[]{:S(2)}, u32[]{:S(2)}) collective-permute-start(f16[72,1152]{1,0:T(8,128)(2,1)S(1)} %get-tuple-element.41), channel_id=1, source_target_pairs={{0,96},{1,97},{2,98},{3,99},{4,100},{5,101},{6,102},{7,103},{8,104... | collective-permute-start | bytes 497672 | tf_op jit(solution)/shard_map/ppermute | solution.py:51
  90.0 11.5 %collective-permute-start.19 = (f16[72,1152]{1,0:T(8,128)(2,1)S(1)}, f16[72,1152]{1,0:T(8,128)(2,1)S(1)}, u32[]{:S(2)}, u32[]{:S(2)}) collective-permute-start(f16[72,1152]{1,0:T(8,128)(2,1)S(1)} %get-tuple-element.42), channel_id=1, source_target_pairs={{0,32},{1,33},{2,34},{3,35},{4,36},{5,37},{6,38},{7,39},{8,40},{9,... | collective-permute-start | bytes 497672 | tf_op jit(solution)/shard_map/ppermute | solution.py:51
  91.1 11.7 %collective-permute-start.21 = (f16[72,1152]{1,0:T(8,128)(2,1)S(1)}, f16[72,1152]{1,0:T(8,128)(2,1)S(1)}, u32[]{:S(2)}, u32[]{:S(2)}) collective-permute-start(f16[72,1152]{1,0:T(8,128)(2,1)S(1)} %get-tuple-element.43), channel_id=1, source_target_pairs={{0,96},{1,97},{2,98},{3,99},{4,100},{5,101},{6,102},{7,103},{8,104... | collective-permute-start | bytes 497672 | tf_op jit(solution)/shard_map/ppermute | solution.py:51
  103.3 9.2 %collective-permute-start.16 = (f16[72,1152]{1,0:T(8,128)(2,1)S(1)}, f16[72,1152]{1,0:T(8,128)(2,1)S(1)}, u32[]{:S(2)}, u32[]{:S(2)}) collective-permute-start(f16[72,1152]{1,0:T(8,128)(2,1)S(1)} %get-tuple-element.37), channel_id=1, source_target_pairs={{0,32},{1,33},{2,34},{3,35},{4,36},{5,37},{6,38},{7,39},{8,40},{9,... | collective-permute-start | bytes 497672 | tf_op jit(solution)/shard_map/ppermute | solution.py:51
  103.9 8.7 %collective-permute-start.18 = (f16[72,1152]{1,0:T(8,128)(2,1)S(1)}, f16[72,1152]{1,0:T(8,128)(2,1)S(1)}, u32[]{:S(2)}, u32[]{:S(2)}) collective-permute-start(f16[72,1152]{1,0:T(8,128)(2,1)S(1)} %get-tuple-element.38), channel_id=1, source_target_pairs={{0,96},{1,97},{2,98},{3,99},{4,100},{5,101},{6,102},{7,103},{8,104... | collective-permute-start | bytes 497672 | tf_op jit(solution)/shard_map/ppermute | solution.py:51
  107.5 10.8 %collective-permute-start.20 = (f16[72,1152]{1,0:T(8,128)(2,1)S(1)}, f16[72,1152]{1,0:T(8,128)(2,1)S(1)}, u32[]{:S(2)}, u32[]{:S(2)}) collective-permute-start(f16[72,1152]{1,0:T(8,128)(2,1)S(1)} %get-tuple-element.39), channel_id=1, source_target_pairs={{0,16},{1,17},{2,18},{3,19},{4,20},{5,21},{6,22},{7,23},{8,24},{9,... | collective-permute-start | bytes 497672 | tf_op jit(solution)/shard_map/ppermute | solution.py:51
  111.2 7.7 %collective-permute-start.22 = (f16[72,1152]{1,0:T(8,128)(2,1)S(1)}, f16[72,1152]{1,0:T(8,128)(2,1)S(1)}, u32[]{:S(2)}, u32[]{:S(2)}) collective-permute-start(f16[72,1152]{1,0:T(8,128)(2,1)S(1)} %get-tuple-element.40), channel_id=1, source_target_pairs={{0,112},{1,113},{2,114},{3,115},{4,116},{5,117},{6,118},{7,119},{8... | collective-permute-start | bytes 497672 | tf_op jit(solution)/shard_map/ppermute | solution.py:51
  119.1 3.0 %copy-start.1 = (bf16[64,1152]{1,0:T(8,128)(2,1)S(1)}, bf16[64,1152]{1,0:T(8,128)(2,1)}, u32[]{:S(2)}) copy-start(bf16[64,1152]{1,0:T(8,128)(2,1)} %rows_ref.5) | copy-start | bytes 442372

commit v6 on v5

--- a/solution.py
+++ b/solution.py
@@ -12,7 +12,7 @@
 PLANE = ("x_hi", "y", "x_lo")
 PEERS = 16
 DEPTH = 8
-CODE = 1024.0
+CODE = 512.0
 EXTRA = 8
 PAIRS = 1024.0 * 1024.0
 BF16 = jnp.bfloat16
@@ -230,7 +230,6 @@
         compiler_params=PARAMS,
         cost_estimate=cost(10**6, 3 * 2**20),
     )(images)
-    copies, texts_later = lax.optimization_barrier((copies, texts))
     txt_low = pl.pallas_call(
         low_kernel,
         in_specs=[VMEM],
@@ -238,7 +237,7 @@
         out_shape=jax.ShapeDtypeStruct((rows, emb), BF16),
         compiler_params=PARAMS,
         cost_estimate=cost(10**6, 2**19),
-    )(texts_later)
+    )(texts)
 
     imgs = lax.all_to_all(copies, PLANE, 0, 0).reshape(PEERS * rows, emb)
     up, down = [txt_low], []

time: 123 us -> 123 us (level)
  transfers between devices with their start and end apart: 25 -> 25, of which waited for: 12 -> 12; matrix products, arithmetic and copies ran while one was open for 12% -> 12% of each run, Pallas kernels for 1% -> 2%
where the time goes in v6:
time: 123 us
  starting transfers between devices  52.1 us (42%)
  waiting for transfers between devices  40.4 us (33%)
  Pallas kernels  11.3 us (9%)
  matrix products  9.48 us (8%)
  other arithmetic  5.41 us (4%)
  between operations  2.2 us (2%)
  local copies, waits for them, and re-layouts  1.99 us (2%)
    ppermute x16, waiting for transfers between devices, shifted(): return lax.ppermute(array, AXES, pairs)  31.8 us
    ppermute x16, starting transfers between devices, shifted(): return lax.ppermute(array, AXES, pairs)  28.4 us
    ppermute x6, starting transfers between devices, moved(): return lax.ppermute(array, AXES, pairs)  9.72 us
    pallas_call x1, Pallas kernels, pairs(): pl.pallas_call(pair_kernel, grid=(count // rows,), in_specs=[SMEM, SMEM,...  7.59 us
    all_to_all x1, starting transfers between devices, on_device(): imgs = lax.all_to_all(copies, PLANE, 0, 0).reshape(PEERS * rows, emb)  7.48 us
    all_to_all x1, waiting for transfers between devices, on_device(): imgs = lax.all_to_all(copies, PLANE, 0, 0).reshape(PEERS * rows, emb)  6.98 us
    all_to_all x1, starting transfers between devices, on_device(): img_recv = lax.all_to_all(img_part, PLANE, 0, 0)  6.36 us
    dot_general x1, matrix products, on_device(): lax.dot_general(grad_low, imgs, (((0,), (0,)), ((), ())), preferred_eleme...  4.59 us
  transfers between devices with their start and end apart: 25, of which 12 were waited for; matrix products, arithmetic and copies ran while one was open for 12% of the time, Pallas kernels for 2%

profile of v6, /device:TPU:2, one launch (start us, length us, event | category | flops | bytes accessed | tf_op | source)
XLA Modules:
  0.0 122.9 jit_solution(16437276087629388553)
XLA Ops:
  1.7 5.9 %collective-permute-start.4 = (bf16[64,1152]{1,0:T(8,128)(2,1)S(1)}, bf16[64,1152]{1,0:T(8,128)(2,1)S(1)}, u32[]{:S(2)}, u32[]{:S(2)}) collective-permute-start(bf16[64,1152]{1,0:T(8,128)(2,1)S(1)} %shard_map.68), channel_id=1, source_target_pairs={{0,112},{1,113},{2,114},{3,115},{4,116},{5,117},{6,118},{7,119},{8... | collective-permute-start | bytes 442376 | tf_op jit(solution)/shard_map/ppermute | solution.py:51
  8.5 1.7 %shard_map.67 = bf16[16,64,1152]{2,1,0:T(8,128)(2,1)} custom-call(bf16[64,1152]{1,0:T(8,128)(2,1)S(1)} %copy-done), custom_call_target="tpu_custom_call" | custom-call | flops 1000000 | bytes 3145728 | tf_op jit(solution)/shard_map/pallas_call | solution.py:225
  10.3 7.5 %all-to-all-start = ((bf16[16,64,1152]{2,1,0:T(8,128)(2,1)}), bf16[16,64,1152]{2,1,0:T(8,128)(2,1)}, u32[]{:S(2)}, u32[]{:S(2)}) async-start(bf16[16,64,1152]{2,1,0:T(8,128)(2,1)} %shard_map.67), calls=%async_computation | async-start | bytes 4718592 | tf_op jit(solution)/shard_map/all_to_all | solution.py:242
  17.8 3.3 %collective-permute-start.5 = (bf16[64,1152]{1,0:T(8,128)(2,1)S(1)}, bf16[64,1152]{1,0:T(8,128)(2,1)S(1)}, u32[]{:S(2)}, u32[]{:S(2)}) collective-permute-start(bf16[64,1152]{1,0:T(8,128)(2,1)S(1)} %collective-permute-done.4), channel_id=1, source_target_pairs={{0,112},{1,113},{2,114},{3,115},{4,116},{5,117},{6,118},{7,119},{8... | collective-permute-start | bytes 442376 | tf_op jit(solution)/shard_map/ppermute | solution.py:51
  21.1 2.6 %collective-permute-done.5 = bf16[64,1152]{1,0:T(8,128)(2,1)S(1)} collective-permute-done((bf16[64,1152]{1,0:T(8,128)(2,1)S(1)}, bf16[64,1152]{1,0:T(8,128)(2,1)S(1)}, u32[]{:S(2)}, u32[]{:S(2)}) %collective-permute-start.5) | collective-permute-done | bytes 147488 | tf_op jit(solution)/shard_map/ppermute | solution.py:51
  23.7 3.7 %collective-permute-start.6 = (bf16[64,1152]{1,0:T(8,128)(2,1)S(1)}, bf16[64,1152]{1,0:T(8,128)(2,1)S(1)}, u32[]{:S(2)}, u32[]{:S(2)}) collective-permute-start(bf16[64,1152]{1,0:T(8,128)(2,1)S(1)} %collective-permute-done.5), channel_id=1, source_target_pairs={{0,112},{1,113},{2,114},{3,115},{4,116},{5,117},{6,118},{7,119},{8... | collective-permute-start | bytes 442376 | tf_op jit(solution)/shard_map/ppermute | solution.py:51
  27.5 6.3 %collective-permute-done.2 = bf16[64,1152]{1,0:T(8,128)(2,1)S(1)} collective-permute-done((bf16[64,1152]{1,0:T(8,128)(2,1)S(1)}, bf16[64,1152]{1,0:T(8,128)(2,1)S(1)}, u32[]{:S(2)}, u32[]{:S(2)}) %collective-permute-start.2) | collective-permute-done | bytes 147488 | tf_op jit(solution)/shard_map/ppermute | solution.py:51
  33.8 6.3 %collective-permute-done.3 = bf16[64,1152]{1,0:T(8,128)(2,1)S(1)} collective-permute-done((bf16[64,1152]{1,0:T(8,128)(2,1)S(1)}, bf16[64,1152]{1,0:T(8,128)(2,1)S(1)}, u32[]{:S(2)}, u32[]{:S(2)}) %collective-permute-start.3) | collective-permute-done | bytes 147488 | tf_op jit(solution)/shard_map/ppermute | solution.py:51
  41.7 1.5 %collective-permute-done.7.theirs_ref = bf16[512,1152]{1,0:T(8,128)(2,1)S(1)} collective-permute-done((bf16[512,1152]{1,0:T(8,128)(2,1)S(1)}, bf16[512,1152]{1,0:T(8,128)(2,1)S(1)}, u32[]{:S(2)}, u32[]{:S(2)}) %collective-permute-start.7) | collective-permute-done | bytes 1179680 | tf_op jit(solution)/shard_map/ppermute | solution.py:51
  43.2 7.0 %all-to-all-done = bf16[16,64,1152]{2,1,0:T(8,128)(2,1)} async-done(((bf16[16,64,1152]{2,1,0:T(8,128)(2,1)}), bf16[16,64,1152]{2,1,0:T(8,128)(2,1)}, u32[]{:S(2)}, u32[]{:S(2)}) %all-to-all-start) | async-done | bytes 2359328 | tf_op jit(solution)/shard_map/all_to_all | solution.py:242
  50.2 7.6 %shard_map.69 = (bf16[1024,1024]{1,0:T(8,128)(2,1)S(1)}, f32[3]{0:T(128)S(1)}) custom-call(s32[1]{0:T(128)} %bitcast.first_ref, f32[1]{0:T(128)S(6)} %exp.3.scale_ref, f32[1]{0:T(128)S(6)} %copy.15.shift_ref, bf16[1024,1152]{1,0:T(8,128)(2,1)} %bitcast.1.img_ref, bf16[512,1152]{1,0:T(8,128)(2,1)S(1)} %constant_dynamic-update-slice_fusion.mine_ref, ...), custom_call_target="tpu_custom_call" | custom-call | flops 2415919104 | bytes 8388608 | tf_op jit(solution)/shard_map/pallas_call | solution.py:176
  57.8 1.6 %collective-permute-start.10 = (f32[3]{0:T(128)S(1)}, f32[3]{0:T(128)S(1)}, u32[]{:S(2)}, u32[]{:S(2)}) collective-permute-start(f32[3]{0:T(128)S(1)} %get-tuple-element.15), channel_id=1, source_target_pairs={{0,129},{1,0},{2,131},{3,2},{4,133},{5,4},{6,135},{7,6},{8,137},{9... | collective-permute-start | bytes 44 | tf_op jit(solution)/shard_map/ppermute | solution.py:69
  59.4 1.3 %collective-permute-start.9 = (f32[3]{0:T(128)S(1)}, f32[3]{0:T(128)S(1)}, u32[]{:S(2)}, u32[]{:S(2)}) collective-permute-start(f32[3]{0:T(128)S(1)} %get-tuple-element.15), channel_id=1, source_target_pairs={{0,128},{1,129},{2,130},{3,131},{4,132},{5,133},{6,134},{7,135},{8... | collective-permute-start | bytes 44 | tf_op jit(solution)/shard_map/ppermute | solution.py:69
  60.6 2.0 %collective-permute-start.8 = (f32[3]{0:T(128)S(1)}, f32[3]{0:T(128)S(1)}, u32[]{:S(2)}, u32[]{:S(2)}) collective-permute-start(f32[3]{0:T(128)S(1)} %get-tuple-element.15), channel_id=1, source_target_pairs={{0,1},{1,128},{2,3},{3,130},{4,5},{5,132},{6,7},{7,134},{8,9},{9,1... | collective-permute-start | bytes 44 | tf_op jit(solution)/shard_map/ppermute | solution.py:69
  62.6 4.6 %fusion.20 = f32[1024,1152]{1,0:T(8,128)S(1)} fusion(bf16[1024,1024]{1,0:T(8,128)(2,1)S(1)} %get-tuple-element.16, bf16[1024,1152]{1,0:T(8,128)(2,1)} %bitcast.1.img_ref), kind=kOutput, calls=%fused_computation.63 | convolution fusion | flops 2415919104 | bytes 9175040 | tf_op jit(solution)/shard_map/dot_general | solution.py:256
  67.3 3.9 %collective-permute-start.13 = (f32[3]{0:T(128)S(1)}, f32[3]{0:T(128)S(1)}, u32[]{:S(2)}, u32[]{:S(2)}) collective-permute-start(f32[3]{0:T(128)S(1)} %add_add_fusion.1), channel_id=1, source_target_pairs={{0,6},{1,7},{2,0},{3,1},{4,2},{5,3},{6,4},{7,5},{8,14},{9,15},{10,... | collective-permute-start | bytes 44 | tf_op jit(solution)/shard_map/ppermute | solution.py:69
  71.2 1.0 collective-permute-start.11
  72.8 1.5 %fusion.1 = f32[1024,1152]{1,0:T(8,128)S(1)} fusion(bf16[512,1152]{1,0:T(8,128)(2,1)S(1)} %collective-permute-done.7.theirs_ref, bf16[1024,1024]{1,0:T(8,128)(2,1)S(1)} %get-tuple-element.16), kind=kOutput, calls=%fused_computation.5 | convolution fusion | flops 1207959552 | bytes 6946816 | tf_op jit(solution)/shard_map/dot_general | solution.py:263
  74.3 3.4 %multiply_convert_fusion = f16[1024,1152]{1,0:T(8,128)(2,1)} fusion(f32[1024,1152]{1,0:T(8,128)S(1)} %fusion.1, bf16[512,1152]{1,0:T(8,128)(2,1)S(1)} %constant_dynamic-update-slice_fusion.mine_ref, bf16[1024,1024]{1,0:T(8,128)(2,1)S(1)} %get-tuple-element.16), kind=kOutput, calls=%fused_computation.3 | convolution fusion | flops 1215037440 | bytes 9306112 | tf_op jit(solution)/shard_map/dot_general | solution.py:263
  77.7 6.4 %all-to-all-start.1 = ((f16[16,64,1152]{2,1,0:T(8,128)(2,1)}), f16[16,64,1152]{2,1,0:T(8,128)(2,1)S(1)}, u32[]{:S(2)}, u32[]{:S(2)}) async-start(f16[16,64,1152]{2,1,0:T(8,128)(2,1)} %bitcast.7), calls=%async_computation.1 | async-start | bytes 4718592 | tf_op jit(solution)/shard_map/all_to_all | solution.py:268
  84.1 1.1 collective-permute-done.15
  85.3 2.3 %fusion.12 = (f32[64,1152]{1,0:T(8,128)S(1)}, f32[64,1152]{1,0:T(8,128)S(1)}, f32[64,1152]{1,0:T(8,128)S(1)}, f32[64,1152]{1,0:T(8,128)S(1)}, f32[64,1152]{1,0:T...) fusion(f32[1024,1152]{1,0:T(8,128)} %copy-done.4, ...), kind=kLoop, calls=%fused_computation.42 | loop fusion | flops 2949120 | bytes 5898240 | tf_op jit(solution)/shard_map/add | solution.py:275
  88.0 2.0 %collective-permute-start.17 = (f16[72,1152]{1,0:T(8,128)(2,1)S(1)}, f16[72,1152]{1,0:T(8,128)(2,1)S(1)}, u32[]{:S(2)}, u32[]{:S(2)}) collective-permute-start(f16[72,1152]{1,0:T(8,128)(2,1)S(1)} %get-tuple-element.37), channel_id=1, source_target_pairs={{0,96},{1,97},{2,98},{3,99},{4,100},{5,101},{6,102},{7,103},{8,104... | collective-permute-start | bytes 497672 | tf_op jit(solution)/shard_map/ppermute | solution.py:51
  89.9 1.0 collective-permute-start.19
  91.0 3.1 %collective-permute-start.21 = (f16[72,1152]{1,0:T(8,128)(2,1)S(1)}, f16[72,1152]{1,0:T(8,128)(2,1)S(1)}, u32[]{:S(2)}, u32[]{:S(2)}) collective-permute-start(f16[72,1152]{1,0:T(8,128)(2,1)S(1)} %get-tuple-element.39), channel_id=1, source_target_pairs={{0,96},{1,97},{2,98},{3,99},{4,100},{5,101},{6,102},{7,103},{8,104... | collective-permute-start | bytes 497672 | tf_op jit(solution)/shard_map/ppermute | solution.py:51
  94.1 3.8 %collective-permute-done.17 = f16[72,1152]{1,0:T(8,128)(2,1)S(1)} collective-permute-done((f16[72,1152]{1,0:T(8,128)(2,1)S(1)}, f16[72,1152]{1,0:T(8,128)(2,1)S(1)}, u32[]{:S(2)}, u32[]{:S(2)}) %collective-permute-start.17) | collective-permute-done | bytes 165920 | tf_op jit(solution)/shard_map/ppermute | solution.py:51
  97.9 3.5 %collective-permute-done.19 = f16[72,1152]{1,0:T(8,128)(2,1)S(1)} collective-permute-done((f16[72,1152]{1,0:T(8,128)(2,1)S(1)}, f16[72,1152]{1,0:T(8,128)(2,1)S(1)}, u32[]{:S(2)}, u32[]{:S(2)}) %collective-permute-start.19) | collective-permute-done | bytes 165920 | tf_op jit(solution)/shard_map/ppermute | solution.py:51
  101.4 1.3 %collective-permute-done.21 = f16[72,1152]{1,0:T(8,128)(2,1)S(1)} collective-permute-done((f16[72,1152]{1,0:T(8,128)(2,1)S(1)}, f16[72,1152]{1,0:T(8,128)(2,1)S(1)}, u32[]{:S(2)}, u32[]{:S(2)}) %collective-permute-start.21) | collective-permute-done | bytes 165920 | tf_op jit(solution)/shard_map/ppermute | solution.py:51
  103.8 3.7 %collective-permute-start.18 = (f16[72,1152]{1,0:T(8,128)(2,1)S(1)}, f16[72,1152]{1,0:T(8,128)(2,1)S(1)}, u32[]{:S(2)}, u32[]{:S(2)}) collective-permute-start(f16[72,1152]{1,0:T(8,128)(2,1)S(1)} %get-tuple-element.34), channel_id=1, source_target_pairs={{0,96},{1,97},{2,98},{3,99},{4,100},{5,101},{6,102},{7,103},{8,104... | collective-permute-start | bytes 497672 | tf_op jit(solution)/shard_map/ppermute | solution.py:51
  107.5 3.6 %collective-permute-start.20 = (f16[72,1152]{1,0:T(8,128)(2,1)S(1)}, f16[72,1152]{1,0:T(8,128)(2,1)S(1)}, u32[]{:S(2)}, u32[]{:S(2)}) collective-permute-start(f16[72,1152]{1,0:T(8,128)(2,1)S(1)} %get-tuple-element.35), channel_id=1, source_target_pairs={{0,16},{1,17},{2,18},{3,19},{4,20},{5,21},{6,22},{7,23},{8,24},{9,... | collective-permute-start | bytes 497672 | tf_op jit(solution)/shard_map/ppermute | solution.py:51
  111.1 1.4 %collective-permute-start.22 = (f16[72,1152]{1,0:T(8,128)(2,1)S(1)}, f16[72,1152]{1,0:T(8,128)(2,1)S(1)}, u32[]{:S(2)}, u32[]{:S(2)}) collective-permute-start(f16[72,1152]{1,0:T(8,128)(2,1)S(1)} %get-tuple-element.36), channel_id=1, source_target_pairs={{0,112},{1,113},{2,114},{3,115},{4,116},{5,117},{6,118},{7,119},{8... | collective-permute-start | bytes 497672 | tf_op jit(solution)/shard_map/ppermute | solution.py:51
  112.5 5.7 %collective-permute-done.20 = f16[72,1152]{1,0:T(8,128)(2,1)S(1)} collective-permute-done((f16[72,1152]{1,0:T(8,128)(2,1)S(1)}, f16[72,1152]{1,0:T(8,128)(2,1)S(1)}, u32[]{:S(2)}, u32[]{:S(2)}) %collective-permute-start.20) | collective-permute-done | bytes 165920 | tf_op jit(solution)/shard_map/ppermute | solution.py:51
  (56 shorter events, 9.0 us)
Async XLA Ops:
  0.6 0.9 copy-start.2
  1.7 16.1 %collective-permute-start.4 = (bf16[64,1152]{1,0:T(8,128)(2,1)S(1)}, bf16[64,1152]{1,0:T(8,128)(2,1)S(1)}, u32[]{:S(2)}, u32[]{:S(2)}) collective-permute-start(bf16[64,1152]{1,0:T(8,128)(2,1)S(1)} %shard_map.68), channel_id=1, source_target_pairs={{0,112},{1,113},{2,114},{3,115},{4,116},{5,117},{6,118},{7,119},{8... | collective-permute-start | bytes 442376 | tf_op jit(solution)/shard_map/ppermute | solution.py:51
  7.6 13.5 %collective-permute-start = (bf16[64,1152]{1,0:T(8,128)(2,1)S(1)}, bf16[64,1152]{1,0:T(8,128)(2,1)S(1)}, u32[]{:S(2)}, u32[]{:S(2)}) collective-permute-start(bf16[64,1152]{1,0:T(8,128)(2,1)S(1)} %shard_map.68), channel_id=1, source_target_pairs={{0,16},{1,17},{2,18},{3,19},{4,20},{5,21},{6,22},{7,23},{8,24},{9,... | collective-permute-start | bytes 442376 | tf_op jit(solution)/shard_map/ppermute | solution.py:51
  7.6 0.9 copy-start
  10.3 39.9 %all-to-all-start = ((bf16[16,64,1152]{2,1,0:T(8,128)(2,1)}), bf16[16,64,1152]{2,1,0:T(8,128)(2,1)}, u32[]{:S(2)}, u32[]{:S(2)}) async-start(bf16[16,64,1152]{2,1,0:T(8,128)(2,1)} %shard_map.67), calls=%async_computation | async-start | bytes 4718592 | tf_op jit(solution)/shard_map/all_to_all | solution.py:242
  17.8 6.0 %collective-permute-start.5 = (bf16[64,1152]{1,0:T(8,128)(2,1)S(1)}, bf16[64,1152]{1,0:T(8,128)(2,1)S(1)}, u32[]{:S(2)}, u32[]{:S(2)}) collective-permute-start(bf16[64,1152]{1,0:T(8,128)(2,1)S(1)} %collective-permute-done.4), channel_id=1, source_target_pairs={{0,112},{1,113},{2,114},{3,115},{4,116},{5,117},{6,118},{7,119},{8... | collective-permute-start | bytes 442376 | tf_op jit(solution)/shard_map/ppermute | solution.py:51
  21.1 6.4 %collective-permute-start.1 = (bf16[64,1152]{1,0:T(8,128)(2,1)S(1)}, bf16[64,1152]{1,0:T(8,128)(2,1)S(1)}, u32[]{:S(2)}, u32[]{:S(2)}) collective-permute-start(bf16[64,1152]{1,0:T(8,128)(2,1)S(1)} %collective-permute-done), channel_id=1, source_target_pairs={{0,16},{1,17},{2,18},{3,19},{4,20},{5,21},{6,22},{7,23},{8,24},{9,... | collective-permute-start | bytes 442376 | tf_op jit(solution)/shard_map/ppermute | solution.py:51
  23.7 16.4 %collective-permute-start.6 = (bf16[64,1152]{1,0:T(8,128)(2,1)S(1)}, bf16[64,1152]{1,0:T(8,128)(2,1)S(1)}, u32[]{:S(2)}, u32[]{:S(2)}) collective-permute-start(bf16[64,1152]{1,0:T(8,128)(2,1)S(1)} %collective-permute-done.5), channel_id=1, source_target_pairs={{0,112},{1,113},{2,114},{3,115},{4,116},{5,117},{6,118},{7,119},{8... | collective-permute-start | bytes 442376 | tf_op jit(solution)/shard_map/ppermute | solution.py:51
  27.4 6.4 %collective-permute-start.2 = (bf16[64,1152]{1,0:T(8,128)(2,1)S(1)}, bf16[64,1152]{1,0:T(8,128)(2,1)S(1)}, u32[]{:S(2)}, u32[]{:S(2)}) collective-permute-start(bf16[64,1152]{1,0:T(8,128)(2,1)S(1)} %collective-permute-done.1), channel_id=1, source_target_pairs={{0,16},{1,17},{2,18},{3,19},{4,20},{5,21},{6,22},{7,23},{8,24},{9,... | collective-permute-start | bytes 442376 | tf_op jit(solution)/shard_map/ppermute | solution.py:51
  33.8 6.4 %collective-permute-start.3 = (bf16[64,1152]{1,0:T(8,128)(2,1)S(1)}, bf16[64,1152]{1,0:T(8,128)(2,1)S(1)}, u32[]{:S(2)}, u32[]{:S(2)}) collective-permute-start(bf16[64,1152]{1,0:T(8,128)(2,1)S(1)} %collective-permute-done.2), channel_id=1, source_target_pairs={{0,16},{1,17},{2,18},{3,19},{4,20},{5,21},{6,22},{7,23},{8,24},{9,... | collective-permute-start | bytes 442376 | tf_op jit(solution)/shard_map/ppermute | solution.py:51
  40.2 2.9 %collective-permute-start.7 = (bf16[512,1152]{1,0:T(8,128)(2,1)S(1)}, bf16[512,1152]{1,0:T(8,128)(2,1)S(1)}, u32[]{:S(2)}, u32[]{:S(2)}) collective-permute-start(bf16[512,1152]{1,0:T(8,128)(2,1)S(1)} %constant_dynamic-update-slice_fusion.mine_ref), channel_id=1, source_target_pairs={{0,8},{1,9},{2,10},{3,11},{4,12},{5,13},{6,14},{7,15},{8,0},{9,1},... | collective-permute-start | bytes 3538952 | tf_op jit(solution)/shard_map/ppermute | solution.py:51
  57.8 9.5 %collective-permute-start.10 = (f32[3]{0:T(128)S(1)}, f32[3]{0:T(128)S(1)}, u32[]{:S(2)}, u32[]{:S(2)}) collective-permute-start(f32[3]{0:T(128)S(1)} %get-tuple-element.15), channel_id=1, source_target_pairs={{0,129},{1,0},{2,131},{3,2},{4,133},{5,4},{6,135},{7,6},{8,137},{9... | collective-permute-start | bytes 44 | tf_op jit(solution)/shard_map/ppermute | solution.py:69
  59.4 7.9 %collective-permute-start.9 = (f32[3]{0:T(128)S(1)}, f32[3]{0:T(128)S(1)}, u32[]{:S(2)}, u32[]{:S(2)}) collective-permute-start(f32[3]{0:T(128)S(1)} %get-tuple-element.15), channel_id=1, source_target_pairs={{0,128},{1,129},{2,130},{3,131},{4,132},{5,133},{6,134},{7,135},{8... | collective-permute-start | bytes 44 | tf_op jit(solution)/shard_map/ppermute | solution.py:69
  60.6 6.6 %collective-permute-start.8 = (f32[3]{0:T(128)S(1)}, f32[3]{0:T(128)S(1)}, u32[]{:S(2)}, u32[]{:S(2)}) collective-permute-start(f32[3]{0:T(128)S(1)} %get-tuple-element.15), channel_id=1, source_target_pairs={{0,1},{1,128},{2,3},{3,130},{4,5},{5,132},{6,7},{7,134},{8,9},{9,1... | collective-permute-start | bytes 44 | tf_op jit(solution)/shard_map/ppermute | solution.py:69
  67.2 7.1 %copy-start.4 = (f32[1024,1152]{1,0:T(8,128)}, f32[1024,1152]{1,0:T(8,128)S(1)}, u32[]{:S(2)}) copy-start(f32[1024,1152]{1,0:T(8,128)S(1)} %fusion.20) | copy-start | bytes 14155780
  67.3 10.4 %collective-permute-start.13 = (f32[3]{0:T(128)S(1)}, f32[3]{0:T(128)S(1)}, u32[]{:S(2)}, u32[]{:S(2)}) collective-permute-start(f32[3]{0:T(128)S(1)} %add_add_fusion.1), channel_id=1, source_target_pairs={{0,6},{1,7},{2,0},{3,1},{4,2},{5,3},{6,4},{7,5},{8,14},{9,15},{10,... | collective-permute-start | bytes 44 | tf_op jit(solution)/shard_map/ppermute | solution.py:69
  71.2 6.5 %collective-permute-start.12 = (f32[3]{0:T(128)S(1)}, f32[3]{0:T(128)S(1)}, u32[]{:S(2)}, u32[]{:S(2)}) collective-permute-start(f32[3]{0:T(128)S(1)} %add_add_fusion.1), channel_id=1, source_target_pairs={{0,4},{1,5},{2,6},{3,7},{4,0},{5,1},{6,2},{7,3},{8,12},{9,13},{10,... | collective-permute-start | bytes 44 | tf_op jit(solution)/shard_map/ppermute | solution.py:69
  71.2 6.5 %collective-permute-start.11 = (f32[3]{0:T(128)S(1)}, f32[3]{0:T(128)S(1)}, u32[]{:S(2)}, u32[]{:S(2)}) collective-permute-start(f32[3]{0:T(128)S(1)} %add_add_fusion.1), channel_id=1, source_target_pairs={{0,2},{1,3},{2,4},{3,5},{4,6},{5,7},{6,0},{7,1},{8,10},{9,11},{10,... | collective-permute-start | bytes 44 | tf_op jit(solution)/shard_map/ppermute | solution.py:69
  72.7 12.7 %collective-permute-start.14 = (f16[512,1152]{1,0:T(8,128)(2,1)S(1)}, f16[512,1152]{1,0:T(8,128)(2,1)}, u32[]{:S(2)}, u32[]{:S(2)}) collective-permute-start(f16[512,1152]{1,0:T(8,128)(2,1)S(1)} %multiply_convert_fusion.1), channel_id=1, source_target_pairs={{0,8},{1,9},{2,10},{3,11},{4,12},{5,13},{6,14},{7,15},{8,0},{9,1},... | collective-permute-start | bytes 3538952 | tf_op jit(solution)/shard_map/ppermute | solution.py:51
  77.7 43.5 %all-to-all-start.1 = ((f16[16,64,1152]{2,1,0:T(8,128)(2,1)}), f16[16,64,1152]{2,1,0:T(8,128)(2,1)S(1)}, u32[]{:S(2)}, u32[]{:S(2)}) async-start(f16[16,64,1152]{2,1,0:T(8,128)(2,1)} %bitcast.7), calls=%async_computation.1 | async-start | bytes 4718592 | tf_op jit(solution)/shard_map/all_to_all | solution.py:268
  84.0 1.2 collective-permute-start.15
  88.0 9.9 %collective-permute-start.17 = (f16[72,1152]{1,0:T(8,128)(2,1)S(1)}, f16[72,1152]{1,0:T(8,128)(2,1)S(1)}, u32[]{:S(2)}, u32[]{:S(2)}) collective-permute-start(f16[72,1152]{1,0:T(8,128)(2,1)S(1)} %get-tuple-element.37), channel_id=1, source_target_pairs={{0,96},{1,97},{2,98},{3,99},{4,100},{5,101},{6,102},{7,103},{8,104... | collective-permute-start | bytes 497672 | tf_op jit(solution)/shard_map/ppermute | solution.py:51
  89.9 11.5 %collective-permute-start.19 = (f16[72,1152]{1,0:T(8,128)(2,1)S(1)}, f16[72,1152]{1,0:T(8,128)(2,1)S(1)}, u32[]{:S(2)}, u32[]{:S(2)}) collective-permute-start(f16[72,1152]{1,0:T(8,128)(2,1)S(1)} %get-tuple-element.38), channel_id=1, source_target_pairs={{0,32},{1,33},{2,34},{3,35},{4,36},{5,37},{6,38},{7,39},{8,40},{9,... | collective-permute-start | bytes 497672 | tf_op jit(solution)/shard_map/ppermute | solution.py:51
  91.0 11.7 %collective-permute-start.21 = (f16[72,1152]{1,0:T(8,128)(2,1)S(1)}, f16[72,1152]{1,0:T(8,128)(2,1)S(1)}, u32[]{:S(2)}, u32[]{:S(2)}) collective-permute-start(f16[72,1152]{1,0:T(8,128)(2,1)S(1)} %get-tuple-element.39), channel_id=1, source_target_pairs={{0,96},{1,97},{2,98},{3,99},{4,100},{5,101},{6,102},{7,103},{8,104... | collective-permute-start | bytes 497672 | tf_op jit(solution)/shard_map/ppermute | solution.py:51
  102.7 16.4 %copy-start.3 = (bf16[64,1152]{1,0:T(8,128)(2,1)S(1)}, bf16[64,1152]{1,0:T(8,128)(2,1)}, u32[]{:S(2)}) copy-start(bf16[64,1152]{1,0:T(8,128)(2,1)} %rows_ref.7) | copy-start | bytes 442372
  103.2 9.2 %collective-permute-start.16 = (f16[72,1152]{1,0:T(8,128)(2,1)S(1)}, f16[72,1152]{1,0:T(8,128)(2,1)S(1)}, u32[]{:S(2)}, u32[]{:S(2)}) collective-permute-start(f16[72,1152]{1,0:T(8,128)(2,1)S(1)} %get-tuple-element.33), channel_id=1, source_target_pairs={{0,32},{1,33},{2,34},{3,35},{4,36},{5,37},{6,38},{7,39},{8,40},{9,... | collective-permute-start | bytes 497672 | tf_op jit(solution)/shard_map/ppermute | solution.py:51
  103.8 8.7 %collective-permute-start.18 = (f16[72,1152]{1,0:T(8,128)(2,1)S(1)}, f16[72,1152]{1,0:T(8,128)(2,1)S(1)}, u32[]{:S(2)}, u32[]{:S(2)}) collective-permute-start(f16[72,1152]{1,0:T(8,128)(2,1)S(1)} %get-tuple-element.34), channel_id=1, source_target_pairs={{0,96},{1,97},{2,98},{3,99},{4,100},{5,101},{6,102},{7,103},{8,104... | collective-permute-start | bytes 497672 | tf_op jit(solution)/shard_map/ppermute | solution.py:51
  107.5 10.8 %collective-permute-start.20 = (f16[72,1152]{1,0:T(8,128)(2,1)S(1)}, f16[72,1152]{1,0:T(8,128)(2,1)S(1)}, u32[]{:S(2)}, u32[]{:S(2)}) collective-permute-start(f16[72,1152]{1,0:T(8,128)(2,1)S(1)} %get-tuple-element.35), channel_id=1, source_target_pairs={{0,16},{1,17},{2,18},{3,19},{4,20},{5,21},{6,22},{7,23},{8,24},{9,... | collective-permute-start | bytes 497672 | tf_op jit(solution)/shard_map/ppermute | solution.py:51
  111.1 7.7 %collective-permute-start.22 = (f16[72,1152]{1,0:T(8,128)(2,1)S(1)}, f16[72,1152]{1,0:T(8,128)(2,1)S(1)}, u32[]{:S(2)}, u32[]{:S(2)}) collective-permute-start(f16[72,1152]{1,0:T(8,128)(2,1)S(1)} %get-tuple-element.36), channel_id=1, source_target_pairs={{0,112},{1,113},{2,114},{3,115},{4,116},{5,117},{6,118},{7,119},{8... | collective-permute-start | bytes 497672 | tf_op jit(solution)/shard_map/ppermute | solution.py:51
  119.1 2.9 %copy-start.1 = (bf16[64,1152]{1,0:T(8,128)(2,1)S(1)}, bf16[64,1152]{1,0:T(8,128)(2,1)}, u32[]{:S(2)}) copy-start(bf16[64,1152]{1,0:T(8,128)(2,1)} %rows_ref.6) | copy-start | bytes 442372

commit v7 on v6

--- a/solution.py
+++ b/solution.py
@@ -169,9 +169,9 @@
             sums_ref[k] = jnp.sum(acc_ref[k])
 
 
-def pairs(first, scale, shift, imgs, mine, theirs):
+def pairs(first, scale, shift, imgs, txts):
     count, emb = imgs.shape
-    half = mine.shape[0]
+    half = txts.shape[0] // 2
     rows = 256
     return pl.pallas_call(
         pair_kernel,
@@ -182,7 +182,7 @@
             SMEM,
             pl.BlockSpec((rows, emb), lambda i: (i, 0)),
             pl.BlockSpec((half, emb), lambda i: (0, 0)),
-            pl.BlockSpec((half, emb), lambda i: (0, 0)),
+            pl.BlockSpec((half, emb), lambda i: (1, 0)),
         ],
         out_specs=[
             pl.BlockSpec((rows, 2 * half), lambda i: (i, 0)),
@@ -195,7 +195,7 @@
         scratch_shapes=[pltpu.VMEM((3, 8, 128), F32)],
         compiler_params=PARAMS,
         cost_estimate=cost(2 * count * 2 * half * emb, 8 * 2**20),
-    )(first, scale, shift, imgs, mine, theirs)
+    )(first, scale, shift, imgs, txts, txts)
 
 
 def project_kernel(scale_ref, rows_ref, total_ref, out_ref):
@@ -249,7 +249,8 @@
     mine = jnp.concatenate(up + down[::-1], axis=0)
     theirs = other_core(mine)
 
-    grad_low, sums = pairs(first, scale, bias, imgs, mine, theirs)
+    txts = jnp.concatenate([mine, theirs], axis=0)
+    grad_low, sums = pairs(first, scale, bias, imgs, txts)
     half = DEPTH * rows
 
     arrived = [moved(sums, by, 0) for by in (1, 2, 3)]
@@ -260,9 +261,7 @@
     sums = sums + arrived[0] + arrived[1] + arrived[2]
 
     arrived = [moved(sums, 0, by) for by in (1, 2, 3)]
-    img_part = jnp.dot(grad_low[:, :half], mine, preferred_element_type=F32) + jnp.dot(
-        grad_low[:, half:], theirs, preferred_element_type=F32
-    )
+    img_part = jnp.dot(grad_low, txts, preferred_element_type=F32)
     img_part = coded(img_part).reshape(PEERS, rows, emb)
     img_part, *arrived = lax.optimization_barrier((img_part, *arrived))
     img_recv = lax.all_to_all(img_part, PLANE, 0, 0)

time: 123 us -> 121 us (0.984)
  waiting for transfers between devices: 40.4 us -> 32.2 us
  local copies, waits for them, and re-layouts: 1.99 us -> 9.84 us
  matrix products: 9.48 us -> 7.25 us
    unnamed x17 -> x21, local copies, waits for them, and re-layouts: 1.95 us -> 8.02 us
    all_to_all x1, waiting for transfers between devices: 6.98 us -> 0.99 us  [on_device(): imgs = lax.all_to_all(copies, PLANE, 0, 0).reshape(PEERS * rows, emb)]
    ppermute x16, waiting for transfers between devices: 31.8 us -> 30 us  [shifted(): return lax.ppermute(array, AXES, pairs)]
    dot_general x1, matrix products: 4.59 us -> 2.93 us  [on_device(): lax.dot_general(grad_low, imgs, (((0,), (0,)), ((), ())), preferred_eleme...]
    dot_general x2 -> x1, matrix products: 4.88 us -> 4.32 us  [on_device(): img_part = jnp.dot(grad_low, txts, preferred_element_type=F32)]
  transfers between devices with their start and end apart: 25 -> 25, of which waited for: 12 -> 12; matrix products, arithmetic and copies ran while one was open for 12% -> 15% of each run, Pallas kernels for 2% -> 2%
where the time goes in v7:
time: 121 us
  starting transfers between devices  52.2 us (43%)
  waiting for transfers between devices  32.2 us (27%)
  Pallas kernels  11.8 us (10%)
  local copies, waits for them, and re-layouts  9.84 us (8%)
  matrix products  7.25 us (6%)
  other arithmetic  5.41 us (4%)
  between operations  2.17 us (2%)
    ppermute x16, waiting for transfers between devices, shifted(): return lax.ppermute(array, AXES, pairs)  30 us
    ppermute x16, starting transfers between devices, shifted(): return lax.ppermute(array, AXES, pairs)  28.5 us
    ppermute x6, starting transfers between devices, moved(): return lax.ppermute(array, AXES, pairs)  9.64 us
    pallas_call x1, Pallas kernels, pairs(): pl.pallas_call(pair_kernel, grid=(count // rows,), in_specs=[SMEM, SMEM,...  8.12 us
    unnamed x21, local copies, waits for them, and re-layouts  8.02 us
    all_to_all x1, starting transfers between devices, on_device(): imgs = lax.all_to_all(copies, PLANE, 0, 0).reshape(PEERS * rows, emb)  7.48 us
    all_to_all x1, starting transfers between devices, on_device(): img_recv = lax.all_to_all(img_part, PLANE, 0, 0)  6.45 us
    dot_general x1, matrix products, on_device(): img_part = jnp.dot(grad_low, txts, preferred_element_type=F32)  4.32 us
  transfers between devices with their start and end apart: 25, of which 12 were waited for; matrix products, arithmetic and copies ran while one was open for 15% of the time, Pallas kernels for 2%

profile of v7, /device:TPU:2, one launch (start us, length us, event | category | flops | bytes accessed | tf_op | source)
XLA Modules:
  0.0 120.9 jit_solution(11841941917477718989)
XLA Ops:
  1.7 5.9 %collective-permute-start.4 = (bf16[64,1152]{1,0:T(8,128)(2,1)S(1)}, bf16[64,1152]{1,0:T(8,128)(2,1)S(1)}, u32[]{:S(2)}, u32[]{:S(2)}) collective-permute-start(bf16[64,1152]{1,0:T(8,128)(2,1)S(1)} %shard_map.68), channel_id=1, source_target_pairs={{0,112},{1,113},{2,114},{3,115},{4,116},{5,117},{6,118},{7,119},{8... | collective-permute-start | bytes 442376 | tf_op jit(solution)/shard_map/ppermute | solution.py:51
  8.5 1.7 %shard_map.67 = bf16[16,64,1152]{2,1,0:T(8,128)(2,1)} custom-call(bf16[64,1152]{1,0:T(8,128)(2,1)S(1)} %copy-done), custom_call_target="tpu_custom_call" | custom-call | flops 1000000 | bytes 3145728 | tf_op jit(solution)/shard_map/pallas_call | solution.py:225
  10.2 7.5 %all-to-all-start = ((bf16[16,64,1152]{2,1,0:T(8,128)(2,1)}), bf16[16,64,1152]{2,1,0:T(8,128)(2,1)S(1)}, u32[]{:S(2)}, u32[]{:S(2)}) async-start(bf16[16,64,1152]{2,1,0:T(8,128)(2,1)} %shard_map.67), calls=%async_computation | async-start | bytes 4718592 | tf_op jit(solution)/shard_map/all_to_all | solution.py:242
  18.4 3.2 %collective-permute-start.5 = (bf16[64,1152]{1,0:T(8,128)(2,1)S(1)}, bf16[64,1152]{1,0:T(8,128)(2,1)S(1)}, u32[]{:S(2)}, u32[]{:S(2)}) collective-permute-start(bf16[64,1152]{1,0:T(8,128)(2,1)S(1)} %collective-permute-done.4), channel_id=1, source_target_pairs={{0,112},{1,113},{2,114},{3,115},{4,116},{5,117},{6,118},{7,119},{8... | collective-permute-start | bytes 442376 | tf_op jit(solution)/shard_map/ppermute | solution.py:51
  22.3 2.0 %collective-permute-done.5 = bf16[64,1152]{1,0:T(8,128)(2,1)S(1)} collective-permute-done((bf16[64,1152]{1,0:T(8,128)(2,1)S(1)}, bf16[64,1152]{1,0:T(8,128)(2,1)S(1)}, u32[]{:S(2)}, u32[]{:S(2)}) %collective-permute-start.5) | collective-permute-done | bytes 147488 | tf_op jit(solution)/shard_map/ppermute | solution.py:51
  24.3 3.7 %collective-permute-start.6 = (bf16[64,1152]{1,0:T(8,128)(2,1)S(1)}, bf16[64,1152]{1,0:T(8,128)(2,1)S(1)}, u32[]{:S(2)}, u32[]{:S(2)}) collective-permute-start(bf16[64,1152]{1,0:T(8,128)(2,1)S(1)} %collective-permute-done.5), channel_id=1, source_target_pairs={{0,112},{1,113},{2,114},{3,115},{4,116},{5,117},{6,118},{7,119},{8... | collective-permute-start | bytes 442376 | tf_op jit(solution)/shard_map/ppermute | solution.py:51
  28.7 5.7 %collective-permute-done.2 = bf16[64,1152]{1,0:T(8,128)(2,1)S(1)} collective-permute-done((bf16[64,1152]{1,0:T(8,128)(2,1)S(1)}, bf16[64,1152]{1,0:T(8,128)(2,1)S(1)}, u32[]{:S(2)}, u32[]{:S(2)}) %collective-permute-start.2) | collective-permute-done | bytes 147488 | tf_op jit(solution)/shard_map/ppermute | solution.py:51
  35.0 5.7 %collective-permute-done.3 = bf16[64,1152]{1,0:T(8,128)(2,1)S(1)} collective-permute-done((bf16[64,1152]{1,0:T(8,128)(2,1)S(1)}, bf16[64,1152]{1,0:T(8,128)(2,1)S(1)}, u32[]{:S(2)}, u32[]{:S(2)}) %collective-permute-start.3) | collective-permute-done | bytes 147488 | tf_op jit(solution)/shard_map/ppermute | solution.py:51
  43.4 1.4 %copy-done.5 = bf16[1024,1152]{1,0:T(8,128)(2,1)} copy-done((bf16[1024,1152]{1,0:T(8,128)(2,1)}, bf16[1024,1152]{1,0:T(8,128)(2,1)S(1)}, u32[]{:S(2)}) %copy-start.5) | copy-done | bytes 2359320
  46.2 1.7 %collective-permute-done.7 = bf16[512,1152]{1,0:T(8,128)(2,1)S(1)} collective-permute-done((bf16[512,1152]{1,0:T(8,128)(2,1)}, bf16[512,1152]{1,0:T(8,128)(2,1)S(1)}, u32[]{:S(2)}, u32[]{:S(2)}) %collective-permute-start.7) | collective-permute-done | bytes 1179680 | tf_op jit(solution)/shard_map/ppermute | solution.py:51
  47.9 1.1 constant_dynamic-update-slice_fusion.8.mine_ref.theirs_ref
  49.0 1.0 all-to-all-done
  50.0 8.1 %shard_map.69 = (bf16[1024,1024]{1,0:T(8,128)(2,1)S(1)}, f32[3]{0:T(128)S(1)}) custom-call(s32[1]{0:T(128)} %bitcast.first_ref, f32[1]{0:T(128)S(6)} %exp.3.scale_ref, f32[1]{0:T(128)S(6)} %copy.23.shift_ref, bf16[1024,1152]{1,0:T(8,128)(2,1)S(1)} %bitcast.7, bf16[1024,1152]{1,0:T(8,128)(2,1)} %constant_dynamic-update-slice_fusion.8.mine_ref.theirs_ref, ...), custom_call_target="tpu_custom_call" | custom-call | flops 2415919104 | bytes 8388608 | tf_op jit(solution)/shard_map/pallas_call | solution.py:176
  58.2 1.6 %collective-permute-start.10 = (f32[3]{0:T(128)S(1)}, f32[3]{0:T(128)S(1)}, u32[]{:S(2)}, u32[]{:S(2)}) collective-permute-start(f32[3]{0:T(128)S(1)} %get-tuple-element.15), channel_id=1, source_target_pairs={{0,129},{1,0},{2,131},{3,2},{4,133},{5,4},{6,135},{7,6},{8,137},{9... | collective-permute-start | bytes 44 | tf_op jit(solution)/shard_map/ppermute | solution.py:69
  59.8 1.3 %collective-permute-start.9 = (f32[3]{0:T(128)S(1)}, f32[3]{0:T(128)S(1)}, u32[]{:S(2)}, u32[]{:S(2)}) collective-permute-start(f32[3]{0:T(128)S(1)} %get-tuple-element.15), channel_id=1, source_target_pairs={{0,128},{1,129},{2,130},{3,131},{4,132},{5,133},{6,134},{7,135},{8... | collective-permute-start | bytes 44 | tf_op jit(solution)/shard_map/ppermute | solution.py:69
  61.1 2.0 %collective-permute-start.8 = (f32[3]{0:T(128)S(1)}, f32[3]{0:T(128)S(1)}, u32[]{:S(2)}, u32[]{:S(2)}) collective-permute-start(f32[3]{0:T(128)S(1)} %get-tuple-element.15), channel_id=1, source_target_pairs={{0,1},{1,128},{2,3},{3,130},{4,5},{5,132},{6,7},{7,134},{8,9},{9,1... | collective-permute-start | bytes 44 | tf_op jit(solution)/shard_map/ppermute | solution.py:69
  63.0 2.9 %fusion.17 = f32[1024,1152]{1,0:T(8,128)S(1)} fusion(bf16[1024,1024]{1,0:T(8,128)(2,1)S(1)} %get-tuple-element.16, bf16[1024,1152]{1,0:T(8,128)(2,1)S(1)} %bitcast.8), kind=kOutput, calls=%fused_computation.68 | convolution fusion | flops 2415919104 | bytes 9175040 | tf_op jit(solution)/shard_map/dot_general | solution.py:257
  66.0 3.8 %collective-permute-start.13 = (f32[3]{0:T(128)S(1)}, f32[3]{0:T(128)S(1)}, u32[]{:S(2)}, u32[]{:S(2)}) collective-permute-start(f32[3]{0:T(128)S(1)} %add_add_fusion.1), channel_id=1, source_target_pairs={{0,6},{1,7},{2,0},{3,1},{4,2},{5,3},{6,4},{7,5},{8,14},{9,15},{10,... | collective-permute-start | bytes 44 | tf_op jit(solution)/shard_map/ppermute | solution.py:69
  71.4 4.3 %multiply_convert_fusion = f16[1024,1152]{1,0:T(8,128)(2,1)} fusion(bf16[1024,1024]{1,0:T(8,128)(2,1)S(1)} %get-tuple-element.16, bf16[1024,1152]{1,0:T(8,128)(2,1)S(1)} %copy-done.6), kind=kOutput, calls=%fused_computation.2 | convolution fusion | flops 2421817344 | bytes 6815744 | tf_op jit(solution)/shard_map/dot_general | solution.py:264
  75.8 6.4 %all-to-all-start.1 = ((f16[16,64,1152]{2,1,0:T(8,128)(2,1)}), f16[16,64,1152]{2,1,0:T(8,128)(2,1)S(1)}, u32[]{:S(2)}, u32[]{:S(2)}) async-start(f16[16,64,1152]{2,1,0:T(8,128)(2,1)} %bitcast.9), calls=%async_computation.1 | async-start | bytes 4718592 | tf_op jit(solution)/shard_map/all_to_all | solution.py:267
  82.3 1.1 collective-permute-done.15
  83.5 2.3 %fusion.9 = (f32[64,1152]{1,0:T(8,128)S(1)}, f32[64,1152]{1,0:T(8,128)S(1)}, f32[64,1152]{1,0:T(8,128)S(1)}, f32[64,1152]{1,0:T(8,128)S(1)}, f32[64,1152]{1,0:T(...) fusion(f32[1024,1152]{1,0:T(8,128)} %copy-done.4, ...), kind=kLoop, calls=%fused_computation.38 | loop fusion | flops 2949120 | bytes 5898240 | tf_op jit(solution)/shard_map/add | solution.py:274
  86.2 2.0 %collective-permute-start.17 = (f16[72,1152]{1,0:T(8,128)(2,1)S(1)}, f16[72,1152]{1,0:T(8,128)(2,1)S(1)}, u32[]{:S(2)}, u32[]{:S(2)}) collective-permute-start(f16[72,1152]{1,0:T(8,128)(2,1)S(1)} %get-tuple-element.53), channel_id=1, source_target_pairs={{0,96},{1,97},{2,98},{3,99},{4,100},{5,101},{6,102},{7,103},{8,104... | collective-permute-start | bytes 497672 | tf_op jit(solution)/shard_map/ppermute | solution.py:51
  88.1 1.0 collective-permute-start.19
  89.2 3.1 %collective-permute-start.21 = (f16[72,1152]{1,0:T(8,128)(2,1)S(1)}, f16[72,1152]{1,0:T(8,128)(2,1)S(1)}, u32[]{:S(2)}, u32[]{:S(2)}) collective-permute-start(f16[72,1152]{1,0:T(8,128)(2,1)S(1)} %get-tuple-element.55), channel_id=1, source_target_pairs={{0,96},{1,97},{2,98},{3,99},{4,100},{5,101},{6,102},{7,103},{8,104... | collective-permute-start | bytes 497672 | tf_op jit(solution)/shard_map/ppermute | solution.py:51
  92.3 3.8 %collective-permute-done.17 = f16[72,1152]{1,0:T(8,128)(2,1)S(1)} collective-permute-done((f16[72,1152]{1,0:T(8,128)(2,1)S(1)}, f16[72,1152]{1,0:T(8,128)(2,1)S(1)}, u32[]{:S(2)}, u32[]{:S(2)}) %collective-permute-start.17) | collective-permute-done | bytes 165920 | tf_op jit(solution)/shard_map/ppermute | solution.py:51
  96.1 3.5 %collective-permute-done.19 = f16[72,1152]{1,0:T(8,128)(2,1)S(1)} collective-permute-done((f16[72,1152]{1,0:T(8,128)(2,1)S(1)}, f16[72,1152]{1,0:T(8,128)(2,1)S(1)}, u32[]{:S(2)}, u32[]{:S(2)}) %collective-permute-start.19) | collective-permute-done | bytes 165920 | tf_op jit(solution)/shard_map/ppermute | solution.py:51
  99.6 1.3 %collective-permute-done.21 = f16[72,1152]{1,0:T(8,128)(2,1)S(1)} collective-permute-done((f16[72,1152]{1,0:T(8,128)(2,1)S(1)}, f16[72,1152]{1,0:T(8,128)(2,1)S(1)}, u32[]{:S(2)}, u32[]{:S(2)}) %collective-permute-start.21) | collective-permute-done | bytes 165920 | tf_op jit(solution)/shard_map/ppermute | solution.py:51
  102.2 3.7 %collective-permute-start.18 = (f16[72,1152]{1,0:T(8,128)(2,1)S(1)}, f16[72,1152]{1,0:T(8,128)(2,1)S(1)}, u32[]{:S(2)}, u32[]{:S(2)}) collective-permute-start(f16[72,1152]{1,0:T(8,128)(2,1)S(1)} %get-tuple-element.50), channel_id=1, source_target_pairs={{0,96},{1,97},{2,98},{3,99},{4,100},{5,101},{6,102},{7,103},{8,104... | collective-permute-start | bytes 497672 | tf_op jit(solution)/shard_map/ppermute | solution.py:51
  105.9 3.6 %collective-permute-start.20 = (f16[72,1152]{1,0:T(8,128)(2,1)S(1)}, f16[72,1152]{1,0:T(8,128)(2,1)S(1)}, u32[]{:S(2)}, u32[]{:S(2)}) collective-permute-start(f16[72,1152]{1,0:T(8,128)(2,1)S(1)} %get-tuple-element.51), channel_id=1, source_target_pairs={{0,16},{1,17},{2,18},{3,19},{4,20},{5,21},{6,22},{7,23},{8,24},{9,... | collective-permute-start | bytes 497672 | tf_op jit(solution)/shard_map/ppermute | solution.py:51
  109.5 1.4 %collective-permute-start.22 = (f16[72,1152]{1,0:T(8,128)(2,1)S(1)}, f16[72,1152]{1,0:T(8,128)(2,1)S(1)}, u32[]{:S(2)}, u32[]{:S(2)}) collective-permute-start(f16[72,1152]{1,0:T(8,128)(2,1)S(1)} %get-tuple-element.52), channel_id=1, source_target_pairs={{0,112},{1,113},{2,114},{3,115},{4,116},{5,117},{6,118},{7,119},{8... | collective-permute-start | bytes 497672 | tf_op jit(solution)/shard_map/ppermute | solution.py:51
  110.9 5.7 %collective-permute-done.20 = f16[72,1152]{1,0:T(8,128)(2,1)S(1)} collective-permute-done((f16[72,1152]{1,0:T(8,128)(2,1)S(1)}, f16[72,1152]{1,0:T(8,128)(2,1)S(1)}, u32[]{:S(2)}, u32[]{:S(2)}) %collective-permute-start.20) | collective-permute-done | bytes 165920 | tf_op jit(solution)/shard_map/ppermute | solution.py:51
  (60 shorter events, 15.0 us)
Async XLA Ops:
  0.6 0.9 copy-start.2
  1.7 16.7 %collective-permute-start.4 = (bf16[64,1152]{1,0:T(8,128)(2,1)S(1)}, bf16[64,1152]{1,0:T(8,128)(2,1)S(1)}, u32[]{:S(2)}, u32[]{:S(2)}) collective-permute-start(bf16[64,1152]{1,0:T(8,128)(2,1)S(1)} %shard_map.68), channel_id=1, source_target_pairs={{0,112},{1,113},{2,114},{3,115},{4,116},{5,117},{6,118},{7,119},{8... | collective-permute-start | bytes 442376 | tf_op jit(solution)/shard_map/ppermute | solution.py:51
  7.6 14.0 %collective-permute-start = (bf16[64,1152]{1,0:T(8,128)(2,1)S(1)}, bf16[64,1152]{1,0:T(8,128)(2,1)S(1)}, u32[]{:S(2)}, u32[]{:S(2)}) collective-permute-start(bf16[64,1152]{1,0:T(8,128)(2,1)S(1)} %shard_map.68), channel_id=1, source_target_pairs={{0,16},{1,17},{2,18},{3,19},{4,20},{5,21},{6,22},{7,23},{8,24},{9,... | collective-permute-start | bytes 442376 | tf_op jit(solution)/shard_map/ppermute | solution.py:51
  7.6 0.9 copy-start
  10.2 39.8 %all-to-all-start = ((bf16[16,64,1152]{2,1,0:T(8,128)(2,1)}), bf16[16,64,1152]{2,1,0:T(8,128)(2,1)S(1)}, u32[]{:S(2)}, u32[]{:S(2)}) async-start(bf16[16,64,1152]{2,1,0:T(8,128)(2,1)} %shard_map.67), calls=%async_computation | async-start | bytes 4718592 | tf_op jit(solution)/shard_map/all_to_all | solution.py:242
  18.4 5.9 %collective-permute-start.5 = (bf16[64,1152]{1,0:T(8,128)(2,1)S(1)}, bf16[64,1152]{1,0:T(8,128)(2,1)S(1)}, u32[]{:S(2)}, u32[]{:S(2)}) collective-permute-start(bf16[64,1152]{1,0:T(8,128)(2,1)S(1)} %collective-permute-done.4), channel_id=1, source_target_pairs={{0,112},{1,113},{2,114},{3,115},{4,116},{5,117},{6,118},{7,119},{8... | collective-permute-start | bytes 442376 | tf_op jit(solution)/shard_map/ppermute | solution.py:51
  21.6 6.4 %collective-permute-start.1 = (bf16[64,1152]{1,0:T(8,128)(2,1)S(1)}, bf16[64,1152]{1,0:T(8,128)(2,1)S(1)}, u32[]{:S(2)}, u32[]{:S(2)}) collective-permute-start(bf16[64,1152]{1,0:T(8,128)(2,1)S(1)} %collective-permute-done), channel_id=1, source_target_pairs={{0,16},{1,17},{2,18},{3,19},{4,20},{5,21},{6,22},{7,23},{8,24},{9,... | collective-permute-start | bytes 442376 | tf_op jit(solution)/shard_map/ppermute | solution.py:51
  24.3 17.1 %collective-permute-start.6 = (bf16[64,1152]{1,0:T(8,128)(2,1)S(1)}, bf16[64,1152]{1,0:T(8,128)(2,1)S(1)}, u32[]{:S(2)}, u32[]{:S(2)}) collective-permute-start(bf16[64,1152]{1,0:T(8,128)(2,1)S(1)} %collective-permute-done.5), channel_id=1, source_target_pairs={{0,112},{1,113},{2,114},{3,115},{4,116},{5,117},{6,118},{7,119},{8... | collective-permute-start | bytes 442376 | tf_op jit(solution)/shard_map/ppermute | solution.py:51
  28.0 6.4 %collective-permute-start.2 = (bf16[64,1152]{1,0:T(8,128)(2,1)S(1)}, bf16[64,1152]{1,0:T(8,128)(2,1)S(1)}, u32[]{:S(2)}, u32[]{:S(2)}) collective-permute-start(bf16[64,1152]{1,0:T(8,128)(2,1)S(1)} %collective-permute-done.1), channel_id=1, source_target_pairs={{0,16},{1,17},{2,18},{3,19},{4,20},{5,21},{6,22},{7,23},{8,24},{9,... | collective-permute-start | bytes 442376 | tf_op jit(solution)/shard_map/ppermute | solution.py:51
  34.3 6.4 %collective-permute-start.3 = (bf16[64,1152]{1,0:T(8,128)(2,1)S(1)}, bf16[64,1152]{1,0:T(8,128)(2,1)S(1)}, u32[]{:S(2)}, u32[]{:S(2)}) collective-permute-start(bf16[64,1152]{1,0:T(8,128)(2,1)S(1)} %collective-permute-done.2), channel_id=1, source_target_pairs={{0,16},{1,17},{2,18},{3,19},{4,20},{5,21},{6,22},{7,23},{8,24},{9,... | collective-permute-start | bytes 442376 | tf_op jit(solution)/shard_map/ppermute | solution.py:51
  43.4 1.4 %copy-start.5 = (bf16[1024,1152]{1,0:T(8,128)(2,1)}, bf16[1024,1152]{1,0:T(8,128)(2,1)S(1)}, u32[]{:S(2)}) copy-start(bf16[1024,1152]{1,0:T(8,128)(2,1)S(1)} %get-tuple-element.34) | copy-start | bytes 7077892
  44.9 3.1 %collective-permute-start.7 = (bf16[512,1152]{1,0:T(8,128)(2,1)}, bf16[512,1152]{1,0:T(8,128)(2,1)S(1)}, u32[]{:S(2)}, u32[]{:S(2)}) collective-permute-start(bf16[512,1152]{1,0:T(8,128)(2,1)} %get-tuple-element.33), channel_id=1, source_target_pairs={{0,8},{1,9},{2,10},{3,11},{4,12},{5,13},{6,14},{7,15},{8,0},{9,1},... | collective-permute-start | bytes 3538952 | tf_op jit(solution)/shard_map/ppermute | solution.py:51
  58.2 7.8 %collective-permute-start.10 = (f32[3]{0:T(128)S(1)}, f32[3]{0:T(128)S(1)}, u32[]{:S(2)}, u32[]{:S(2)}) collective-permute-start(f32[3]{0:T(128)S(1)} %get-tuple-element.15), channel_id=1, source_target_pairs={{0,129},{1,0},{2,131},{3,2},{4,133},{5,4},{6,135},{7,6},{8,137},{9... | collective-permute-start | bytes 44 | tf_op jit(solution)/shard_map/ppermute | solution.py:69
  59.8 6.2 %collective-permute-start.9 = (f32[3]{0:T(128)S(1)}, f32[3]{0:T(128)S(1)}, u32[]{:S(2)}, u32[]{:S(2)}) collective-permute-start(f32[3]{0:T(128)S(1)} %get-tuple-element.15), channel_id=1, source_target_pairs={{0,128},{1,129},{2,130},{3,131},{4,132},{5,133},{6,134},{7,135},{8... | collective-permute-start | bytes 44 | tf_op jit(solution)/shard_map/ppermute | solution.py:69
  61.1 4.9 %collective-permute-start.8 = (f32[3]{0:T(128)S(1)}, f32[3]{0:T(128)S(1)}, u32[]{:S(2)}, u32[]{:S(2)}) collective-permute-start(f32[3]{0:T(128)S(1)} %get-tuple-element.15), channel_id=1, source_target_pairs={{0,1},{1,128},{2,3},{3,130},{4,5},{5,132},{6,7},{7,134},{8,9},{9,1... | collective-permute-start | bytes 44 | tf_op jit(solution)/shard_map/ppermute | solution.py:69
  66.0 9.8 %copy-start.4 = (f32[1024,1152]{1,0:T(8,128)}, f32[1024,1152]{1,0:T(8,128)S(1)}, u32[]{:S(2)}) copy-start(f32[1024,1152]{1,0:T(8,128)S(1)} %fusion.17) | copy-start | bytes 14155780
  66.0 5.5 %copy-start.6 = (bf16[1024,1152]{1,0:T(8,128)(2,1)S(1)}, bf16[1024,1152]{1,0:T(8,128)(2,1)}, u32[]{:S(2)}) copy-start(bf16[1024,1152]{1,0:T(8,128)(2,1)} %constant_dynamic-update-slice_fusion.8.mine_ref.theirs_ref) | copy-start | bytes 7077892
  66.0 9.7 %collective-permute-start.13 = (f32[3]{0:T(128)S(1)}, f32[3]{0:T(128)S(1)}, u32[]{:S(2)}, u32[]{:S(2)}) collective-permute-start(f32[3]{0:T(128)S(1)} %add_add_fusion.1), channel_id=1, source_target_pairs={{0,6},{1,7},{2,0},{3,1},{4,2},{5,3},{6,4},{7,5},{8,14},{9,15},{10,... | collective-permute-start | bytes 44 | tf_op jit(solution)/shard_map/ppermute | solution.py:69
  69.8 5.9 %collective-permute-start.12 = (f32[3]{0:T(128)S(1)}, f32[3]{0:T(128)S(1)}, u32[]{:S(2)}, u32[]{:S(2)}) collective-permute-start(f32[3]{0:T(128)S(1)} %add_add_fusion.1), channel_id=1, source_target_pairs={{0,4},{1,5},{2,6},{3,7},{4,0},{5,1},{6,2},{7,3},{8,12},{9,13},{10,... | collective-permute-start | bytes 44 | tf_op jit(solution)/shard_map/ppermute | solution.py:69
  69.9 5.9 %collective-permute-start.11 = (f32[3]{0:T(128)S(1)}, f32[3]{0:T(128)S(1)}, u32[]{:S(2)}, u32[]{:S(2)}) collective-permute-start(f32[3]{0:T(128)S(1)} %add_add_fusion.1), channel_id=1, source_target_pairs={{0,2},{1,3},{2,4},{3,5},{4,6},{5,7},{6,0},{7,1},{8,10},{9,11},{10,... | collective-permute-start | bytes 44 | tf_op jit(solution)/shard_map/ppermute | solution.py:69
  71.3 12.2 %collective-permute-start.14 = (f16[512,1152]{1,0:T(8,128)(2,1)S(1)}, f16[512,1152]{1,0:T(8,128)(2,1)}, u32[]{:S(2)}, u32[]{:S(2)}) collective-permute-start(f16[512,1152]{1,0:T(8,128)(2,1)S(1)} %multiply_convert_fusion.1), channel_id=1, source_target_pairs={{0,8},{1,9},{2,10},{3,11},{4,12},{5,13},{6,14},{7,15},{8,0},{9,1},... | collective-permute-start | bytes 3538952 | tf_op jit(solution)/shard_map/ppermute | solution.py:51
  75.8 43.4 %all-to-all-start.1 = ((f16[16,64,1152]{2,1,0:T(8,128)(2,1)}), f16[16,64,1152]{2,1,0:T(8,128)(2,1)S(1)}, u32[]{:S(2)}, u32[]{:S(2)}) async-start(f16[16,64,1152]{2,1,0:T(8,128)(2,1)} %bitcast.9), calls=%async_computation.1 | async-start | bytes 4718592 | tf_op jit(solution)/shard_map/all_to_all | solution.py:267
  82.2 1.2 collective-permute-start.15
  86.2 31.4 %copy-start.3 = (bf16[64,1152]{1,0:T(8,128)(2,1)S(1)}, bf16[64,1152]{1,0:T(8,128)(2,1)}, u32[]{:S(2)}) copy-start(bf16[64,1152]{1,0:T(8,128)(2,1)} %rows_ref.7) | copy-start | bytes 442372
  86.2 9.9 %collective-permute-start.17 = (f16[72,1152]{1,0:T(8,128)(2,1)S(1)}, f16[72,1152]{1,0:T(8,128)(2,1)S(1)}, u32[]{:S(2)}, u32[]{:S(2)}) collective-permute-start(f16[72,1152]{1,0:T(8,128)(2,1)S(1)} %get-tuple-element.53), channel_id=1, source_target_pairs={{0,96},{1,97},{2,98},{3,99},{4,100},{5,101},{6,102},{7,103},{8,104... | collective-permute-start | bytes 497672 | tf_op jit(solution)/shard_map/ppermute | solution.py:51
  88.1 11.5 %collective-permute-start.19 = (f16[72,1152]{1,0:T(8,128)(2,1)S(1)}, f16[72,1152]{1,0:T(8,128)(2,1)S(1)}, u32[]{:S(2)}, u32[]{:S(2)}) collective-permute-start(f16[72,1152]{1,0:T(8,128)(2,1)S(1)} %get-tuple-element.54), channel_id=1, source_target_pairs={{0,32},{1,33},{2,34},{3,35},{4,36},{5,37},{6,38},{7,39},{8,40},{9,... | collective-permute-start | bytes 497672 | tf_op jit(solution)/shard_map/ppermute | solution.py:51
  89.2 11.7 %collective-permute-start.21 = (f16[72,1152]{1,0:T(8,128)(2,1)S(1)}, f16[72,1152]{1,0:T(8,128)(2,1)S(1)}, u32[]{:S(2)}, u32[]{:S(2)}) collective-permute-start(f16[72,1152]{1,0:T(8,128)(2,1)S(1)} %get-tuple-element.55), channel_id=1, source_target_pairs={{0,96},{1,97},{2,98},{3,99},{4,100},{5,101},{6,102},{7,103},{8,104... | collective-permute-start | bytes 497672 | tf_op jit(solution)/shard_map/ppermute | solution.py:51
  101.4 9.5 %collective-permute-start.16 = (f16[72,1152]{1,0:T(8,128)(2,1)S(1)}, f16[72,1152]{1,0:T(8,128)(2,1)S(1)}, u32[]{:S(2)}, u32[]{:S(2)}) collective-permute-start(f16[72,1152]{1,0:T(8,128)(2,1)S(1)} %get-tuple-element.49), channel_id=1, source_target_pairs={{0,32},{1,33},{2,34},{3,35},{4,36},{5,37},{6,38},{7,39},{8,40},{9,... | collective-permute-start | bytes 497672 | tf_op jit(solution)/shard_map/ppermute | solution.py:51
  102.2 8.7 %collective-permute-start.18 = (f16[72,1152]{1,0:T(8,128)(2,1)S(1)}, f16[72,1152]{1,0:T(8,128)(2,1)S(1)}, u32[]{:S(2)}, u32[]{:S(2)}) collective-permute-start(f16[72,1152]{1,0:T(8,128)(2,1)S(1)} %get-tuple-element.50), channel_id=1, source_target_pairs={{0,96},{1,97},{2,98},{3,99},{4,100},{5,101},{6,102},{7,103},{8,104... | collective-permute-start | bytes 497672 | tf_op jit(solution)/shard_map/ppermute | solution.py:51
  105.9 10.7 %collective-permute-start.20 = (f16[72,1152]{1,0:T(8,128)(2,1)S(1)}, f16[72,1152]{1,0:T(8,128)(2,1)S(1)}, u32[]{:S(2)}, u32[]{:S(2)}) collective-permute-start(f16[72,1152]{1,0:T(8,128)(2,1)S(1)} %get-tuple-element.51), channel_id=1, source_target_pairs={{0,16},{1,17},{2,18},{3,19},{4,20},{5,21},{6,22},{7,23},{8,24},{9,... | collective-permute-start | bytes 497672 | tf_op jit(solution)/shard_map/ppermute | solution.py:51
  109.5 7.7 %collective-permute-start.22 = (f16[72,1152]{1,0:T(8,128)(2,1)S(1)}, f16[72,1152]{1,0:T(8,128)(2,1)S(1)}, u32[]{:S(2)}, u32[]{:S(2)}) collective-permute-start(f16[72,1152]{1,0:T(8,128)(2,1)S(1)} %get-tuple-element.52), channel_id=1, source_target_pairs={{0,112},{1,113},{2,114},{3,115},{4,116},{5,117},{6,118},{7,119},{8... | collective-permute-start | bytes 497672 | tf_op jit(solution)/shard_map/ppermute | solution.py:51
  117.2 2.7 %copy-start.1 = (bf16[64,1152]{1,0:T(8,128)(2,1)S(1)}, bf16[64,1152]{1,0:T(8,128)(2,1)}, u32[]{:S(2)}) copy-start(bf16[64,1152]{1,0:T(8,128)(2,1)} %rows_ref.6) | copy-start | bytes 442372

commit v8 on v7

--- a/solution.py
+++ b/solution.py
@@ -172,7 +172,7 @@
 def pairs(first, scale, shift, imgs, txts):
     count, emb = imgs.shape
     half = txts.shape[0] // 2
-    rows = 256
+    rows = 512
     return pl.pallas_call(
         pair_kernel,
         grid=(count // rows,),

time: 121 us -> 121 us (level)
  transfers between devices with their start and end apart: 25 -> 25, of which waited for: 12 -> 11; matrix products, arithmetic and copies ran while one was open for 15% -> 15% of each run, Pallas kernels for 2% -> 2%
where the time goes in v8:
time: 121 us; the launch traced here: 120 us
  starting transfers between devices  52.1 us (43%)
  waiting for transfers between devices  32.2 us (27%)
  Pallas kernels  11.5 us (10%)
  local copies, waits for them, and re-layouts  9.84 us (8%)
  matrix products  7.25 us (6%)
  other arithmetic  5.41 us (4%)
  between operations  2.17 us (2%)
    ppermute x16, waiting for transfers between devices, shifted(): return lax.ppermute(array, AXES, pairs)  30.1 us
    ppermute x16, starting transfers between devices, shifted(): return lax.ppermute(array, AXES, pairs)  28.5 us
    ppermute x6, starting transfers between devices, moved(): return lax.ppermute(array, AXES, pairs)  9.64 us
    unnamed x21, local copies, waits for them, and re-layouts  8.02 us
    pallas_call x1, Pallas kernels, pairs(): pl.pallas_call(pair_kernel, grid=(count // rows,), in_specs=[SMEM, SMEM,...  7.75 us
    all_to_all x1, starting transfers between devices, on_device(): imgs = lax.all_to_all(copies, PLANE, 0, 0).reshape(PEERS * rows, emb)  7.48 us
    all_to_all x1, starting transfers between devices, on_device(): img_recv = lax.all_to_all(img_part, PLANE, 0, 0)  6.46 us
    dot_general x1, matrix products, on_device(): img_part = jnp.dot(grad_low, txts, preferred_element_type=F32)  4.32 us
  transfers between devices with their start and end apart: 25, of which 11 were waited for; matrix products, arithmetic and copies ran while one was open for 15% of the time, Pallas kernels for 2%

profile of v8, /device:TPU:2, one launch (start us, length us, event | category | flops | bytes accessed | tf_op | source)
XLA Modules:
  0.0 120.5 jit_solution(2889238176876490710)
XLA Ops:
  1.7 5.9 %collective-permute-start.4 = (bf16[64,1152]{1,0:T(8,128)(2,1)S(1)}, bf16[64,1152]{1,0:T(8,128)(2,1)S(1)}, u32[]{:S(2)}, u32[]{:S(2)}) collective-permute-start(bf16[64,1152]{1,0:T(8,128)(2,1)S(1)} %shard_map.68), channel_id=1, source_target_pairs={{0,112},{1,113},{2,114},{3,115},{4,116},{5,117},{6,118},{7,119},{8... | collective-permute-start | bytes 442376 | tf_op jit(solution)/shard_map/ppermute | solution.py:51
  8.5 1.7 %shard_map.67 = bf16[16,64,1152]{2,1,0:T(8,128)(2,1)} custom-call(bf16[64,1152]{1,0:T(8,128)(2,1)S(1)} %copy-done), custom_call_target="tpu_custom_call" | custom-call | flops 1000000 | bytes 3145728 | tf_op jit(solution)/shard_map/pallas_call | solution.py:225
  10.2 7.5 %all-to-all-start = ((bf16[16,64,1152]{2,1,0:T(8,128)(2,1)}), bf16[16,64,1152]{2,1,0:T(8,128)(2,1)S(1)}, u32[]{:S(2)}, u32[]{:S(2)}) async-start(bf16[16,64,1152]{2,1,0:T(8,128)(2,1)} %shard_map.67), calls=%async_computation | async-start | bytes 4718592 | tf_op jit(solution)/shard_map/all_to_all | solution.py:242
  18.4 3.2 %collective-permute-start.5 = (bf16[64,1152]{1,0:T(8,128)(2,1)S(1)}, bf16[64,1152]{1,0:T(8,128)(2,1)S(1)}, u32[]{:S(2)}, u32[]{:S(2)}) collective-permute-start(bf16[64,1152]{1,0:T(8,128)(2,1)S(1)} %collective-permute-done.4), channel_id=1, source_target_pairs={{0,112},{1,113},{2,114},{3,115},{4,116},{5,117},{6,118},{7,119},{8... | collective-permute-start | bytes 442376 | tf_op jit(solution)/shard_map/ppermute | solution.py:51
  22.3 2.0 %collective-permute-done.5 = bf16[64,1152]{1,0:T(8,128)(2,1)S(1)} collective-permute-done((bf16[64,1152]{1,0:T(8,128)(2,1)S(1)}, bf16[64,1152]{1,0:T(8,128)(2,1)S(1)}, u32[]{:S(2)}, u32[]{:S(2)}) %collective-permute-start.5) | collective-permute-done | bytes 147488 | tf_op jit(solution)/shard_map/ppermute | solution.py:51
  24.3 3.7 %collective-permute-start.6 = (bf16[64,1152]{1,0:T(8,128)(2,1)S(1)}, bf16[64,1152]{1,0:T(8,128)(2,1)S(1)}, u32[]{:S(2)}, u32[]{:S(2)}) collective-permute-start(bf16[64,1152]{1,0:T(8,128)(2,1)S(1)} %collective-permute-done.5), channel_id=1, source_target_pairs={{0,112},{1,113},{2,114},{3,115},{4,116},{5,117},{6,118},{7,119},{8... | collective-permute-start | bytes 442376 | tf_op jit(solution)/shard_map/ppermute | solution.py:51
  28.7 5.7 %collective-permute-done.2 = bf16[64,1152]{1,0:T(8,128)(2,1)S(1)} collective-permute-done((bf16[64,1152]{1,0:T(8,128)(2,1)S(1)}, bf16[64,1152]{1,0:T(8,128)(2,1)S(1)}, u32[]{:S(2)}, u32[]{:S(2)}) %collective-permute-start.2) | collective-permute-done | bytes 147488 | tf_op jit(solution)/shard_map/ppermute | solution.py:51
  35.0 5.7 %collective-permute-done.3 = bf16[64,1152]{1,0:T(8,128)(2,1)S(1)} collective-permute-done((bf16[64,1152]{1,0:T(8,128)(2,1)S(1)}, bf16[64,1152]{1,0:T(8,128)(2,1)S(1)}, u32[]{:S(2)}, u32[]{:S(2)}) %collective-permute-start.3) | collective-permute-done | bytes 147488 | tf_op jit(solution)/shard_map/ppermute | solution.py:51
  43.4 1.4 %copy-done.5 = bf16[1024,1152]{1,0:T(8,128)(2,1)} copy-done((bf16[1024,1152]{1,0:T(8,128)(2,1)}, bf16[1024,1152]{1,0:T(8,128)(2,1)S(1)}, u32[]{:S(2)}) %copy-start.5) | copy-done | bytes 2359320
  46.2 1.7 %collective-permute-done.7 = bf16[512,1152]{1,0:T(8,128)(2,1)S(1)} collective-permute-done((bf16[512,1152]{1,0:T(8,128)(2,1)}, bf16[512,1152]{1,0:T(8,128)(2,1)S(1)}, u32[]{:S(2)}, u32[]{:S(2)}) %collective-permute-start.7) | collective-permute-done | bytes 1179680 | tf_op jit(solution)/shard_map/ppermute | solution.py:51
  47.9 1.1 constant_dynamic-update-slice_fusion.8.mine_ref.theirs_ref
  49.0 1.0 all-to-all-done
  50.0 7.7 %shard_map.69 = (bf16[1024,1024]{1,0:T(8,128)(2,1)S(1)}, f32[3]{0:T(128)S(1)}) custom-call(s32[1]{0:T(128)} %bitcast.first_ref, f32[1]{0:T(128)S(6)} %exp.3.scale_ref, f32[1]{0:T(128)S(6)} %copy.23.shift_ref, bf16[1024,1152]{1,0:T(8,128)(2,1)S(1)} %bitcast.7, bf16[1024,1152]{1,0:T(8,128)(2,1)} %constant_dynamic-update-slice_fusion.8.mine_ref.theirs_ref, ...), custom_call_target="tpu_custom_call" | custom-call | flops 2415919104 | bytes 8388608 | tf_op jit(solution)/shard_map/pallas_call | solution.py:176
  57.8 1.6 %collective-permute-start.10 = (f32[3]{0:T(128)S(1)}, f32[3]{0:T(128)S(1)}, u32[]{:S(2)}, u32[]{:S(2)}) collective-permute-start(f32[3]{0:T(128)S(1)} %get-tuple-element.15), channel_id=1, source_target_pairs={{0,129},{1,0},{2,131},{3,2},{4,133},{5,4},{6,135},{7,6},{8,137},{9... | collective-permute-start | bytes 44 | tf_op jit(solution)/shard_map/ppermute | solution.py:69
  59.4 1.3 %collective-permute-start.9 = (f32[3]{0:T(128)S(1)}, f32[3]{0:T(128)S(1)}, u32[]{:S(2)}, u32[]{:S(2)}) collective-permute-start(f32[3]{0:T(128)S(1)} %get-tuple-element.15), channel_id=1, source_target_pairs={{0,128},{1,129},{2,130},{3,131},{4,132},{5,133},{6,134},{7,135},{8... | collective-permute-start | bytes 44 | tf_op jit(solution)/shard_map/ppermute | solution.py:69
  60.7 2.0 %collective-permute-start.8 = (f32[3]{0:T(128)S(1)}, f32[3]{0:T(128)S(1)}, u32[]{:S(2)}, u32[]{:S(2)}) collective-permute-start(f32[3]{0:T(128)S(1)} %get-tuple-element.15), channel_id=1, source_target_pairs={{0,1},{1,128},{2,3},{3,130},{4,5},{5,132},{6,7},{7,134},{8,9},{9,1... | collective-permute-start | bytes 44 | tf_op jit(solution)/shard_map/ppermute | solution.py:69
  62.6 2.9 %fusion.17 = f32[1024,1152]{1,0:T(8,128)S(1)} fusion(bf16[1024,1024]{1,0:T(8,128)(2,1)S(1)} %get-tuple-element.16, bf16[1024,1152]{1,0:T(8,128)(2,1)S(1)} %bitcast.8), kind=kOutput, calls=%fused_computation.68 | convolution fusion | flops 2415919104 | bytes 9175040 | tf_op jit(solution)/shard_map/dot_general | solution.py:257
  65.6 3.8 %collective-permute-start.13 = (f32[3]{0:T(128)S(1)}, f32[3]{0:T(128)S(1)}, u32[]{:S(2)}, u32[]{:S(2)}) collective-permute-start(f32[3]{0:T(128)S(1)} %add_add_fusion.1), channel_id=1, source_target_pairs={{0,6},{1,7},{2,0},{3,1},{4,2},{5,3},{6,4},{7,5},{8,14},{9,15},{10,... | collective-permute-start | bytes 44 | tf_op jit(solution)/shard_map/ppermute | solution.py:69
  71.1 4.3 %multiply_convert_fusion = f16[1024,1152]{1,0:T(8,128)(2,1)} fusion(bf16[1024,1024]{1,0:T(8,128)(2,1)S(1)} %get-tuple-element.16, bf16[1024,1152]{1,0:T(8,128)(2,1)S(1)} %copy-done.6), kind=kOutput, calls=%fused_computation.2 | convolution fusion | flops 2421817344 | bytes 6815744 | tf_op jit(solution)/shard_map/dot_general | solution.py:264
  75.4 6.5 %all-to-all-start.1 = ((f16[16,64,1152]{2,1,0:T(8,128)(2,1)}), f16[16,64,1152]{2,1,0:T(8,128)(2,1)S(1)}, u32[]{:S(2)}, u32[]{:S(2)}) async-start(f16[16,64,1152]{2,1,0:T(8,128)(2,1)} %bitcast.9), calls=%async_computation.1 | async-start | bytes 4718592 | tf_op jit(solution)/shard_map/all_to_all | solution.py:267
  82.0 1.1 collective-permute-done.15
  83.2 2.3 %fusion.9 = (f32[64,1152]{1,0:T(8,128)S(1)}, f32[64,1152]{1,0:T(8,128)S(1)}, f32[64,1152]{1,0:T(8,128)S(1)}, f32[64,1152]{1,0:T(8,128)S(1)}, f32[64,1152]{1,0:T(...) fusion(f32[1024,1152]{1,0:T(8,128)} %copy-done.4, ...), kind=kLoop, calls=%fused_computation.38 | loop fusion | flops 2949120 | bytes 5898240 | tf_op jit(solution)/shard_map/add | solution.py:274
  85.8 2.0 %collective-permute-start.17 = (f16[72,1152]{1,0:T(8,128)(2,1)S(1)}, f16[72,1152]{1,0:T(8,128)(2,1)S(1)}, u32[]{:S(2)}, u32[]{:S(2)}) collective-permute-start(f16[72,1152]{1,0:T(8,128)(2,1)S(1)} %get-tuple-element.53), channel_id=1, source_target_pairs={{0,96},{1,97},{2,98},{3,99},{4,100},{5,101},{6,102},{7,103},{8,104... | collective-permute-start | bytes 497672 | tf_op jit(solution)/shard_map/ppermute | solution.py:51
  87.8 1.1 collective-permute-start.19
  88.8 3.1 %collective-permute-start.21 = (f16[72,1152]{1,0:T(8,128)(2,1)S(1)}, f16[72,1152]{1,0:T(8,128)(2,1)S(1)}, u32[]{:S(2)}, u32[]{:S(2)}) collective-permute-start(f16[72,1152]{1,0:T(8,128)(2,1)S(1)} %get-tuple-element.55), channel_id=1, source_target_pairs={{0,96},{1,97},{2,98},{3,99},{4,100},{5,101},{6,102},{7,103},{8,104... | collective-permute-start | bytes 497672 | tf_op jit(solution)/shard_map/ppermute | solution.py:51
  91.9 3.8 %collective-permute-done.17 = f16[72,1152]{1,0:T(8,128)(2,1)S(1)} collective-permute-done((f16[72,1152]{1,0:T(8,128)(2,1)S(1)}, f16[72,1152]{1,0:T(8,128)(2,1)S(1)}, u32[]{:S(2)}, u32[]{:S(2)}) %collective-permute-start.17) | collective-permute-done | bytes 165920 | tf_op jit(solution)/shard_map/ppermute | solution.py:51
  95.7 3.5 %collective-permute-done.19 = f16[72,1152]{1,0:T(8,128)(2,1)S(1)} collective-permute-done((f16[72,1152]{1,0:T(8,128)(2,1)S(1)}, f16[72,1152]{1,0:T(8,128)(2,1)S(1)}, u32[]{:S(2)}, u32[]{:S(2)}) %collective-permute-start.19) | collective-permute-done | bytes 165920 | tf_op jit(solution)/shard_map/ppermute | solution.py:51
  99.2 1.4 %collective-permute-done.21 = f16[72,1152]{1,0:T(8,128)(2,1)S(1)} collective-permute-done((f16[72,1152]{1,0:T(8,128)(2,1)S(1)}, f16[72,1152]{1,0:T(8,128)(2,1)S(1)}, u32[]{:S(2)}, u32[]{:S(2)}) %collective-permute-start.21) | collective-permute-done | bytes 165920 | tf_op jit(solution)/shard_map/ppermute | solution.py:51
  101.9 3.7 %collective-permute-start.18 = (f16[72,1152]{1,0:T(8,128)(2,1)S(1)}, f16[72,1152]{1,0:T(8,128)(2,1)S(1)}, u32[]{:S(2)}, u32[]{:S(2)}) collective-permute-start(f16[72,1152]{1,0:T(8,128)(2,1)S(1)} %get-tuple-element.50), channel_id=1, source_target_pairs={{0,96},{1,97},{2,98},{3,99},{4,100},{5,101},{6,102},{7,103},{8,104... | collective-permute-start | bytes 497672 | tf_op jit(solution)/shard_map/ppermute | solution.py:51
  105.5 3.6 %collective-permute-start.20 = (f16[72,1152]{1,0:T(8,128)(2,1)S(1)}, f16[72,1152]{1,0:T(8,128)(2,1)S(1)}, u32[]{:S(2)}, u32[]{:S(2)}) collective-permute-start(f16[72,1152]{1,0:T(8,128)(2,1)S(1)} %get-tuple-element.51), channel_id=1, source_target_pairs={{0,16},{1,17},{2,18},{3,19},{4,20},{5,21},{6,22},{7,23},{8,24},{9,... | collective-permute-start | bytes 497672 | tf_op jit(solution)/shard_map/ppermute | solution.py:51
  109.2 1.4 %collective-permute-start.22 = (f16[72,1152]{1,0:T(8,128)(2,1)S(1)}, f16[72,1152]{1,0:T(8,128)(2,1)S(1)}, u32[]{:S(2)}, u32[]{:S(2)}) collective-permute-start(f16[72,1152]{1,0:T(8,128)(2,1)S(1)} %get-tuple-element.52), channel_id=1, source_target_pairs={{0,112},{1,113},{2,114},{3,115},{4,116},{5,117},{6,118},{7,119},{8... | collective-permute-start | bytes 497672 | tf_op jit(solution)/shard_map/ppermute | solution.py:51
  110.5 5.7 %collective-permute-done.20 = f16[72,1152]{1,0:T(8,128)(2,1)S(1)} collective-permute-done((f16[72,1152]{1,0:T(8,128)(2,1)S(1)}, f16[72,1152]{1,0:T(8,128)(2,1)S(1)}, u32[]{:S(2)}, u32[]{:S(2)}) %collective-permute-start.20) | collective-permute-done | bytes 165920 | tf_op jit(solution)/shard_map/ppermute | solution.py:51
  (60 shorter events, 14.9 us)
Async XLA Ops:
  0.6 0.9 copy-start.2
  1.7 16.7 %collective-permute-start.4 = (bf16[64,1152]{1,0:T(8,128)(2,1)S(1)}, bf16[64,1152]{1,0:T(8,128)(2,1)S(1)}, u32[]{:S(2)}, u32[]{:S(2)}) collective-permute-start(bf16[64,1152]{1,0:T(8,128)(2,1)S(1)} %shard_map.68), channel_id=1, source_target_pairs={{0,112},{1,113},{2,114},{3,115},{4,116},{5,117},{6,118},{7,119},{8... | collective-permute-start | bytes 442376 | tf_op jit(solution)/shard_map/ppermute | solution.py:51
  7.6 14.0 %collective-permute-start = (bf16[64,1152]{1,0:T(8,128)(2,1)S(1)}, bf16[64,1152]{1,0:T(8,128)(2,1)S(1)}, u32[]{:S(2)}, u32[]{:S(2)}) collective-permute-start(bf16[64,1152]{1,0:T(8,128)(2,1)S(1)} %shard_map.68), channel_id=1, source_target_pairs={{0,16},{1,17},{2,18},{3,19},{4,20},{5,21},{6,22},{7,23},{8,24},{9,... | collective-permute-start | bytes 442376 | tf_op jit(solution)/shard_map/ppermute | solution.py:51
  7.6 0.9 copy-start
  10.2 39.8 %all-to-all-start = ((bf16[16,64,1152]{2,1,0:T(8,128)(2,1)}), bf16[16,64,1152]{2,1,0:T(8,128)(2,1)S(1)}, u32[]{:S(2)}, u32[]{:S(2)}) async-start(bf16[16,64,1152]{2,1,0:T(8,128)(2,1)} %shard_map.67), calls=%async_computation | async-start | bytes 4718592 | tf_op jit(solution)/shard_map/all_to_all | solution.py:242
  18.4 5.9 %collective-permute-start.5 = (bf16[64,1152]{1,0:T(8,128)(2,1)S(1)}, bf16[64,1152]{1,0:T(8,128)(2,1)S(1)}, u32[]{:S(2)}, u32[]{:S(2)}) collective-permute-start(bf16[64,1152]{1,0:T(8,128)(2,1)S(1)} %collective-permute-done.4), channel_id=1, source_target_pairs={{0,112},{1,113},{2,114},{3,115},{4,116},{5,117},{6,118},{7,119},{8... | collective-permute-start | bytes 442376 | tf_op jit(solution)/shard_map/ppermute | solution.py:51
  21.6 6.4 %collective-permute-start.1 = (bf16[64,1152]{1,0:T(8,128)(2,1)S(1)}, bf16[64,1152]{1,0:T(8,128)(2,1)S(1)}, u32[]{:S(2)}, u32[]{:S(2)}) collective-permute-start(bf16[64,1152]{1,0:T(8,128)(2,1)S(1)} %collective-permute-done), channel_id=1, source_target_pairs={{0,16},{1,17},{2,18},{3,19},{4,20},{5,21},{6,22},{7,23},{8,24},{9,... | collective-permute-start | bytes 442376 | tf_op jit(solution)/shard_map/ppermute | solution.py:51
  24.3 17.1 %collective-permute-start.6 = (bf16[64,1152]{1,0:T(8,128)(2,1)S(1)}, bf16[64,1152]{1,0:T(8,128)(2,1)S(1)}, u32[]{:S(2)}, u32[]{:S(2)}) collective-permute-start(bf16[64,1152]{1,0:T(8,128)(2,1)S(1)} %collective-permute-done.5), channel_id=1, source_target_pairs={{0,112},{1,113},{2,114},{3,115},{4,116},{5,117},{6,118},{7,119},{8... | collective-permute-start | bytes 442376 | tf_op jit(solution)/shard_map/ppermute | solution.py:51
  28.0 6.4 %collective-permute-start.2 = (bf16[64,1152]{1,0:T(8,128)(2,1)S(1)}, bf16[64,1152]{1,0:T(8,128)(2,1)S(1)}, u32[]{:S(2)}, u32[]{:S(2)}) collective-permute-start(bf16[64,1152]{1,0:T(8,128)(2,1)S(1)} %collective-permute-done.1), channel_id=1, source_target_pairs={{0,16},{1,17},{2,18},{3,19},{4,20},{5,21},{6,22},{7,23},{8,24},{9,... | collective-permute-start | bytes 442376 | tf_op jit(solution)/shard_map/ppermute | solution.py:51
  34.3 6.4 %collective-permute-start.3 = (bf16[64,1152]{1,0:T(8,128)(2,1)S(1)}, bf16[64,1152]{1,0:T(8,128)(2,1)S(1)}, u32[]{:S(2)}, u32[]{:S(2)}) collective-permute-start(bf16[64,1152]{1,0:T(8,128)(2,1)S(1)} %collective-permute-done.2), channel_id=1, source_target_pairs={{0,16},{1,17},{2,18},{3,19},{4,20},{5,21},{6,22},{7,23},{8,24},{9,... | collective-permute-start | bytes 442376 | tf_op jit(solution)/shard_map/ppermute | solution.py:51
  43.4 1.4 %copy-start.5 = (bf16[1024,1152]{1,0:T(8,128)(2,1)}, bf16[1024,1152]{1,0:T(8,128)(2,1)S(1)}, u32[]{:S(2)}) copy-start(bf16[1024,1152]{1,0:T(8,128)(2,1)S(1)} %get-tuple-element.34) | copy-start | bytes 7077892
  44.9 3.1 %collective-permute-start.7 = (bf16[512,1152]{1,0:T(8,128)(2,1)}, bf16[512,1152]{1,0:T(8,128)(2,1)S(1)}, u32[]{:S(2)}, u32[]{:S(2)}) collective-permute-start(bf16[512,1152]{1,0:T(8,128)(2,1)} %get-tuple-element.33), channel_id=1, source_target_pairs={{0,8},{1,9},{2,10},{3,11},{4,12},{5,13},{6,14},{7,15},{8,0},{9,1},... | collective-permute-start | bytes 3538952 | tf_op jit(solution)/shard_map/ppermute | solution.py:51
  57.8 7.8 %collective-permute-start.10 = (f32[3]{0:T(128)S(1)}, f32[3]{0:T(128)S(1)}, u32[]{:S(2)}, u32[]{:S(2)}) collective-permute-start(f32[3]{0:T(128)S(1)} %get-tuple-element.15), channel_id=1, source_target_pairs={{0,129},{1,0},{2,131},{3,2},{4,133},{5,4},{6,135},{7,6},{8,137},{9... | collective-permute-start | bytes 44 | tf_op jit(solution)/shard_map/ppermute | solution.py:69
  59.4 6.2 %collective-permute-start.9 = (f32[3]{0:T(128)S(1)}, f32[3]{0:T(128)S(1)}, u32[]{:S(2)}, u32[]{:S(2)}) collective-permute-start(f32[3]{0:T(128)S(1)} %get-tuple-element.15), channel_id=1, source_target_pairs={{0,128},{1,129},{2,130},{3,131},{4,132},{5,133},{6,134},{7,135},{8... | collective-permute-start | bytes 44 | tf_op jit(solution)/shard_map/ppermute | solution.py:69
  60.7 4.9 %collective-permute-start.8 = (f32[3]{0:T(128)S(1)}, f32[3]{0:T(128)S(1)}, u32[]{:S(2)}, u32[]{:S(2)}) collective-permute-start(f32[3]{0:T(128)S(1)} %get-tuple-element.15), channel_id=1, source_target_pairs={{0,1},{1,128},{2,3},{3,130},{4,5},{5,132},{6,7},{7,134},{8,9},{9,1... | collective-permute-start | bytes 44 | tf_op jit(solution)/shard_map/ppermute | solution.py:69
  65.6 9.8 %copy-start.4 = (f32[1024,1152]{1,0:T(8,128)}, f32[1024,1152]{1,0:T(8,128)S(1)}, u32[]{:S(2)}) copy-start(f32[1024,1152]{1,0:T(8,128)S(1)} %fusion.17) | copy-start | bytes 14155780
  65.6 5.5 %copy-start.6 = (bf16[1024,1152]{1,0:T(8,128)(2,1)S(1)}, bf16[1024,1152]{1,0:T(8,128)(2,1)}, u32[]{:S(2)}) copy-start(bf16[1024,1152]{1,0:T(8,128)(2,1)} %constant_dynamic-update-slice_fusion.8.mine_ref.theirs_ref) | copy-start | bytes 7077892
  65.6 9.7 %collective-permute-start.13 = (f32[3]{0:T(128)S(1)}, f32[3]{0:T(128)S(1)}, u32[]{:S(2)}, u32[]{:S(2)}) collective-permute-start(f32[3]{0:T(128)S(1)} %add_add_fusion.1), channel_id=1, source_target_pairs={{0,6},{1,7},{2,0},{3,1},{4,2},{5,3},{6,4},{7,5},{8,14},{9,15},{10,... | collective-permute-start | bytes 44 | tf_op jit(solution)/shard_map/ppermute | solution.py:69
  69.5 5.9 %collective-permute-start.12 = (f32[3]{0:T(128)S(1)}, f32[3]{0:T(128)S(1)}, u32[]{:S(2)}, u32[]{:S(2)}) collective-permute-start(f32[3]{0:T(128)S(1)} %add_add_fusion.1), channel_id=1, source_target_pairs={{0,4},{1,5},{2,6},{3,7},{4,0},{5,1},{6,2},{7,3},{8,12},{9,13},{10,... | collective-permute-start | bytes 44 | tf_op jit(solution)/shard_map/ppermute | solution.py:69
  69.5 5.9 %collective-permute-start.11 = (f32[3]{0:T(128)S(1)}, f32[3]{0:T(128)S(1)}, u32[]{:S(2)}, u32[]{:S(2)}) collective-permute-start(f32[3]{0:T(128)S(1)} %add_add_fusion.1), channel_id=1, source_target_pairs={{0,2},{1,3},{2,4},{3,5},{4,6},{5,7},{6,0},{7,1},{8,10},{9,11},{10,... | collective-permute-start | bytes 44 | tf_op jit(solution)/shard_map/ppermute | solution.py:69
  71.0 12.2 %collective-permute-start.14 = (f16[512,1152]{1,0:T(8,128)(2,1)S(1)}, f16[512,1152]{1,0:T(8,128)(2,1)}, u32[]{:S(2)}, u32[]{:S(2)}) collective-permute-start(f16[512,1152]{1,0:T(8,128)(2,1)S(1)} %multiply_convert_fusion.1), channel_id=1, source_target_pairs={{0,8},{1,9},{2,10},{3,11},{4,12},{5,13},{6,14},{7,15},{8,0},{9,1},... | collective-permute-start | bytes 3538952 | tf_op jit(solution)/shard_map/ppermute | solution.py:51
  75.4 43.3 %all-to-all-start.1 = ((f16[16,64,1152]{2,1,0:T(8,128)(2,1)}), f16[16,64,1152]{2,1,0:T(8,128)(2,1)S(1)}, u32[]{:S(2)}, u32[]{:S(2)}) async-start(f16[16,64,1152]{2,1,0:T(8,128)(2,1)} %bitcast.9), calls=%async_computation.1 | async-start | bytes 4718592 | tf_op jit(solution)/shard_map/all_to_all | solution.py:267
  81.9 1.2 %collective-permute-start.15 = (f32[3]{0:T(128)S(1)}, f32[3]{0:T(128)S(1)}, u32[]{:S(2)}, u32[]{:S(2)}) collective-permute-start(f32[3]{0:T(128)S(1)} %add_add_fusion), channel_id=1, source_target_pairs={{0,8},{1,9},{2,10},{3,11},{4,12},{5,13},{6,14},{7,15},{8,0},{9,1},... | collective-permute-start | bytes 44 | tf_op jit(solution)/shard_map/ppermute | solution.py:60
  85.8 31.4 %copy-start.3 = (bf16[64,1152]{1,0:T(8,128)(2,1)S(1)}, bf16[64,1152]{1,0:T(8,128)(2,1)}, u32[]{:S(2)}) copy-start(bf16[64,1152]{1,0:T(8,128)(2,1)} %rows_ref.7) | copy-start | bytes 442372
  85.8 9.9 %collective-permute-start.17 = (f16[72,1152]{1,0:T(8,128)(2,1)S(1)}, f16[72,1152]{1,0:T(8,128)(2,1)S(1)}, u32[]{:S(2)}, u32[]{:S(2)}) collective-permute-start(f16[72,1152]{1,0:T(8,128)(2,1)S(1)} %get-tuple-element.53), channel_id=1, source_target_pairs={{0,96},{1,97},{2,98},{3,99},{4,100},{5,101},{6,102},{7,103},{8,104... | collective-permute-start | bytes 497672 | tf_op jit(solution)/shard_map/ppermute | solution.py:51
  87.8 11.4 %collective-permute-start.19 = (f16[72,1152]{1,0:T(8,128)(2,1)S(1)}, f16[72,1152]{1,0:T(8,128)(2,1)S(1)}, u32[]{:S(2)}, u32[]{:S(2)}) collective-permute-start(f16[72,1152]{1,0:T(8,128)(2,1)S(1)} %get-tuple-element.54), channel_id=1, source_target_pairs={{0,32},{1,33},{2,34},{3,35},{4,36},{5,37},{6,38},{7,39},{8,40},{9,... | collective-permute-start | bytes 497672 | tf_op jit(solution)/shard_map/ppermute | solution.py:51
  88.8 11.7 %collective-permute-start.21 = (f16[72,1152]{1,0:T(8,128)(2,1)S(1)}, f16[72,1152]{1,0:T(8,128)(2,1)S(1)}, u32[]{:S(2)}, u32[]{:S(2)}) collective-permute-start(f16[72,1152]{1,0:T(8,128)(2,1)S(1)} %get-tuple-element.55), channel_id=1, source_target_pairs={{0,96},{1,97},{2,98},{3,99},{4,100},{5,101},{6,102},{7,103},{8,104... | collective-permute-start | bytes 497672 | tf_op jit(solution)/shard_map/ppermute | solution.py:51
  101.1 9.5 %collective-permute-start.16 = (f16[72,1152]{1,0:T(8,128)(2,1)S(1)}, f16[72,1152]{1,0:T(8,128)(2,1)S(1)}, u32[]{:S(2)}, u32[]{:S(2)}) collective-permute-start(f16[72,1152]{1,0:T(8,128)(2,1)S(1)} %get-tuple-element.49), channel_id=1, source_target_pairs={{0,32},{1,33},{2,34},{3,35},{4,36},{5,37},{6,38},{7,39},{8,40},{9,... | collective-permute-start | bytes 497672 | tf_op jit(solution)/shard_map/ppermute | solution.py:51
  101.9 8.7 %collective-permute-start.18 = (f16[72,1152]{1,0:T(8,128)(2,1)S(1)}, f16[72,1152]{1,0:T(8,128)(2,1)S(1)}, u32[]{:S(2)}, u32[]{:S(2)}) collective-permute-start(f16[72,1152]{1,0:T(8,128)(2,1)S(1)} %get-tuple-element.50), channel_id=1, source_target_pairs={{0,96},{1,97},{2,98},{3,99},{4,100},{5,101},{6,102},{7,103},{8,104... | collective-permute-start | bytes 497672 | tf_op jit(solution)/shard_map/ppermute | solution.py:51
  105.5 10.7 %collective-permute-start.20 = (f16[72,1152]{1,0:T(8,128)(2,1)S(1)}, f16[72,1152]{1,0:T(8,128)(2,1)S(1)}, u32[]{:S(2)}, u32[]{:S(2)}) collective-permute-start(f16[72,1152]{1,0:T(8,128)(2,1)S(1)} %get-tuple-element.51), channel_id=1, source_target_pairs={{0,16},{1,17},{2,18},{3,19},{4,20},{5,21},{6,22},{7,23},{8,24},{9,... | collective-permute-start | bytes 497672 | tf_op jit(solution)/shard_map/ppermute | solution.py:51
  109.2 7.7 %collective-permute-start.22 = (f16[72,1152]{1,0:T(8,128)(2,1)S(1)}, f16[72,1152]{1,0:T(8,128)(2,1)S(1)}, u32[]{:S(2)}, u32[]{:S(2)}) collective-permute-start(f16[72,1152]{1,0:T(8,128)(2,1)S(1)} %get-tuple-element.52), channel_id=1, source_target_pairs={{0,112},{1,113},{2,114},{3,115},{4,116},{5,117},{6,118},{7,119},{8... | collective-permute-start | bytes 497672 | tf_op jit(solution)/shard_map/ppermute | solution.py:51
  116.9 2.6 %copy-start.1 = (bf16[64,1152]{1,0:T(8,128)(2,1)S(1)}, bf16[64,1152]{1,0:T(8,128)(2,1)}, u32[]{:S(2)}) copy-start(bf16[64,1152]{1,0:T(8,128)(2,1)} %rows_ref.6) | copy-start | bytes 442372
